TPU v7x, 128 devices: a whole 4x4x4 slice. The times are simulated.
128 devices in a mesh: seq: 64 (over x, y, z), head: 2 (over core).
Axes of the slice: x: 4, y: 4, z: 4, core: 2. Of those that a mesh axis runs over, the one named last changes fastest.
Arguments:
- queries: bfloat16 [65536, 2048], P(('seq', 'head')), may hold values from -120 to 120
- keys: bfloat16 [65536, 2048], P(('seq', 'head')), may hold values from -4.5 to 4.5
- values: bfloat16 [65536, 2048], P(('seq', 'head')), may hold values from -6 to 6
- offsets: int32 [2, 4], replicated, may hold values from 0 to 31, as said below
Outputs:
- attention_out: bfloat16 [65536, 2048], P(('seq', 'head'))
Inputs may be any that keep to these rules, and one draw needn't show every extreme that they name: offsets[0, g] is below 2 and offsets[1, g] is below 32; some head group has offsets[0, g] = 0 and some head group has offsets[1, g] = 31.
All inputs are finite; a program needn't handle non-finite values.
Results may differ from a plain program's by a relative error of at most 0.0032.
Values may be sent and summed in bfloat16 or wider, within the bound.
No kernel may reach another device: no remote copies, remote signals or barrier semaphores. Data moves between devices by JAX's collectives and lax.ppermute only.
A program may use at most 128 MiB of HBM per device.

v0:
```python
import jax
import jax.numpy as jnp
from jax import lax
from jax.sharding import PartitionSpec as P

HEADS_DEV = 8
HD = 128
GROUP_HEADS = 4
BLK = 128
TOK_DEV = 1024
R1 = 2
W1 = 2048
R2 = 32


def shifted(block, axis, distance):
    devices = range(lax.axis_size(axis))
    route = [(i - distance, i) for i in devices if i - distance in devices]
    return lax.ppermute(block, axis, route)


def attend(query_rows, key_rows, value_rows, allowed):
    scores = jnp.einsum(
        "qhd,khd->hqk", query_rows, key_rows, preferred_element_type=jnp.float32
    ) * HD ** (-0.5)
    scores = jnp.where(allowed[None], scores, -jnp.inf)
    highest = jnp.max(scores, axis=-1)
    raised = jnp.exp(scores - highest[..., None])
    totals = jnp.sum(raised, axis=-1)
    weights = raised.astype(jnp.bfloat16)
    output = (
        jnp.einsum("hqk,khd->qhd", weights, value_rows, preferred_element_type=jnp.float32)
        / jnp.transpose(totals)[:, :, None]
    )
    return (output, jnp.transpose(highest + jnp.log(totals)))


def collect(slot_data, stride, slots_count, level_id):
    stacked = jnp.zeros((slots_count,) + slot_data.shape, slot_data.dtype).at[0].set(slot_data)

    def advance(number, state_pair):
        current, gathered = state_pair
        if level_id == 1:
            current = shifted(current, "seq", stride)
        else:
            current = shifted(current, "seq", stride)
        gathered = lax.dynamic_update_index_in_dim(gathered, current, number, 0)
        return (current, gathered)

    return lax.fori_loop(1, slots_count, advance, (slot_data, stacked))[1]


def local(queries, keys, values, offsets):
    local_q, local_k, local_v = (
        lax.all_to_all(queries, "head", split_axis=1, concat_axis=0, tiled=True),
        lax.all_to_all(keys, "head", split_axis=1, concat_axis=0, tiled=True),
        lax.all_to_all(values, "head", split_axis=1, concat_axis=0, tiled=True),
    )
    rows_here = local_q.shape[0]
    blocks_here = rows_here // BLK
    groups_here = HEADS_DEV // GROUP_HEADS
    group_width = GROUP_HEADS * HD
    seq_place = lax.axis_index("seq")
    head_place = lax.axis_index("head")
    near_span = W1 // TOK_DEV
    far_stride = R2 * BLK // rows_here
    far_count = lax.axis_size("seq") // far_stride
    near_blocks = rows_here // (R1 * BLK)
    near_rows = near_blocks * BLK
    query_heads = local_q.reshape(rows_here, HEADS_DEV, HD)
    key_heads = local_k.reshape(rows_here, HEADS_DEV, HD)
    value_heads = local_v.reshape(rows_here, HEADS_DEV, HD)
    block_rows = min(512, rows_here)

    def local_block(number):
        first_row = number * block_rows
        query_rows = lax.dynamic_slice_in_dim(query_heads, first_row, block_rows, 0)
        allowed = (first_row + jnp.arange(block_rows))[:, None] >= jnp.arange(rows_here)[None, :]
        return attend(query_rows, key_heads, value_heads, allowed)

    local_out, local_mass = lax.map(local_block, jnp.arange(rows_here // block_rows))
    local_out = local_out.reshape(rows_here, HEADS_DEV, HD)
    local_mass = local_mass.reshape(rows_here, HEADS_DEV)
    near_offsets = []
    far_offsets = []
    near_query = []
    far_query = []
    near_keys = []
    near_values = []
    far_keys = []
    far_values = []
    for member in range(groups_here):
        group_id = head_place * groups_here + member
        near_offset = offsets[0, group_id]
        far_offset = offsets[1, group_id]
        columns = slice(member * group_width, (member + 1) * group_width)
        far_block = far_offset % blocks_here
        near_offsets.append(near_offset)
        far_offsets.append(far_offset)
        for source, near_list, far_list in (
            (local_q, near_query, far_query),
            (local_k, near_keys, far_keys),
            (local_v, near_values, far_values),
        ):
            near_list.append(
                lax.dynamic_index_in_dim(
                    source[:, columns].reshape(near_blocks, R1, BLK, group_width),
                    near_offset,
                    1,
                    keepdims=False,
                )
            )
            far_list.append(
                lax.dynamic_index_in_dim(
                    source[:, columns].reshape(blocks_here, BLK, group_width),
                    far_block,
                    0,
                    keepdims=False,
                )
            )
    near_send = jnp.stack([jnp.stack(near_keys), jnp.stack(near_values)])
    far_send = jnp.stack([jnp.stack(far_keys), jnp.stack(far_values)])
    near_all = collect(near_send, 1, near_span, 1)
    far_all = collect(far_send, far_stride, far_count, 2)
    near_outs = []
    near_masses = []
    far_outs = []
    far_masses = []
    for member in range(groups_here):
        query_rows = near_query[member].reshape(near_rows, GROUP_HEADS, HD)
        key_rows = near_all[:, 0, member].reshape(near_span * near_rows, GROUP_HEADS, HD)
        value_rows = near_all[:, 1, member].reshape(near_span * near_rows, GROUP_HEADS, HD)
        source_ids = jnp.arange(near_span * near_rows) // near_rows
        within = jnp.arange(near_span * near_rows) % near_rows
        allowed = jnp.where(
            source_ids[None, :] == 0,
            within[None, :] <= jnp.arange(near_rows)[:, None],
            (seq_place % near_span >= source_ids)[None, :],
        )
        output, log_mass = attend(query_rows, key_rows, value_rows, allowed)
        chosen = jnp.arange(R1) == near_offsets[member]
        near_outs.append(
            jnp.where(
                chosen[None, :, None, None, None],
                output.reshape(near_blocks, 1, BLK, GROUP_HEADS, HD),
                0.0,
            ).reshape(rows_here, GROUP_HEADS, HD)
        )
        near_masses.append(
            jnp.where(
                chosen[None, :, None, None],
                log_mass.reshape(near_blocks, 1, BLK, GROUP_HEADS),
                -jnp.inf,
            ).reshape(rows_here, GROUP_HEADS)
        )
        query_rows = far_query[member].reshape(BLK, GROUP_HEADS, HD)
        key_rows = far_all[:, 0, member].reshape(far_count * BLK, GROUP_HEADS, HD)
        value_rows = far_all[:, 1, member].reshape(far_count * BLK, GROUP_HEADS, HD)
        source_ids = jnp.arange(far_count * BLK) // BLK
        within = jnp.arange(far_count * BLK) % BLK
        allowed = jnp.where(
            source_ids[None, :] == 0,
            within[None, :] <= jnp.arange(BLK)[:, None],
            (seq_place >= far_stride * source_ids)[None, :],
        )
        output, log_mass = attend(query_rows, key_rows, value_rows, allowed)
        holder = seq_place % far_stride == far_offsets[member] // blocks_here
        chosen = (jnp.arange(blocks_here) == far_offsets[member] % blocks_here) & holder
        far_outs.append(
            jnp.where(chosen[:, None, None, None], output[None], 0.0).reshape(
                rows_here, GROUP_HEADS, HD
            )
        )
        far_masses.append(
            jnp.where(chosen[:, None, None], log_mass[None], -jnp.inf).reshape(
                rows_here, GROUP_HEADS
            )
        )
    near_out = jnp.concatenate(near_outs, axis=1)
    near_mass = jnp.concatenate(near_masses, axis=1)
    far_out = jnp.concatenate(far_outs, axis=1)
    far_mass = jnp.concatenate(far_masses, axis=1)
    masses = jnp.stack([local_mass, near_mass, far_mass])
    summit = jnp.max(masses, axis=0)
    scales = jnp.exp(masses - summit[None])
    blended = (
        scales[0][..., None] * local_out
        + scales[1][..., None] * near_out
        + scales[2][..., None] * far_out
    ) / jnp.sum(scales, axis=0)[..., None]
    blended = blended.astype(jnp.bfloat16).reshape(rows_here, HEADS_DEV * HD)
    return lax.all_to_all(blended, "head", split_axis=0, concat_axis=1, tiled=True)


def solution(mesh):
    placed = (P(("seq", "head"), None), P(("seq", "head"), None), P(("seq", "head"), None), P())
    return jax.shard_map(
        local, mesh=mesh, in_specs=placed, out_specs=P(("seq", "head"), None), check_vma=False
    )
```

profile of v0, /device:TPU:5, one launch (start us, length us, event | category | flops | bytes accessed | tf_op | source)
XLA Modules:
  0.0 532.1 jit_solution(16012659745136644684)
XLA Ops:
  72.5 44.6 %while.35 = (s32[]{:T(128)}, f32[2,512,8,128]{1,3,2,0:T(8,128)}, f32[2,512,8]{1,2,0:T(8,128)}, s32[2]{0:T(128)}, bf16[1024,8,128]{2,1,0:T(8,128)(2,1)}, /*index=...) while((s32[]{:T(128)}, f32[2,512,8,128]{1,3,2,0:T(8,128)}, ...), condition=%wide.region_3.4_spmd, body=%wide.region_0.3_spmd.sunk | while | flops 2194665984 | bytes 78778576 | solution.py:81
  85.2 5.7 %fusion.151 = f32[1,512,8,128]{3,1,2,0:T(8,128)} fusion(bf16[1024,8,128]{2,0,1:T(8,128)(2,1)S(1)} %copy-done.8, f32[8,512,1024]{2,1,0:T(8,128)S(1)} %get-tuple-element.302, f32[8,512]{1,0:T(8,128)S(1)} %get-tuple-element.303, pred[512,1024]{1,0:T(8,128)(4,1)S(1)} %iota_compare_fusion.6, f32[512,8]{0,1:T(8,128)S(1)} %bitcast.262), kind=kOutput, calls=%fused_computation.8.clone.1 | convolution fusion | flops 1091043328 | bytes 21528576 | tf_op jit(solution)/shard_map/while/body/eval_jaxpr/hqk,khd->qhd/dot_general | solution.py:32
  127.8 232.3 %while.36 = (s32[]{:T(128)}, bf16[2,2,128,512]{3,2,1,0:T(8,128)(2,1)S(1)}, bf16[16,2,2,128,512]{4,3,2,1,0:T(8,128)(2,1)}, s32[]{:T(128)}, s32[]{:T(128)}, /*index=5*/s32[]{:T(128)}) while((s32[]{:T(128)}, bf16[2,2,128,512]{3,2,1,0:T(8,128)(2,1)S(1)}, bf16[16,2,2,128,512]{4,3,2,1,0:T(8,128)(2,1)}, s32[]{:T(128)}, s32[]{:T(128)}, ...), condition=%wide.region_9.10_spmd, body=%wide.region_8.9_spmd.sunk | while | flops 5 | bytes 4194451 | solution.py:50
  131.0 13.6 %collective-permute-done = bf16[2,2,128,512]{3,2,1,0:T(8,128)(2,1)S(1)} collective-permute-done((bf16[2,2,128,512]{3,2,1,0:T(8,128)(2,1)S(1)}, bf16[2,2,128,512]{3,2,1,0:T(8,128)(2,1)S(1)}, u32[]{:S(2)}, u32[]{:S(2)}) %collective-permute-start) | collective-permute-done | bytes 524320 | tf_op jit(solution)/shard_map/while/body/eval_jaxpr/ppermute | solution.py:19
  147.4 14.0 %collective-permute-done = bf16[2,2,128,512]{3,2,1,0:T(8,128)(2,1)S(1)} collective-permute-done((bf16[2,2,128,512]{3,2,1,0:T(8,128)(2,1)S(1)}, bf16[2,2,128,512]{3,2,1,0:T(8,128)(2,1)S(1)}, u32[]{:S(2)}, u32[]{:S(2)}) %collective-permute-start) | collective-permute-done | bytes 524320 | tf_op jit(solution)/shard_map/while/body/eval_jaxpr/ppermute | solution.py:19
  164.2 13.1 %collective-permute-done = bf16[2,2,128,512]{3,2,1,0:T(8,128)(2,1)S(1)} collective-permute-done((bf16[2,2,128,512]{3,2,1,0:T(8,128)(2,1)S(1)}, bf16[2,2,128,512]{3,2,1,0:T(8,128)(2,1)S(1)}, u32[]{:S(2)}, u32[]{:S(2)}) %collective-permute-start) | collective-permute-done | bytes 524320 | tf_op jit(solution)/shard_map/while/body/eval_jaxpr/ppermute | solution.py:19
  180.1 12.1 %collective-permute-done = bf16[2,2,128,512]{3,2,1,0:T(8,128)(2,1)S(1)} collective-permute-done((bf16[2,2,128,512]{3,2,1,0:T(8,128)(2,1)S(1)}, bf16[2,2,128,512]{3,2,1,0:T(8,128)(2,1)S(1)}, u32[]{:S(2)}, u32[]{:S(2)}) %collective-permute-start) | collective-permute-done | bytes 524320 | tf_op jit(solution)/shard_map/while/body/eval_jaxpr/ppermute | solution.py:19
  195.0 11.2 %collective-permute-done = bf16[2,2,128,512]{3,2,1,0:T(8,128)(2,1)S(1)} collective-permute-done((bf16[2,2,128,512]{3,2,1,0:T(8,128)(2,1)S(1)}, bf16[2,2,128,512]{3,2,1,0:T(8,128)(2,1)S(1)}, u32[]{:S(2)}, u32[]{:S(2)}) %collective-permute-start) | collective-permute-done | bytes 524320 | tf_op jit(solution)/shard_map/while/body/eval_jaxpr/ppermute | solution.py:19
  209.0 10.1 %collective-permute-done = bf16[2,2,128,512]{3,2,1,0:T(8,128)(2,1)S(1)} collective-permute-done((bf16[2,2,128,512]{3,2,1,0:T(8,128)(2,1)S(1)}, bf16[2,2,128,512]{3,2,1,0:T(8,128)(2,1)S(1)}, u32[]{:S(2)}, u32[]{:S(2)}) %collective-permute-start) | collective-permute-done | bytes 524320 | tf_op jit(solution)/shard_map/while/body/eval_jaxpr/ppermute | solution.py:19
  221.9 10.1 %collective-permute-done = bf16[2,2,128,512]{3,2,1,0:T(8,128)(2,1)S(1)} collective-permute-done((bf16[2,2,128,512]{3,2,1,0:T(8,128)(2,1)S(1)}, bf16[2,2,128,512]{3,2,1,0:T(8,128)(2,1)S(1)}, u32[]{:S(2)}, u32[]{:S(2)}) %collective-permute-start) | collective-permute-done | bytes 524320 | tf_op jit(solution)/shard_map/while/body/eval_jaxpr/ppermute | solution.py:19
  234.8 10.1 %collective-permute-done = bf16[2,2,128,512]{3,2,1,0:T(8,128)(2,1)S(1)} collective-permute-done((bf16[2,2,128,512]{3,2,1,0:T(8,128)(2,1)S(1)}, bf16[2,2,128,512]{3,2,1,0:T(8,128)(2,1)S(1)}, u32[]{:S(2)}, u32[]{:S(2)}) %collective-permute-start) | collective-permute-done | bytes 524320 | tf_op jit(solution)/shard_map/while/body/eval_jaxpr/ppermute | solution.py:19
  247.7 10.8 %collective-permute-done = bf16[2,2,128,512]{3,2,1,0:T(8,128)(2,1)S(1)} collective-permute-done((bf16[2,2,128,512]{3,2,1,0:T(8,128)(2,1)S(1)}, bf16[2,2,128,512]{3,2,1,0:T(8,128)(2,1)S(1)}, u32[]{:S(2)}, u32[]{:S(2)}) %collective-permute-start) | collective-permute-done | bytes 524320 | tf_op jit(solution)/shard_map/while/body/eval_jaxpr/ppermute | solution.py:19
  261.3 11.9 %collective-permute-done = bf16[2,2,128,512]{3,2,1,0:T(8,128)(2,1)S(1)} collective-permute-done((bf16[2,2,128,512]{3,2,1,0:T(8,128)(2,1)S(1)}, bf16[2,2,128,512]{3,2,1,0:T(8,128)(2,1)S(1)}, u32[]{:S(2)}, u32[]{:S(2)}) %collective-permute-start) | collective-permute-done | bytes 524320 | tf_op jit(solution)/shard_map/while/body/eval_jaxpr/ppermute | solution.py:19
  276.0 12.9 %collective-permute-done = bf16[2,2,128,512]{3,2,1,0:T(8,128)(2,1)S(1)} collective-permute-done((bf16[2,2,128,512]{3,2,1,0:T(8,128)(2,1)S(1)}, bf16[2,2,128,512]{3,2,1,0:T(8,128)(2,1)S(1)}, u32[]{:S(2)}, u32[]{:S(2)}) %collective-permute-start) | collective-permute-done | bytes 524320 | tf_op jit(solution)/shard_map/while/body/eval_jaxpr/ppermute | solution.py:19
  291.7 14.0 %collective-permute-done = bf16[2,2,128,512]{3,2,1,0:T(8,128)(2,1)S(1)} collective-permute-done((bf16[2,2,128,512]{3,2,1,0:T(8,128)(2,1)S(1)}, bf16[2,2,128,512]{3,2,1,0:T(8,128)(2,1)S(1)}, u32[]{:S(2)}, u32[]{:S(2)}) %collective-permute-start) | collective-permute-done | bytes 524320 | tf_op jit(solution)/shard_map/while/body/eval_jaxpr/ppermute | solution.py:19
  308.5 15.1 %collective-permute-done = bf16[2,2,128,512]{3,2,1,0:T(8,128)(2,1)S(1)} collective-permute-done((bf16[2,2,128,512]{3,2,1,0:T(8,128)(2,1)S(1)}, bf16[2,2,128,512]{3,2,1,0:T(8,128)(2,1)S(1)}, u32[]{:S(2)}, u32[]{:S(2)}) %collective-permute-start) | collective-permute-done | bytes 524320 | tf_op jit(solution)/shard_map/while/body/eval_jaxpr/ppermute | solution.py:19
  326.4 15.5 %collective-permute-done = bf16[2,2,128,512]{3,2,1,0:T(8,128)(2,1)S(1)} collective-permute-done((bf16[2,2,128,512]{3,2,1,0:T(8,128)(2,1)S(1)}, bf16[2,2,128,512]{3,2,1,0:T(8,128)(2,1)S(1)}, u32[]{:S(2)}, u32[]{:S(2)}) %collective-permute-start) | collective-permute-done | bytes 524320 | tf_op jit(solution)/shard_map/while/body/eval_jaxpr/ppermute | solution.py:19
  344.6 14.6 %collective-permute-done = bf16[2,2,128,512]{3,2,1,0:T(8,128)(2,1)S(1)} collective-permute-done((bf16[2,2,128,512]{3,2,1,0:T(8,128)(2,1)S(1)}, bf16[2,2,128,512]{3,2,1,0:T(8,128)(2,1)S(1)}, u32[]{:S(2)}, u32[]{:S(2)}) %collective-permute-start) | collective-permute-done | bytes 524320 | tf_op jit(solution)/shard_map/while/body/eval_jaxpr/ppermute | solution.py:19
  414.3 6.6 %fusion.16 = (f32[4,512]{1,0:T(4,128)S(1)}, f32[4,512]{1,0:T(4,128)S(1)}, f32[4,512,1024]{2,1,0:T(8,128)}) fusion(f32[4,512,1024]{2,1,0:T(8,128)S(1)} %get-tuple-element.224, f32[4,512]{1,0:T(4,128)S(1)} %get-tuple-element.223, pred[512,1024]{1,0:T(8,128)(4,1)S(1)} %copy-done.7, bf16[1024,4,128]{2,1,0:T(4,128)(2,1)S(1)} %copy-done.12, ...), kind=kOutput, calls=%fused_computation.27 | convolution fusion | flops 551546880 | bytes 18898944 | tf_op jit(solution)/shard_map/qhd,khd->hqk/dot_general | solution.py:23
  421.0 7.2 %fusion.91 = f32[512,4,128]{0,2,1:T(8,128)} fusion(f32[4,512,1024]{2,1,0:T(8,128)} %copy-done.19, f32[4,512]{1,0:T(4,128)S(1)} %get-tuple-element.223, pred[512,1024]{1,0:T(8,128)(4,1)S(1)} %copy-done.7, bf16[1024,4,128]{2,1,0:T(4,128)(2,1)} %reshape.505, f32[512,4]{0,1:T(4,128)S(1)} %bitcast.267), kind=kOutput, calls=%fused_computation.99 | convolution fusion | flops 545521664 | bytes 11026432 | tf_op jit(solution)/shard_map/hqk,khd->qhd/dot_general | solution.py:32
  434.6 7.3 %fusion.86 = f32[512,4,128]{0,2,1:T(8,128)} fusion(f32[4,512,1024]{2,1,0:T(8,128)} %get-tuple-element.225, f32[4,512]{1,0:T(4,128)S(1)} %get-tuple-element.168, pred[512,1024]{1,0:T(8,128)(4,1)} %fusion.47, bf16[1024,4,128]{2,1,0:T(4,128)(2,1)} %reshape.506, f32[512,4]{0,1:T(4,128)S(1)} %bitcast.265), kind=kOutput, calls=%fused_computation.98 | convolution fusion | flops 545521664 | bytes 11026432 | tf_op jit(solution)/shard_map/hqk,khd->qhd/dot_general | solution.py:32
  458.5 6.1 %maximum_multiply_fusion = f32[1024,8,128]{2,1,0:T(8,128)} fusion(f32[1024,4,128]{2,1,0:T(4,128)} %bitcast_select_fusion.2, f32[1024,4,128]{2,1,0:T(4,128)} %bitcast_select_fusion.3, f32[1024,8]{1,0:T(8,128)} %copy.131), kind=kLoop, calls=%fused_computation.36 | loop fusion | flops 2097152 | bytes 8421376 | tf_op jit(solution)/shard_map/mul | solution.py:188
  494.9 9.6 %divide_convert_fusion = bf16[2,512,1024]{2,1,0:T(8,128)(2,1)S(1)} fusion(f32[2,512,1024]{2,1,0:T(8,128)} %div.110, f32[2,512,1024]{2,1,0:T(8,128)} %mul.94, f32[2,512,1024]{2,1,0:T(8,128)} %mul.90, f32[2,512,1024]{2,1,0:T(8,128)} %mul.85, f32[2,512,1024]{2,1,0:T(8,128)} %copy.130), kind=kLoop, calls=%fused_computation.38 | loop fusion | flops 5242880 | bytes 23068672 | tf_op jit(solution)/shard_map/convert_element_type | solution.py:191
  504.4 20.9 %all_to_all.73 = bf16[2,512,1024]{2,1,0:T(8,128)(2,1)S(1)} all-to-all(bf16[2,512,1024]{2,1,0:T(8,128)(2,1)S(1)} %divide_convert_fusion), channel_id=1, replica_groups=mesh['seq'=64,'head'=2] {'head'}, dimensions={0} | all-to-all | bytes 4194304 | tf_op jit(solution)/shard_map/all_to_all | solution.py:192
  (223 shorter events, 268.4 us)
Async XLA Ops:
  0.0 8.4 %copy-start.18 = (s32[2,4]{1,0:T(2,128)S(1)}, s32[2,4]{1,0:T(2,128)}, u32[]{:S(2)}) copy-start(s32[2,4]{1,0:T(2,128)} %param.15) | copy-start | bytes 100
  3.9 10.5 %all-to-all-start = ((bf16[512,2,1024]{0,2,1:T(8,128)(2,1)}), bf16[512,2,1024]{0,2,1:T(8,128)(2,1)S(1)}, u32[]{:S(2)}, u32[]{:S(2)}) async-start(bf16[512,2,1024]{0,2,1:T(8,128)(2,1)} %bitcast.238), calls=%async_computation | async-start | bytes 4194304 | tf_op jit(solution)/shard_map/all_to_all | solution.py:55
  15.8 10.9 %all-to-all-start.2 = ((bf16[512,2,1024]{2,0,1:T(8,128)(2,1)}), bf16[512,2,1024]{2,0,1:T(8,128)(2,1)S(1)}, u32[]{:S(2)}, u32[]{:S(2)}) async-start(bf16[512,2,1024]{2,0,1:T(8,128)(2,1)} %bitcast.239), calls=%async_computation.2 | async-start | bytes 4194304 | tf_op jit(solution)/shard_map/all_to_all | solution.py:57
  26.6 7.5 %all-to-all-start.1 = ((bf16[512,2,1024]{2,0,1:T(8,128)(2,1)}), bf16[512,2,1024]{2,0,1:T(8,128)(2,1)}, u32[]{:S(2)}, u32[]{:S(2)}) async-start(bf16[512,2,1024]{2,0,1:T(8,128)(2,1)} %bitcast.240), calls=%async_computation.1 | async-start | bytes 4194304 | tf_op jit(solution)/shard_map/all_to_all | solution.py:56
  45.9 353.8 %collective-permute-start.1 = (bf16[2,2,4,128,512]{4,3,2,1,0:T(8,128)(2,1)}, bf16[2,2,4,128,512]{4,3,2,1,0:T(8,128)(2,1)}, u32[]{:S(2)}, u32[]{:S(2)}) collective-permute-start(bf16[2,2,4,128,512]{4,3,2,1,0:T(8,128)(2,1)} %get-tuple-element.203), channel_id=1, source_target_pairs={{0,2},{2,4},{4,6},{6,8},{8,10},{10,12},{12,14},{14,16},{16,18},{18... | collective-permute-start | bytes 6291464 | tf_op jit(solution)/shard_map/while/body/eval_jaxpr/ppermute | solution.py:19
  65.6 5.5 %copy-start.6 = (bf16[4,1,128,512]{3,2,0,1:T(8,128)(2,1)S(1)}, bf16[4,1,128,512]{3,2,0,1:T(8,128)(2,1)}, u32[]{:S(2)}) copy-start(bf16[4,1,128,512]{3,2,0,1:T(8,128)(2,1)} %get-tuple-element.235) | copy-start | bytes 1572868
  127.8 16.8 %collective-permute-start = (bf16[2,2,128,512]{3,2,1,0:T(8,128)(2,1)S(1)}, bf16[2,2,128,512]{3,2,1,0:T(8,128)(2,1)S(1)}, u32[]{:S(2)}, u32[]{:S(2)}) collective-permute-start(bf16[2,2,128,512]{3,2,1,0:T(8,128)(2,1)S(1)} %get-tuple-element.314), channel_id=1, source_target_pairs={{0,8},{2,10},{4,12},{6,14},{8,16},{10,18},{12,20},{14,22},{16,24},... | collective-permute-start | bytes 1572872 | tf_op jit(solution)/shard_map/while/body/eval_jaxpr/ppermute | solution.py:19
  145.5 15.9 %collective-permute-start = (bf16[2,2,128,512]{3,2,1,0:T(8,128)(2,1)S(1)}, bf16[2,2,128,512]{3,2,1,0:T(8,128)(2,1)S(1)}, u32[]{:S(2)}, u32[]{:S(2)}) collective-permute-start(bf16[2,2,128,512]{3,2,1,0:T(8,128)(2,1)S(1)} %get-tuple-element.314), channel_id=1, source_target_pairs={{0,8},{2,10},{4,12},{6,14},{8,16},{10,18},{12,20},{14,22},{16,24},... | collective-permute-start | bytes 1572872 | tf_op jit(solution)/shard_map/while/body/eval_jaxpr/ppermute | solution.py:19
  162.3 15.0 %collective-permute-start = (bf16[2,2,128,512]{3,2,1,0:T(8,128)(2,1)S(1)}, bf16[2,2,128,512]{3,2,1,0:T(8,128)(2,1)S(1)}, u32[]{:S(2)}, u32[]{:S(2)}) collective-permute-start(bf16[2,2,128,512]{3,2,1,0:T(8,128)(2,1)S(1)} %get-tuple-element.314), channel_id=1, source_target_pairs={{0,8},{2,10},{4,12},{6,14},{8,16},{10,18},{12,20},{14,22},{16,24},... | collective-permute-start | bytes 1572872 | tf_op jit(solution)/shard_map/while/body/eval_jaxpr/ppermute | solution.py:19
  178.2 14.1 %collective-permute-start = (bf16[2,2,128,512]{3,2,1,0:T(8,128)(2,1)S(1)}, bf16[2,2,128,512]{3,2,1,0:T(8,128)(2,1)S(1)}, u32[]{:S(2)}, u32[]{:S(2)}) collective-permute-start(bf16[2,2,128,512]{3,2,1,0:T(8,128)(2,1)S(1)} %get-tuple-element.314), channel_id=1, source_target_pairs={{0,8},{2,10},{4,12},{6,14},{8,16},{10,18},{12,20},{14,22},{16,24},... | collective-permute-start | bytes 1572872 | tf_op jit(solution)/shard_map/while/body/eval_jaxpr/ppermute | solution.py:19
  193.1 13.1 %collective-permute-start = (bf16[2,2,128,512]{3,2,1,0:T(8,128)(2,1)S(1)}, bf16[2,2,128,512]{3,2,1,0:T(8,128)(2,1)S(1)}, u32[]{:S(2)}, u32[]{:S(2)}) collective-permute-start(bf16[2,2,128,512]{3,2,1,0:T(8,128)(2,1)S(1)} %get-tuple-element.314), channel_id=1, source_target_pairs={{0,8},{2,10},{4,12},{6,14},{8,16},{10,18},{12,20},{14,22},{16,24},... | collective-permute-start | bytes 1572872 | tf_op jit(solution)/shard_map/while/body/eval_jaxpr/ppermute | solution.py:19
  207.1 12.0 %collective-permute-start = (bf16[2,2,128,512]{3,2,1,0:T(8,128)(2,1)S(1)}, bf16[2,2,128,512]{3,2,1,0:T(8,128)(2,1)S(1)}, u32[]{:S(2)}, u32[]{:S(2)}) collective-permute-start(bf16[2,2,128,512]{3,2,1,0:T(8,128)(2,1)S(1)} %get-tuple-element.314), channel_id=1, source_target_pairs={{0,8},{2,10},{4,12},{6,14},{8,16},{10,18},{12,20},{14,22},{16,24},... | collective-permute-start | bytes 1572872 | tf_op jit(solution)/shard_map/while/body/eval_jaxpr/ppermute | solution.py:19
  220.0 12.0 %collective-permute-start = (bf16[2,2,128,512]{3,2,1,0:T(8,128)(2,1)S(1)}, bf16[2,2,128,512]{3,2,1,0:T(8,128)(2,1)S(1)}, u32[]{:S(2)}, u32[]{:S(2)}) collective-permute-start(bf16[2,2,128,512]{3,2,1,0:T(8,128)(2,1)S(1)} %get-tuple-element.314), channel_id=1, source_target_pairs={{0,8},{2,10},{4,12},{6,14},{8,16},{10,18},{12,20},{14,22},{16,24},... | collective-permute-start | bytes 1572872 | tf_op jit(solution)/shard_map/while/body/eval_jaxpr/ppermute | solution.py:19
  232.9 12.0 %collective-permute-start = (bf16[2,2,128,512]{3,2,1,0:T(8,128)(2,1)S(1)}, bf16[2,2,128,512]{3,2,1,0:T(8,128)(2,1)S(1)}, u32[]{:S(2)}, u32[]{:S(2)}) collective-permute-start(bf16[2,2,128,512]{3,2,1,0:T(8,128)(2,1)S(1)} %get-tuple-element.314), channel_id=1, source_target_pairs={{0,8},{2,10},{4,12},{6,14},{8,16},{10,18},{12,20},{14,22},{16,24},... | collective-permute-start | bytes 1572872 | tf_op jit(solution)/shard_map/while/body/eval_jaxpr/ppermute | solution.py:19
  245.8 12.7 %collective-permute-start = (bf16[2,2,128,512]{3,2,1,0:T(8,128)(2,1)S(1)}, bf16[2,2,128,512]{3,2,1,0:T(8,128)(2,1)S(1)}, u32[]{:S(2)}, u32[]{:S(2)}) collective-permute-start(bf16[2,2,128,512]{3,2,1,0:T(8,128)(2,1)S(1)} %get-tuple-element.314), channel_id=1, source_target_pairs={{0,8},{2,10},{4,12},{6,14},{8,16},{10,18},{12,20},{14,22},{16,24},... | collective-permute-start | bytes 1572872 | tf_op jit(solution)/shard_map/while/body/eval_jaxpr/ppermute | solution.py:19
  259.4 13.8 %collective-permute-start = (bf16[2,2,128,512]{3,2,1,0:T(8,128)(2,1)S(1)}, bf16[2,2,128,512]{3,2,1,0:T(8,128)(2,1)S(1)}, u32[]{:S(2)}, u32[]{:S(2)}) collective-permute-start(bf16[2,2,128,512]{3,2,1,0:T(8,128)(2,1)S(1)} %get-tuple-element.314), channel_id=1, source_target_pairs={{0,8},{2,10},{4,12},{6,14},{8,16},{10,18},{12,20},{14,22},{16,24},... | collective-permute-start | bytes 1572872 | tf_op jit(solution)/shard_map/while/body/eval_jaxpr/ppermute | solution.py:19
  274.0 14.8 %collective-permute-start = (bf16[2,2,128,512]{3,2,1,0:T(8,128)(2,1)S(1)}, bf16[2,2,128,512]{3,2,1,0:T(8,128)(2,1)S(1)}, u32[]{:S(2)}, u32[]{:S(2)}) collective-permute-start(bf16[2,2,128,512]{3,2,1,0:T(8,128)(2,1)S(1)} %get-tuple-element.314), channel_id=1, source_target_pairs={{0,8},{2,10},{4,12},{6,14},{8,16},{10,18},{12,20},{14,22},{16,24},... | collective-permute-start | bytes 1572872 | tf_op jit(solution)/shard_map/while/body/eval_jaxpr/ppermute | solution.py:19
  289.8 15.9 %collective-permute-start = (bf16[2,2,128,512]{3,2,1,0:T(8,128)(2,1)S(1)}, bf16[2,2,128,512]{3,2,1,0:T(8,128)(2,1)S(1)}, u32[]{:S(2)}, u32[]{:S(2)}) collective-permute-start(bf16[2,2,128,512]{3,2,1,0:T(8,128)(2,1)S(1)} %get-tuple-element.314), channel_id=1, source_target_pairs={{0,8},{2,10},{4,12},{6,14},{8,16},{10,18},{12,20},{14,22},{16,24},... | collective-permute-start | bytes 1572872 | tf_op jit(solution)/shard_map/while/body/eval_jaxpr/ppermute | solution.py:19
  306.6 17.0 %collective-permute-start = (bf16[2,2,128,512]{3,2,1,0:T(8,128)(2,1)S(1)}, bf16[2,2,128,512]{3,2,1,0:T(8,128)(2,1)S(1)}, u32[]{:S(2)}, u32[]{:S(2)}) collective-permute-start(bf16[2,2,128,512]{3,2,1,0:T(8,128)(2,1)S(1)} %get-tuple-element.314), channel_id=1, source_target_pairs={{0,8},{2,10},{4,12},{6,14},{8,16},{10,18},{12,20},{14,22},{16,24},... | collective-permute-start | bytes 1572872 | tf_op jit(solution)/shard_map/while/body/eval_jaxpr/ppermute | solution.py:19
  324.5 17.4 %collective-permute-start = (bf16[2,2,128,512]{3,2,1,0:T(8,128)(2,1)S(1)}, bf16[2,2,128,512]{3,2,1,0:T(8,128)(2,1)S(1)}, u32[]{:S(2)}, u32[]{:S(2)}) collective-permute-start(bf16[2,2,128,512]{3,2,1,0:T(8,128)(2,1)S(1)} %get-tuple-element.314), channel_id=1, source_target_pairs={{0,8},{2,10},{4,12},{6,14},{8,16},{10,18},{12,20},{14,22},{16,24},... | collective-permute-start | bytes 1572872 | tf_op jit(solution)/shard_map/while/body/eval_jaxpr/ppermute | solution.py:19
  342.7 16.5 %collective-permute-start = (bf16[2,2,128,512]{3,2,1,0:T(8,128)(2,1)S(1)}, bf16[2,2,128,512]{3,2,1,0:T(8,128)(2,1)S(1)}, u32[]{:S(2)}, u32[]{:S(2)}) collective-permute-start(bf16[2,2,128,512]{3,2,1,0:T(8,128)(2,1)S(1)} %get-tuple-element.314), channel_id=1, source_target_pairs={{0,8},{2,10},{4,12},{6,14},{8,16},{10,18},{12,20},{14,22},{16,24},... | collective-permute-start | bytes 1572872 | tf_op jit(solution)/shard_map/while/body/eval_jaxpr/ppermute | solution.py:19
  414.2 6.7 %copy-start.19 = (f32[4,512,1024]{2,1,0:T(8,128)}, f32[4,512,1024]{2,1,0:T(8,128)S(1)}, u32[]{:S(2)}) copy-start(f32[4,512,1024]{2,1,0:T(8,128)S(1)} %get-tuple-element.224) | copy-start | bytes 25165828
  434.6 9.9 %copy-start.16 = (pred[1024]{0:T(1024)(128)(4,1)S(1)}, pred[1024]{0:T(1024)(128)(4,1)}, u32[]{:S(2)}) copy-start(pred[1024]{0:T(1024)(128)(4,1)} %broadcast_in_dim.327) | copy-start | bytes 3076
  441.8 7.0 %copy-start.15 = (pred[1024]{0:T(1024)(128)(4,1)S(1)}, pred[1024]{0:T(1024)(128)(4,1)}, u32[]{:S(2)}) copy-start(pred[1024]{0:T(1024)(128)(4,1)} %broadcast_in_dim.339) | copy-start | bytes 3076
  (16 other events, 47.2 us)
where the time goes:
time: 539 us; the launch traced here: 532 us
  waiting for transfers between devices  190 us (35%)
  local copies, waits for them, and re-layouts  143 us (27%)
  other arithmetic  67.7 us (13%)
  matrix products  52.5 us (10%)
  starting transfers between devices  46.5 us (9%)
  blocking collectives  20.9 us (4%)
  between operations  9.13 us (2%)
    ppermute x16, waiting for transfers between devices, shifted(): return lax.ppermute(block, axis, route)  189 us
    ppermute x16, starting transfers between devices, shifted(): return lax.ppermute(block, axis, route)  33.4 us
    dot_general x6, matrix products, attend(): jnp.einsum('hqk,khd->qhd', weights, value_rows, preferred_element_type=jn...  28.8 us
    dot_general x6, matrix products, attend(): jnp.einsum('qhd,khd->hqk', query_rows, key_rows, preferred_element_type=j...  23.6 us
    all_to_all x1, blocking collectives, local(): lax.all_to_all(blended, 'head', split_axis=0, concat_axis=1, tiled=True)  20.9 us
    reduce_sum x4, other arithmetic, attend(): totals = jnp.sum(raised, axis=-1)  16.6 us
    unnamed x48, local copies, waits for them, and re-layouts  13.8 us
    dynamic_update_slice x15, local copies, waits for them, and re-layouts, advance(): gathered = lax.dynamic_update_index_in_dim(gathered, current, number, 0)  12.7 us
  transfers between devices with their start and end apart: 19, of which 16 were waited for; matrix products, arithmetic and copies ran while one was open for 26% of the time, Pallas kernels for 0%

commit v1 on v0

v1 whole, which is shorter than its diff:
```python
import functools

import jax
import jax.numpy as jnp
import numpy as np
from jax import lax
from jax.experimental import pallas as pl
from jax.experimental.pallas import tpu as pltpu
from jax.sharding import Mesh
from jax.sharding import PartitionSpec as P

HD = 128
BLK = 128
HALF = 64
HEADS = 16
GROUPS = 4
GH = 4
GW = GH * HD
ROWS = 512
NSEL = 256
AXES = ("x", "y", "z", "c")
SIZES = (4, 4, 4, 2)
SCALE = float(HD**-0.5 * np.log2(np.e))
LOW = -1e30
BF, F32 = jnp.bfloat16, jnp.float32

I_CORE, I_ODD, I_FACTIVE, I_PAR, I_NEAR, I_FBLK, I_FMINE = 0, 1, 2, 3, 4, 8, 12


def route(step):
    pairs = []
    for index in np.ndindex(*SIZES):
        target = step(*index)
        if target is not None:
            pairs.append((int(np.ravel_multi_index(index, SIZES)), int(np.ravel_multi_index(target, SIZES))))
    return pairs


CORE = route(lambda x, y, z, c: (x, y, z, 1 - c))
TO_EVEN = route(lambda x, y, z, c: (x, y, z - 1, c) if z % 2 else None)
TO_ODD = route(lambda x, y, z, c: (x, y, z + 1, c) if z % 2 == 0 else None)


def move(array, pairs):
    return lax.ppermute(array, AXES, pairs)


def cost(flops, nbytes, exps=0):
    return pl.CostEstimate(flops=int(flops), bytes_accessed=int(nbytes), transcendentals=int(exps))


ANY = pl.BlockSpec(memory_space=pl.ANY)
SMEM = pl.BlockSpec(memory_space=pltpu.SMEM)
PARAMS = dict(vmem_limit_bytes=48 * 1024 * 1024)


def nt(a, b):
    return lax.dot_general(a, b, (((1,), (1,)), ((), ())), preferred_element_type=F32)


def nn(a, b):
    return lax.dot_general(a, b, (((1,), (0,)), ((), ())), preferred_element_type=F32)


def three(x):
    hi = x.astype(BF).astype(F32)
    rest = x - hi
    mid = rest.astype(BF).astype(F32)
    return hi, mid, rest - mid


def run_copies(copies):
    for copy in copies:
        copy.start()
    for copy in copies:
        copy.wait()


def pack_first(info, q, k, v, *rest):
    near_outs, far_out, sems = rest[:GROUPS], rest[GROUPS], rest[GROUPS + 1]
    core = info[I_CORE]
    copies = []
    n = 0
    for g in range(GROUPS):
        cols = pl.ds(g * GW, GW)
        for half in range(2):
            first = pl.multiple_of((info[I_NEAR + g] + 2 * half) * BLK, BLK)
            copies.append(
                pltpu.make_async_copy(
                    q.at[pl.ds(first, BLK), cols], near_outs[g].at[pl.ds(half * BLK, BLK)], sems.at[n]
                )
            )
            n += 1
        first = pl.multiple_of((info[I_FBLK + g] % 4) * BLK + (1 - core) * HALF, HALF)
        for t, source in enumerate((q, k, v)):
            copies.append(
                pltpu.make_async_copy(source.at[pl.ds(first, HALF), cols], far_out.at[g, t], sems.at[n])
            )
            n += 1
    run_copies(copies)


def pack_second(info, q, k, v, received, out, sems):
    core = info[I_CORE]

    def all_copies(g, mine):
        copies = []
        first = pl.multiple_of((info[I_FBLK + g] % 4) * BLK + core * HALF, HALF)
        for t, source in enumerate((q, k, v)):
            for h in range(GH):
                if mine:
                    piece = source.at[pl.ds(first, HALF), pl.ds(g * GW + h * HD, HD)]
                else:
                    piece = received.at[g, t, :, pl.ds(h * HD, HD)]
                copies.append(
                    pltpu.make_async_copy(piece, out.at[h * GROUPS + g, t], sems.at[(g * 3 + t) * GH + h])
                )
        return copies

    for g in range(GROUPS):
        here = info[I_FBLK + g] // 4 == core

        @pl.when(here)
        def _():
            for copy in all_copies(g, True):
                copy.start()

        @pl.when(jnp.logical_not(here))
        def _():
            for copy in all_copies(g, False):
                copy.start()

    for g in range(GROUPS):
        for copy in all_copies(g, False):
            copy.wait()


def softmax_parts(parts, values):
    top = functools.reduce(jnp.maximum, [jnp.max(s, axis=1, keepdims=True) for s in parts]) * SCALE
    total = 0.0
    out = 0.0
    for s, val in zip(parts, values):
        p = jnp.exp2(s * SCALE - top)
        total = total + jnp.sum(p, axis=1, keepdims=True)
        out = out + nn(p.astype(BF), val)
    return out / total, top + jnp.log2(total)


def local_kernel(info, q, k, v, ko, vo, out, mass):
    head = pl.program_id(0)
    near = info[I_NEAR + head // GH]
    extra = [jnp.where(near == i, 1.0, 0.0).astype(F32) for i in range(2)]

    def tile(t, with_other):
        rows = pl.ds(t * 256, 256)
        qt = q[rows, :]
        width = (t + 1) * 256
        s = nt(qt, k[0:width, :])
        ri = lax.broadcasted_iota(jnp.int32, (256, 256), 0)
        ci = lax.broadcasted_iota(jnp.int32, (256, 256), 1)
        diag = jnp.where(ri >= ci, s[:, t * 256 :], LOW)
        s = diag if t == 0 else jnp.concatenate([s[:, : t * 256], diag], axis=1)
        scores = [(s, v[0:width, :])]
        if with_other:
            scores.append((nt(qt, ko[...]), vo[...]))
        ps = [[] for _ in scores]
        totals, tops = [], []
        for i in range(2):
            mine = [sc[i * 128 : (i + 1) * 128] for sc, _ in scores]
            top = functools.reduce(jnp.maximum, [jnp.max(m, axis=1, keepdims=True) for m in mine]) * SCALE
            raised = top - extra[i]
            total = 0.0
            for n, m in enumerate(mine):
                pieces = []
                for j in range(m.shape[1] // 128):
                    p = jnp.exp2(m[:, j * 128 : (j + 1) * 128] * SCALE - (raised if j % 2 == i else top))
                    total = total + p
                    pieces.append(p.astype(BF))
                ps[n].append(jnp.concatenate(pieces, axis=1))
            totals.append(jnp.sum(total, axis=1, keepdims=True))
            tops.append(top)
        acc = 0.0
        for n, (_, val) in enumerate(scores):
            acc = acc + nn(jnp.concatenate(ps[n], axis=0), val)
        total = jnp.concatenate(totals, axis=0)
        top = jnp.concatenate(tops, axis=0)
        out[rows, :] = acc / total
        lane = lax.broadcasted_iota(jnp.int32, (256, HD), 1)
        mass[rows, :] = jnp.where(lane == head, top + jnp.log2(total), mass[rows, :])

    for with_other in (False, True):

        @pl.when(info[I_CORE] == int(with_other))
        def _():
            tile(0, with_other)
            tile(1, with_other)


def near_kernel(group, info, qr, k0, k1, ko0, ko1, v0, v1, vo0, vo1, out):
    @pl.when(info[I_ODD] == 0)
    def _():
        lane = lax.broadcasted_iota(jnp.int32, (NSEL, HD), 1)
        stats = jnp.zeros((NSEL, HD), F32)
        for h in range(GH):
            cols = slice(h * HD, (h + 1) * HD)
            keys = jnp.concatenate([r[:, cols] for r in (k0, k1, ko0, ko1)], axis=0)
            vals = jnp.concatenate([r[:, cols] for r in (v0, v1, vo0, vo1)], axis=0)
            o, m = softmax_parts([nt(qr[:, cols], keys)], [vals])
            out[:, cols] = o.astype(BF)
            for n, term in enumerate(three(m)):
                stats = jnp.where(lane == n * GH + h, term, stats)
        out[:, GW:] = stats.astype(BF)


def far_kernel(info, mine, other, out):
    @pl.when(info[I_FACTIVE] == 1)
    def _():
        late = info[I_CORE] == 1
        for t in range(4):
            upto = 4 * t + 4
            q = mine[4 * t : upto, 0].reshape(256, HD)
            ri = lax.broadcasted_iota(jnp.int32, (256, 256), 0)
            ci = lax.broadcasted_iota(jnp.int32, (256, 256), 1)
            own_ok = (ci // HALF < ri // HALF) | ((ci // HALF == ri // HALF) & (ci <= ri))
            oth_ok = (ci // HALF < ri // HALF) | ((ci // HALF == ri // HALF) & late)
            parts, vals = [], []
            for source, ok in ((mine, own_ok), (other, oth_ok)):
                s = nt(q, source[0:upto, 1].reshape(upto * HALF, HD))
                d = jnp.where(ok, s[:, t * 256 :], LOW)
                parts.append(d if t == 0 else jnp.concatenate([s[:, : t * 256], d], axis=1))
                vals.append(source[0:upto, 2].reshape(upto * HALF, HD))
            o, m = softmax_parts(parts, vals)
            o = o.astype(BF)
            turned = jnp.transpose(jnp.broadcast_to(m, (256, HD)))[0:16]
            row = lax.broadcasted_iota(jnp.int32, (16, 256), 0)
            stats = jnp.zeros((16, 256), F32)
            for n, term in enumerate(three(turned)):
                stats = jnp.where(row == n, term, stats)
            stats = stats.astype(BF)
            for b in range(4):
                out[4 * t + b, 0:HALF] = o[b * HALF : (b + 1) * HALF]
                out[4 * t + b, HALF:] = stats[:, (b // 2) * 128 : (b // 2) * 128 + 128]


def merge_kernel(info, local_out, mass, near, far_own, far_oth, out):
    g = pl.program_id(0)
    core = info[I_CORE]
    near_par = info[I_NEAR + g]
    odd = info[I_ODD] == 1
    far_here = info[I_FMINE + g] == 1
    far_blk = info[I_FBLK + g] % 4
    second = info[I_PAR] == 1
    lane = lax.broadcasted_iota(jnp.int32, (BLK, HD), 1)

    def column(array, place):
        picked = jnp.where(lane == place, array, 0.0)
        return jnp.sum(picked, axis=1, keepdims=True)

    for h in range(GH):
        cols = slice(h * HD, (h + 1) * HD)
        halves, masses = [], []
        for source in (far_own, far_oth):
            halves.append(source[h, 0, 0:HALF].astype(F32))
            st = source[h, 0, HALF:].astype(F32)
            line = st[0:1] + st[1:2] + st[2:3]
            turned = jnp.transpose(jnp.broadcast_to(line, (128, 128)))
            masses.append(jnp.where(second, turned[HALF:], turned[:HALF]))
        first = core == 0
        far_o = jnp.concatenate(
            [jnp.where(first, halves[0], halves[1]), jnp.where(first, halves[1], halves[0])], axis=0
        )
        far_m = jnp.concatenate(
            [jnp.where(first, masses[0], masses[1]), jnp.where(first, masses[1], masses[0])], axis=0
        )
        for i in range(4):
            rows = slice(i * BLK, (i + 1) * BLK)
            half = slice((i // 2) * BLK, (i // 2 + 1) * BLK)
            m0 = column(mass[rows, :], g * GH + h)
            st = near[0, half, GW:].astype(F32)
            st = jnp.where((lane == h) | (lane == GH + h) | (lane == 2 * GH + h), st, 0.0)
            near_on = odd & (near_par == i % 2)
            m1 = jnp.where(near_on, jnp.sum(st, axis=1, keepdims=True), LOW)
            o1 = jnp.where(near_on, near[0, half, cols].astype(F32), 0.0)
            far_on = far_here & (far_blk == i)
            m2 = jnp.where(far_on, far_m, LOW)
            o2 = jnp.where(far_on, far_o, 0.0)
            top = jnp.maximum(jnp.maximum(m0, m1), m2)
            e0, e1, e2 = jnp.exp2(m0 - top), jnp.exp2(m1 - top), jnp.exp2(m2 - top)
            mixed = (e0 * local_out[rows, cols] + e1 * o1 + e2 * o2) / (e0 + e1 + e2)
            out[rows, cols] = mixed.astype(BF)


def device_part(q, k, v, offsets):
    x, y, z, c = (lax.axis_index(a) for a in AXES)
    near_off, far_off = offsets[0], offsets[1]
    far_z = far_off // 8
    far_blk = far_off % 8
    info = jnp.concatenate(
        [
            jnp.stack([c, z % 2, (far_z[y] == z).astype(jnp.int32), y % 2]).astype(jnp.int32),
            near_off,
            far_blk,
            ((far_z == z) & (far_blk // 4 == c)).astype(jnp.int32),
        ]
    )

    packed = pl.pallas_call(
        pack_first,
        out_shape=[jax.ShapeDtypeStruct((NSEL, GW), BF)] * GROUPS
        + [jax.ShapeDtypeStruct((GROUPS, 3, HALF, GW), BF)],
        in_specs=[SMEM, ANY, ANY, ANY],
        out_specs=[ANY] * (GROUPS + 1),
        scratch_shapes=[pltpu.SemaphoreType.DMA((5 * GROUPS,))],
        cost_estimate=cost(0, 4 << 20),
        name="pack_first",
    )(info, q, k, v)
    near_q, far_send = packed[:GROUPS], packed[GROUPS]

    far_recv = move(far_send, CORE)
    near_recv = [move(a, TO_EVEN) for a in near_q]
    ko, vo = move(k, CORE), move(v, CORE)

    far_pack = pl.pallas_call(
        pack_second,
        out_shape=jax.ShapeDtypeStruct((HEADS, 3, HALF, HD), BF),
        in_specs=[SMEM, ANY, ANY, ANY, ANY],
        out_specs=ANY,
        scratch_shapes=[pltpu.SemaphoreType.DMA((HEADS * 3,))],
        cost_estimate=cost(0, 3 << 20),
        name="pack_second",
    )(info, q, k, v, far_recv)
    far_mine = lax.all_to_all(far_pack, ("x", "y"), 0, 0, tiled=True)
    far_other = move(far_mine, CORE)
    far_out = pl.pallas_call(
        far_kernel,
        out_shape=jax.ShapeDtypeStruct((HEADS, HALF + 16, HD), BF),
        in_specs=[SMEM, pl.BlockSpec(memory_space=pltpu.VMEM), pl.BlockSpec(memory_space=pltpu.VMEM)],
        out_specs=pl.BlockSpec(memory_space=pltpu.VMEM),
        compiler_params=pltpu.CompilerParams(**PARAMS),
        cost_estimate=cost(4 * 1024 * 1280 * 128, 2 << 20, 1024 * 1280),
        name="far",
    )(info, far_mine, far_other)
    far_back = lax.all_to_all(far_out, ("x", "y"), 0, 0, tiled=True)
    far_back_other = move(far_back, CORE)

    near_back = []
    for g in range(GROUPS):

        def sel(half, g=g):
            return pl.BlockSpec((BLK, GW), lambda i, info: (info[I_NEAR + g] + 2 * half, g))

        near_out = pl.pallas_call(
            functools.partial(near_kernel, g),
            out_shape=jax.ShapeDtypeStruct((NSEL, GW + HD), BF),
            grid_spec=pltpu.PrefetchScalarGridSpec(
                num_scalar_prefetch=1,
                grid=(1,),
                in_specs=[pl.BlockSpec((NSEL, GW), lambda i, info: (0, 0))]
                + [sel(0), sel(1)] * 4,
                out_specs=pl.BlockSpec((NSEL, GW + HD), lambda i, info: (0, 0)),
            ),
            compiler_params=pltpu.CompilerParams(**PARAMS),
            cost_estimate=cost(4 * 4 * NSEL * 512 * HD, 2 << 20, 4 * NSEL * 512),
            name="near",
        )(info, near_recv[g], k, k, ko, ko, v, v, vo, vo)
        near_back.append(move(near_out, TO_ODD))

    def head_block():
        return pl.BlockSpec((ROWS, HD), lambda h, info: (0, h))

    local_out, mass = pl.pallas_call(
        local_kernel,
        out_shape=[
            jax.ShapeDtypeStruct((ROWS, HEADS * HD), F32),
            jax.ShapeDtypeStruct((ROWS, HD), F32),
        ],
        grid_spec=pltpu.PrefetchScalarGridSpec(
            num_scalar_prefetch=1,
            grid=(HEADS,),
            in_specs=[head_block()] * 5,
            out_specs=[head_block(), pl.BlockSpec((ROWS, HD), lambda h, info: (0, 0))],
        ),
        compiler_params=pltpu.CompilerParams(**PARAMS),
        cost_estimate=cost(4 * 16 * 512 * 832 * HD, 15 << 20, 16 * 512 * 832),
        name="local",
    )(info, q, k, v, ko, vo)

    def far_spec():
        return pl.BlockSpec((GH, 1, HALF + 16, HD), lambda g, info: (0, g, 0, 0))

    return pl.pallas_call(
        merge_kernel,
        out_shape=jax.ShapeDtypeStruct((ROWS, HEADS * HD), BF),
        grid_spec=pltpu.PrefetchScalarGridSpec(
            num_scalar_prefetch=1,
            grid=(GROUPS,),
            in_specs=[
                pl.BlockSpec((ROWS, GW), lambda g, info: (0, g)),
                pl.BlockSpec((ROWS, HD), lambda g, info: (0, 0)),
                pl.BlockSpec((1, NSEL, GW + HD), lambda g, info: (g, 0, 0)),
                far_spec(),
                far_spec(),
            ],
            out_specs=pl.BlockSpec((ROWS, GW), lambda g, info: (0, g)),
        ),
        compiler_params=pltpu.CompilerParams(**PARAMS),
        cost_estimate=cost(1 << 22, 8 << 20),
        name="merge",
    )(
        info,
        local_out,
        mass,
        jnp.stack(near_back),
        far_back.reshape(GH, GROUPS, HALF + 16, HD),
        far_back_other.reshape(GH, GROUPS, HALF + 16, HD),
    )


def solution(mesh):
    cube = Mesh(mesh.devices.reshape(SIZES), AXES)
    rows = P(AXES, None)
    return jax.shard_map(
        device_part, mesh=cube, in_specs=(rows, rows, rows, P()), out_specs=rows, check_vma=False
    )
```

time: 539 us -> 189 us (0.35)
  the two profiles are of different devices: /device:TPU:5 before, /device:TPU:65 now
where the time goes in v1:
time: 189 us; the launch traced here: 187 us
  Pallas kernels  131 us (69%)
  starting transfers between devices  21.2 us (11%)
  blocking collectives  20.1 us (11%)
  local copies, waits for them, and re-layouts  9.67 us (5%)
  other arithmetic  2.07 us (1%)
    pallas_call x1, Pallas kernels, device_part(): pl.pallas_call(pack_first, out_shape=[jax.ShapeDtypeStruct((NSEL, GW), BF...  57.5 us
    pallas_call x1, Pallas kernels, device_part(): pl.pallas_call(pack_second, out_shape=jax.ShapeDtypeStruct((HEADS, 3, HAL...  26.1 us
    pallas_call x1, Pallas kernels, device_part(): pl.pallas_call(local_kernel, out_shape=[jax.ShapeDtypeStruct((ROWS, HEADS...  22.5 us
    all_to_all x1, blocking collectives, device_part(): far_mine = lax.all_to_all(far_pack, ('x', 'y'), 0, 0, tiled=True)  20.1 us
    ppermute x13, starting transfers between devices, move(): return lax.ppermute(array, AXES, pairs)  17.7 us
    pallas_call x4, Pallas kernels, device_part(): pl.pallas_call(functools.partial(near_kernel, g), out_shape=jax.ShapeDtyp...  13.8 us
    unnamed x20, local copies, waits for them, and re-layouts  7.66 us
    pallas_call x1, Pallas kernels, device_part(): pl.pallas_call(merge_kernel, out_shape=jax.ShapeDtypeStruct((ROWS, HEADS...  7.53 us
  transfers between devices with their start and end apart: 14, of which 1 were waited for; matrix products, arithmetic and copies ran while one was open for 1% of the time, Pallas kernels for 35%

profile of v1, /device:TPU:65, one launch (start us, length us, event | category | flops | bytes accessed | tf_op | source)
XLA Modules:
  0.0 186.9 jit_solution(13135606883269407166)
XLA Ops:
  3.4 57.5 %pack_first.1 = (bf16[256,512]{1,0:T(8,128)(2,1)}, bf16[256,512]{1,0:T(8,128)(2,1)}, bf16[256,512]{1,0:T(8,128)(2,1)}, bf16[256,512]{1,0:T(8,128)(2,1)}, bf16[4,3,64,512]{3,2,1,0:T(8,128)(2,1)}) custom-call(s32[16]{0:T(128)} %concatenate.3.info, bf16[512,2048]{1,0:T(8,128)(2,1)} %q.5, bf16[512,2048]{1,0:T(8,128)(2,1)} %k.5, bf16[512,2048]{1,0:T(8,128)(2,1)} %v.5), custom_call_target="tpu_custom_call" | custom-call | bytes 4194304 | tf_op jit(solution)/shard_map/pack_first/pallas_call | solution.py:307
  62.2 1.6 collective-permute-done.10.received
  64.7 26.1 %pack_second.1 = bf16[16,3,64,128]{3,2,1,0:T(8,128)(2,1)} custom-call(s32[16]{0:T(128)} %concatenate.3.info, bf16[512,2048]{1,0:T(8,128)(2,1)} %q.5, bf16[512,2048]{1,0:T(8,128)(2,1)} %k.5, bf16[512,2048]{1,0:T(8,128)(2,1)} %v.5, bf16[4,3,64,512]{3,2,1,0:T(8,128)(2,1)} %copy-done.9), custom_call_target="tpu_custom_call" | custom-call | bytes 3145728 | tf_op jit(solution)/shard_map/pack_second/pallas_call | solution.py:323
  90.8 20.1 %all_to_all.10.mine = bf16[16,3,64,128]{3,2,1,0:T(8,128)(2,1)S(1)} all-to-all(bf16[16,3,64,128]{3,2,1,0:T(8,128)(2,1)} %pack_second.1), channel_id=1, replica_groups=mesh['x'=4,'y'=4,'z'=4,'c'=2] {'x','y'}, dimensions={0} | all-to-all | bytes 1572864 | tf_op jit(solution)/shard_map/all_to_all | solution.py:332
  110.9 1.8 collective-permute-start.11
  112.6 1.3 collective-permute-start.2
  113.9 1.3 collective-permute-start.4
  115.2 1.3 collective-permute-start.6
  116.5 3.8 %far.1 = bf16[16,80,128]{2,1,0:T(8,128)(2,1)} custom-call(s32[16]{0:T(128)S(1)} %copy-done.8, bf16[16,3,64,128]{3,2,1,0:T(8,128)(2,1)S(1)} %all_to_all.10.mine, bf16[16,3,64,128]{3,2,1,0:T(8,128)(2,1)S(1)} %collective-permute-done.11.other), custom_call_target="tpu_custom_call" | custom-call | flops 671088640 | bytes 2097152 | tf_op jit(solution)/shard_map/far/pallas_call | solution.py:334
  120.4 3.5 %all-to-all-start.1 = ((bf16[16,80,128]{2,1,0:T(8,128)(2,1)}), bf16[16,80,128]{2,1,0:T(8,128)(2,1)S(1)}, u32[]{:S(2)}, u32[]{:S(2)}) async-start(bf16[16,80,128]{2,1,0:T(8,128)(2,1)} %far.1), calls=%async_computation.1 | async-start | bytes 655360 | tf_op jit(solution)/shard_map/all_to_all | solution.py:343
  124.6 1.3 collective-permute-start.8
  126.0 1.2 copy-done.7
  127.1 3.3 %near.4 = bf16[256,640]{1,0:T(8,128)(2,1)S(1)} custom-call(s32[16]{0:T(128)S(1)} %copy-done.8, bf16[256,512]{1,0:T(8,128)(2,1)S(1)} %copy-done.7, bf16[512,2048]{1,0:T(8,128)(2,1)} %k.5, bf16[512,2048]{1,0:T(8,128)(2,1)} %k.5, bf16[512,2048]{1,0:T(8,128)(2,1)S(1)} %collective-permute-done.ko.ko0.ko1, bf16[512,2048]{1,0:T(8,128)(2,1)S(1)} %collective-permute-done.ko.ko0.ko1, ...), custom_call_target="tpu_custom_call" | custom-call | flops 268435456 | bytes 2097152 | tf_op jit(solution)/shard_map/near/pallas_call | solution.py:352
  130.4 3.2 %collective-permute-start.3 = (bf16[256,640]{1,0:T(8,128)(2,1)S(1)}, bf16[256,640]{1,0:T(8,128)(2,1)}, u32[]{:S(2)}, u32[]{:S(2)}) collective-permute-start(bf16[256,640]{1,0:T(8,128)(2,1)S(1)} %near.4), channel_id=1, source_target_pairs={{0,2},{1,3},{4,6},{5,7},{8,10},{9,11},{12,14},{13,15},{16,18},{17,... | collective-permute-start | bytes 983048 | tf_op jit(solution)/shard_map/ppermute | solution.py:45
  135.3 3.3 %near.5 = bf16[256,640]{1,0:T(8,128)(2,1)S(1)} custom-call(s32[16]{0:T(128)S(1)} %copy-done.8, bf16[256,512]{1,0:T(8,128)(2,1)S(1)} %copy-done.5, bf16[512,2048]{1,0:T(8,128)(2,1)} %k.5, bf16[512,2048]{1,0:T(8,128)(2,1)} %k.5, bf16[512,2048]{1,0:T(8,128)(2,1)S(1)} %collective-permute-done.ko.ko0.ko1, bf16[512,2048]{1,0:T(8,128)(2,1)S(1)} %collective-permute-done.ko.ko0.ko1, ...), custom_call_target="tpu_custom_call" | custom-call | flops 268435456 | bytes 2097152 | tf_op jit(solution)/shard_map/near/pallas_call | solution.py:352
  138.5 2.1 %collective-permute-start.5 = (bf16[256,640]{1,0:T(8,128)(2,1)S(1)}, bf16[256,640]{1,0:T(8,128)(2,1)}, u32[]{:S(2)}, u32[]{:S(2)}) collective-permute-start(bf16[256,640]{1,0:T(8,128)(2,1)S(1)} %near.5), channel_id=1, source_target_pairs={{0,2},{1,3},{4,6},{5,7},{8,10},{9,11},{12,14},{13,15},{16,18},{17,... | collective-permute-start | bytes 983048 | tf_op jit(solution)/shard_map/ppermute | solution.py:45
  142.3 3.3 %near.6 = bf16[256,640]{1,0:T(8,128)(2,1)S(1)} custom-call(s32[16]{0:T(128)S(1)} %copy-done.8, bf16[256,512]{1,0:T(8,128)(2,1)S(1)} %copy-done.3, bf16[512,2048]{1,0:T(8,128)(2,1)} %k.5, bf16[512,2048]{1,0:T(8,128)(2,1)} %k.5, bf16[512,2048]{1,0:T(8,128)(2,1)S(1)} %collective-permute-done.ko.ko0.ko1, bf16[512,2048]{1,0:T(8,128)(2,1)S(1)} %collective-permute-done.ko.ko0.ko1, ...), custom_call_target="tpu_custom_call" | custom-call | flops 268435456 | bytes 2097152 | tf_op jit(solution)/shard_map/near/pallas_call | solution.py:352
  145.5 2.0 %collective-permute-start.7 = (bf16[256,640]{1,0:T(8,128)(2,1)S(1)}, bf16[256,640]{1,0:T(8,128)(2,1)}, u32[]{:S(2)}, u32[]{:S(2)}) collective-permute-start(bf16[256,640]{1,0:T(8,128)(2,1)S(1)} %near.6), channel_id=1, source_target_pairs={{0,2},{1,3},{4,6},{5,7},{8,10},{9,11},{12,14},{13,15},{16,18},{17,... | collective-permute-start | bytes 983048 | tf_op jit(solution)/shard_map/ppermute | solution.py:45
  147.5 4.0 %near.7 = bf16[256,640]{1,0:T(8,128)(2,1)} custom-call(s32[16]{0:T(128)S(1)} %copy-done.8, bf16[256,512]{1,0:T(8,128)(2,1)S(1)} %collective-permute-done.8.qr, bf16[512,2048]{1,0:T(8,128)(2,1)} %k.5, bf16[512,2048]{1,0:T(8,128)(2,1)} %k.5, bf16[512,2048]{1,0:T(8,128)(2,1)S(1)} %collective-permute-done.ko.ko0.ko1, ...), custom_call_target="tpu_custom_call" | custom-call | flops 268435456 | bytes 2097152 | tf_op jit(solution)/shard_map/near/pallas_call | solution.py:352
  151.5 1.3 collective-permute-start.9
  153.8 1.6 copy-done.1
  155.4 22.5 %local.1 = (f32[512,2048]{1,0:T(8,128)}, f32[512,128]{1,0:T(8,128)S(1)}) custom-call(s32[16]{0:T(128)S(1)} %copy-done.8, bf16[512,2048]{1,0:T(8,128)(2,1)S(1)} %copy-done.1, bf16[512,2048]{1,0:T(8,128)(2,1)} %k.5, bf16[512,2048]{1,0:T(8,128)(2,1)} %v.5, bf16[512,2048]{1,0:T(8,128)(2,1)} %copy-done, bf16[512,2048]{1,0:T(8,128)(2,1)} %collective-permute-done.1.vo.vo0.vo1), custom_call_target="tpu_custom_call" | custom-call | flops 3489660928 | bytes 15728640 | tf_op jit(solution)/shard_map/local/pallas_call | solution.py:371
  177.9 1.4 pad_maximum_fusion.near
  179.3 7.5 %merge.1 = bf16[512,2048]{1,0:T(8,128)(2,1)} custom-call(s32[16]{0:T(128)S(1)} %copy-done.8, f32[512,2048]{1,0:T(8,128)} %get-tuple-element.12.local_out, f32[512,128]{1,0:T(8,128)S(1)} %get-tuple-element.13.mass, bf16[4,256,640]{2,1,0:T(8,128)(2,1)S(1)} %pad_maximum_fusion.near, bf16[4,4,80,128]{3,2,1,0:T(8,128)(2,1)S(1)} %bitcast.26, ...), custom_call_target="tpu_custom_call" | custom-call | flops 4194304 | bytes 8388608 | tf_op jit(solution)/shard_map/merge/pallas_call | solution.py:391
  (40 shorter events, 9.9 us)
Async XLA Ops:
  61.0 2.9 %collective-permute-start.10 = (bf16[4,3,64,512]{3,2,1,0:T(8,128)(2,1)}, bf16[4,3,64,512]{3,2,1,0:T(8,128)(2,1)S(1)}, u32[]{:S(2)}, u32[]{:S(2)}) collective-permute-start(bf16[4,3,64,512]{3,2,1,0:T(8,128)(2,1)} %get-tuple-element.18), channel_id=1, source_target_pairs={{0,1},{1,0},{2,3},{3,2},{4,5},{5,4},{6,7},{7,6},{8,9},{9,8},{10,11... | collective-permute-start | bytes 2359304 | tf_op jit(solution)/shard_map/ppermute | solution.py:45
  61.7 64.2 %collective-permute-start = (bf16[512,2048]{1,0:T(8,128)(2,1)}, bf16[512,2048]{1,0:T(8,128)(2,1)S(1)}, u32[]{:S(2)}, u32[]{:S(2)}) collective-permute-start(bf16[512,2048]{1,0:T(8,128)(2,1)} %k.5), channel_id=1, source_target_pairs={{0,1},{1,0},{2,3},{3,2},{4,5},{5,4},{6,7},{7,6},{8,9},{9,8},{10,11... | collective-permute-start | bytes 6291464 | tf_op jit(solution)/shard_map/ppermute | solution.py:45
  61.8 64.1 %collective-permute-start.1 = (bf16[512,2048]{1,0:T(8,128)(2,1)}, bf16[512,2048]{1,0:T(8,128)(2,1)}, u32[]{:S(2)}, u32[]{:S(2)}) collective-permute-start(bf16[512,2048]{1,0:T(8,128)(2,1)} %v.5), channel_id=1, source_target_pairs={{0,1},{1,0},{2,3},{3,2},{4,5},{5,4},{6,7},{7,6},{8,9},{9,8},{10,11... | collective-permute-start | bytes 6291464 | tf_op jit(solution)/shard_map/ppermute | solution.py:45
  63.8 0.9 copy-start.9
  90.8 25.8 %copy-start.8 = (s32[16]{0:T(128)S(1)}, s32[16]{0:T(128)}, u32[]{:S(2)}) copy-start(s32[16]{0:T(128)} %concatenate.3.info) | copy-start | bytes 196
  110.9 4.4 %collective-permute-start.11 = (bf16[16,3,64,128]{3,2,1,0:T(8,128)(2,1)S(1)}, bf16[16,3,64,128]{3,2,1,0:T(8,128)(2,1)S(1)}, u32[]{:S(2)}, u32[]{:S(2)}) collective-permute-start(bf16[16,3,64,128]{3,2,1,0:T(8,128)(2,1)S(1)} %all_to_all.10.mine), channel_id=1, source_target_pairs={{0,1},{1,0},{2,3},{3,2},{4,5},{5,4},{6,7},{7,6},{8,9},{9,8},{10,11... | collective-permute-start | bytes 2359304 | tf_op jit(solution)/shard_map/ppermute | solution.py:45
  112.6 11.3 %collective-permute-start.2 = (bf16[256,512]{1,0:T(8,128)(2,1)}, bf16[256,512]{1,0:T(8,128)(2,1)S(1)}, u32[]{:S(2)}, u32[]{:S(2)}) collective-permute-start(bf16[256,512]{1,0:T(8,128)(2,1)} %get-tuple-element.14), channel_id=1, source_target_pairs={{2,0},{3,1},{6,4},{7,5},{10,8},{11,9},{14,12},{15,13},{18,16},{19,... | collective-permute-start | bytes 786440 | tf_op jit(solution)/shard_map/ppermute | solution.py:45
  113.9 19.7 %collective-permute-start.4 = (bf16[256,512]{1,0:T(8,128)(2,1)}, bf16[256,512]{1,0:T(8,128)(2,1)S(1)}, u32[]{:S(2)}, u32[]{:S(2)}) collective-permute-start(bf16[256,512]{1,0:T(8,128)(2,1)} %get-tuple-element.15), channel_id=1, source_target_pairs={{2,0},{3,1},{6,4},{7,5},{10,8},{11,9},{14,12},{15,13},{18,16},{19,... | collective-permute-start | bytes 786440 | tf_op jit(solution)/shard_map/ppermute | solution.py:45
  115.2 25.4 %collective-permute-start.6 = (bf16[256,512]{1,0:T(8,128)(2,1)}, bf16[256,512]{1,0:T(8,128)(2,1)S(1)}, u32[]{:S(2)}, u32[]{:S(2)}) collective-permute-start(bf16[256,512]{1,0:T(8,128)(2,1)} %get-tuple-element.16), channel_id=1, source_target_pairs={{2,0},{3,1},{6,4},{7,5},{10,8},{11,9},{14,12},{15,13},{18,16},{19,... | collective-permute-start | bytes 786440 | tf_op jit(solution)/shard_map/ppermute | solution.py:45
  120.4 32.5 %all-to-all-start.1 = ((bf16[16,80,128]{2,1,0:T(8,128)(2,1)}), bf16[16,80,128]{2,1,0:T(8,128)(2,1)S(1)}, u32[]{:S(2)}, u32[]{:S(2)}) async-start(bf16[16,80,128]{2,1,0:T(8,128)(2,1)} %far.1), calls=%async_computation.1 | async-start | bytes 655360 | tf_op jit(solution)/shard_map/all_to_all | solution.py:343
  123.9 0.7 copy-start.6
  124.6 22.9 %collective-permute-start.8 = (bf16[256,512]{1,0:T(8,128)(2,1)}, bf16[256,512]{1,0:T(8,128)(2,1)S(1)}, u32[]{:S(2)}, u32[]{:S(2)}) collective-permute-start(bf16[256,512]{1,0:T(8,128)(2,1)} %get-tuple-element.17), channel_id=1, source_target_pairs={{2,0},{3,1},{6,4},{7,5},{10,8},{11,9},{14,12},{15,13},{18,16},{19,... | collective-permute-start | bytes 786440 | tf_op jit(solution)/shard_map/ppermute | solution.py:45
  125.9 21.6 %copy-start = (bf16[512,2048]{1,0:T(8,128)(2,1)}, bf16[512,2048]{1,0:T(8,128)(2,1)S(1)}, u32[]{:S(2)}) copy-start(bf16[512,2048]{1,0:T(8,128)(2,1)S(1)} %collective-permute-done.ko.ko0.ko1) | copy-start | bytes 6291460
  125.9 1.2 copy-start.7
  130.4 47.5 %collective-permute-start.3 = (bf16[256,640]{1,0:T(8,128)(2,1)S(1)}, bf16[256,640]{1,0:T(8,128)(2,1)}, u32[]{:S(2)}, u32[]{:S(2)}) collective-permute-start(bf16[256,640]{1,0:T(8,128)(2,1)S(1)} %near.4), channel_id=1, source_target_pairs={{0,2},{1,3},{4,6},{5,7},{8,10},{9,11},{12,14},{13,15},{16,18},{17,... | collective-permute-start | bytes 983048 | tf_op jit(solution)/shard_map/ppermute | solution.py:45
  133.6 0.7 copy-start.4
  134.3 0.9 copy-start.5
  138.5 39.4 %collective-permute-start.5 = (bf16[256,640]{1,0:T(8,128)(2,1)S(1)}, bf16[256,640]{1,0:T(8,128)(2,1)}, u32[]{:S(2)}, u32[]{:S(2)}) collective-permute-start(bf16[256,640]{1,0:T(8,128)(2,1)S(1)} %near.5), channel_id=1, source_target_pairs={{0,2},{1,3},{4,6},{5,7},{8,10},{9,11},{12,14},{13,15},{16,18},{17,... | collective-permute-start | bytes 983048 | tf_op jit(solution)/shard_map/ppermute | solution.py:45
  140.6 0.7 copy-start.2
  141.3 0.9 copy-start.3
  145.5 32.4 %collective-permute-start.7 = (bf16[256,640]{1,0:T(8,128)(2,1)S(1)}, bf16[256,640]{1,0:T(8,128)(2,1)}, u32[]{:S(2)}, u32[]{:S(2)}) collective-permute-start(bf16[256,640]{1,0:T(8,128)(2,1)S(1)} %near.6), channel_id=1, source_target_pairs={{0,2},{1,3},{4,6},{5,7},{8,10},{9,11},{12,14},{13,15},{16,18},{17,... | collective-permute-start | bytes 983048 | tf_op jit(solution)/shard_map/ppermute | solution.py:45
  151.5 26.4 %collective-permute-start.9 = (bf16[256,640]{1,0:T(8,128)(2,1)}, bf16[256,640]{1,0:T(8,128)(2,1)S(1)}, u32[]{:S(2)}, u32[]{:S(2)}) collective-permute-start(bf16[256,640]{1,0:T(8,128)(2,1)} %near.7), channel_id=1, source_target_pairs={{0,2},{1,3},{4,6},{5,7},{8,10},{9,11},{12,14},{13,15},{16,18},{17,... | collective-permute-start | bytes 983048 | tf_op jit(solution)/shard_map/ppermute | solution.py:45
  152.8 26.5 %collective-permute-start.12 = (bf16[16,80,128]{2,1,0:T(8,128)(2,1)S(1)}, bf16[16,80,128]{2,1,0:T(8,128)(2,1)S(1)}, u32[]{:S(2)}, u32[]{:S(2)}) collective-permute-start(bf16[16,80,128]{2,1,0:T(8,128)(2,1)S(1)} %all-to-all-done.1), channel_id=1, source_target_pairs={{0,1},{1,0},{2,3},{3,2},{4,5},{5,4},{6,7},{7,6},{8,9},{9,8},{10,11... | collective-permute-start | bytes 983048 | tf_op jit(solution)/shard_map/ppermute | solution.py:45
  153.8 1.6 copy-start.1

commit v2 on v1

v2 whole, which is shorter than its diff:
```python
import functools

import jax
import jax.numpy as jnp
import numpy as np
from jax import lax
from jax.experimental import pallas as pl
from jax.experimental.pallas import tpu as pltpu
from jax.sharding import Mesh
from jax.sharding import PartitionSpec as P

HD = 128
BLK = 128
HALF = 64
HEADS = 16
GROUPS = 4
GH = 4
GW = GH * HD
ROWS = 512
NSEL = 256
AXES = ("x", "y", "z", "c")
SIZES = (4, 4, 4, 2)
SCALE = float(HD**-0.5 * np.log2(np.e))
LOW = -1e30
BF, F32 = jnp.bfloat16, jnp.float32

I_CORE, I_ODD, I_FACTIVE, I_PAR, I_NEAR, I_FBLK, I_FMINE = 0, 1, 2, 3, 4, 8, 12


def route(step):
    pairs = []
    for index in np.ndindex(*SIZES):
        target = step(*index)
        if target is not None:
            pairs.append((int(np.ravel_multi_index(index, SIZES)), int(np.ravel_multi_index(target, SIZES))))
    return pairs


CORE = route(lambda x, y, z, c: (x, y, z, 1 - c))
TO_EVEN = route(lambda x, y, z, c: (x, y, z - 1, c) if z % 2 else None)
TO_ODD = route(lambda x, y, z, c: (x, y, z + 1, c) if z % 2 == 0 else None)


def move(array, pairs):
    return lax.ppermute(array, AXES, pairs)


def cost(flops, nbytes, exps=0):
    return pl.CostEstimate(flops=int(flops), bytes_accessed=int(nbytes), transcendentals=int(exps))


ANY = pl.BlockSpec(memory_space=pl.ANY)
SMEM = pl.BlockSpec(memory_space=pltpu.SMEM)
PARAMS = dict(vmem_limit_bytes=16 * 1024 * 1024)


def nt(a, b):
    return lax.dot_general(a, b, (((1,), (1,)), ((), ())), preferred_element_type=F32)


def nn(a, b):
    return lax.dot_general(a, b, (((1,), (0,)), ((), ())), preferred_element_type=F32)


def three(x):
    hi = x.astype(BF).astype(F32)
    rest = x - hi
    mid = rest.astype(BF).astype(F32)
    return hi, mid, rest - mid


def rows_at(first, count):
    return pl.ds(pl.multiple_of(first, count), count)


def pack_first(info, q, k, v, near0, near1, near2, near3, far_out):
    for g, near in enumerate((near0, near1, near2, near3)):
        cols = slice(g * GW, (g + 1) * GW)
        for half in range(2):
            near[half * BLK : (half + 1) * BLK, :] = q[rows_at((info[I_NEAR + g] + 2 * half) * BLK, BLK), cols]
        away = rows_at((info[I_FBLK + g] % 4) * BLK + (1 - info[I_CORE]) * HALF, HALF)
        for t, source in enumerate((q, k, v)):
            far_out[g, t] = source[away, cols]


def pack_second(info, q, k, v, received, out):
    for g in range(GROUPS):
        here = info[I_FBLK + g] // 4 == info[I_CORE]
        cols = slice(g * GW, (g + 1) * GW)
        kept = rows_at((info[I_FBLK + g] % 4) * BLK + info[I_CORE] * HALF, HALF)

        def put(pick, g=g):
            for t in range(3):
                for h in range(GH):
                    out[h * GROUPS + g, t] = pick(t)[:, h * HD : (h + 1) * HD]

        @pl.when(here)
        def _():
            put(lambda t: (q, k, v)[t][kept, cols])

        @pl.when(jnp.logical_not(here))
        def _():
            put(lambda t: received[g, t])


def softmax_parts(parts, values):
    top = functools.reduce(jnp.maximum, [jnp.max(s, axis=1, keepdims=True) for s in parts]) * SCALE
    total = 0.0
    out = 0.0
    for s, val in zip(parts, values):
        p = jnp.exp2(s * SCALE - top)
        total = total + jnp.sum(p, axis=1, keepdims=True)
        out = out + nn(p.astype(BF), val)
    return out / total, top + jnp.log2(total)


def local_kernel(info, q, k, v, ko, vo, out, mass):
    mass[...] = jnp.zeros_like(mass)

    def tile(head, t, with_other):
        rows = slice(t * 256, t * 256 + 256)
        cols = pl.ds(pl.multiple_of(head * HD, HD), HD)
        near = info[I_NEAR + head // GH]
        extra = [jnp.where(near == i, 1.0, 0.0).astype(F32) for i in range(2)]
        qt = q[rows, cols]
        width = (t + 1) * 256
        s = nt(qt, k[0:width, cols])
        ri = lax.broadcasted_iota(jnp.int32, (256, 256), 0)
        ci = lax.broadcasted_iota(jnp.int32, (256, 256), 1)
        diag = jnp.where(ri >= ci, s[:, t * 256 :], LOW)
        s = diag if t == 0 else jnp.concatenate([s[:, : t * 256], diag], axis=1)
        scores = [(s, v[0:width, cols])]
        if with_other:
            scores.append((nt(qt, ko[:, cols]), vo[:, cols]))
        ps = [[] for _ in scores]
        totals, tops = [], []
        for i in range(2):
            mine = [sc[i * 128 : (i + 1) * 128] for sc, _ in scores]
            top = functools.reduce(jnp.maximum, [jnp.max(m, axis=1, keepdims=True) for m in mine]) * SCALE
            raised = top - extra[i]
            total = 0.0
            for n, m in enumerate(mine):
                pieces = []
                for j in range(m.shape[1] // 128):
                    p = jnp.exp2(m[:, j * 128 : (j + 1) * 128] * SCALE - (raised if j % 2 == i else top))
                    total = total + p
                    pieces.append(p.astype(BF))
                ps[n].append(jnp.concatenate(pieces, axis=1))
            totals.append(jnp.sum(total, axis=1, keepdims=True))
            tops.append(top)
        acc = 0.0
        for n, (_, val) in enumerate(scores):
            acc = acc + nn(jnp.concatenate(ps[n], axis=0), val)
        total = jnp.concatenate(totals, axis=0)
        top = jnp.concatenate(tops, axis=0)
        out[rows, cols] = acc / total
        lane = lax.broadcasted_iota(jnp.int32, (256, HD), 1)
        mass[rows, :] = jnp.where(lane == head, top + jnp.log2(total), mass[rows, :])

    for with_other in (False, True):

        @pl.when(info[I_CORE] == int(with_other))
        def _():
            @pl.loop(0, HEADS)
            def _(head):
                tile(head, 0, with_other)
                tile(head, 1, with_other)


def near_kernel(group, info, qr, k, ko, v, vo, out):
    @pl.when(info[I_ODD] == 0)
    def _():
        first = info[I_NEAR + group] * BLK
        rows = [pl.ds(pl.multiple_of(first + 2 * half * BLK, BLK), BLK) for half in range(2)]
        lane = lax.broadcasted_iota(jnp.int32, (NSEL, HD), 1)
        stats = jnp.zeros((NSEL, HD), F32)
        for h in range(GH):
            cols = slice(h * HD, (h + 1) * HD)
            place = slice(group * GW + h * HD, group * GW + (h + 1) * HD)
            keys = jnp.concatenate([r[sel, place] for r in (k, ko) for sel in rows], axis=0)
            vals = jnp.concatenate([r[sel, place] for r in (v, vo) for sel in rows], axis=0)
            o, m = softmax_parts([nt(qr[:, cols], keys)], [vals])
            out[:, cols] = o.astype(BF)
            for n, term in enumerate(three(m)):
                stats = jnp.where(lane == n * GH + h, term, stats)
        out[:, GW:] = stats.astype(BF)


def far_kernel(info, mine, other, out):
    @pl.when(info[I_FACTIVE] == 1)
    def _():
        late = info[I_CORE] == 1
        for t in range(4):
            upto = 4 * t + 4
            q = mine[4 * t : upto, 0].reshape(256, HD)
            ri = lax.broadcasted_iota(jnp.int32, (256, 256), 0)
            ci = lax.broadcasted_iota(jnp.int32, (256, 256), 1)
            own_ok = (ci // HALF < ri // HALF) | ((ci // HALF == ri // HALF) & (ci <= ri))
            oth_ok = (ci // HALF < ri // HALF) | ((ci // HALF == ri // HALF) & late)
            parts, vals = [], []
            for source, ok in ((mine, own_ok), (other, oth_ok)):
                s = nt(q, source[0:upto, 1].reshape(upto * HALF, HD))
                d = jnp.where(ok, s[:, t * 256 :], LOW)
                parts.append(d if t == 0 else jnp.concatenate([s[:, : t * 256], d], axis=1))
                vals.append(source[0:upto, 2].reshape(upto * HALF, HD))
            o, m = softmax_parts(parts, vals)
            o = o.astype(BF)
            turned = jnp.transpose(jnp.broadcast_to(m, (256, HD)))[0:16]
            row = lax.broadcasted_iota(jnp.int32, (16, 256), 0)
            stats = jnp.zeros((16, 256), F32)
            for n, term in enumerate(three(turned)):
                stats = jnp.where(row == n, term, stats)
            stats = stats.astype(BF)
            for b in range(4):
                out[4 * t + b, 0:HALF] = o[b * HALF : (b + 1) * HALF]
                out[4 * t + b, HALF:] = stats[:, (b // 2) * 128 : (b // 2) * 128 + 128]


def merge_kernel(info, local_out, mass, near0, near1, near2, near3, far_own, far_oth, out, done, sems):
    core = info[I_CORE]
    odd = info[I_ODD] == 1
    second = info[I_PAR] == 1
    first = core == 0
    lane = lax.broadcasted_iota(jnp.int32, (BLK, HD), 1)

    def column(array, places):
        hit = functools.reduce(jnp.logical_or, [lane == p for p in places])
        return jnp.sum(jnp.where(hit, array, 0.0), axis=1, keepdims=True)

    copies = []
    for g, near in enumerate((near0, near1, near2, near3)):
        near_par = info[I_NEAR + g]
        far_here = info[I_FMINE + g] == 1
        far_blk = info[I_FBLK + g] % 4
        for h in range(GH):
            cols = slice(h * HD, (h + 1) * HD)
            place = slice(g * GW + h * HD, g * GW + (h + 1) * HD)
            halves, masses = [], []
            for source in (far_own, far_oth):
                tile = source[h * GROUPS + g]
                halves.append(tile[0:HALF].astype(F32))
                st = tile[HALF:].astype(F32)
                line = st[0:1] + st[1:2] + st[2:3]
                turned = jnp.transpose(jnp.broadcast_to(line, (128, 128)))
                masses.append(jnp.where(second, turned[HALF:], turned[:HALF]))
            far_o = jnp.concatenate(
                [jnp.where(first, halves[0], halves[1]), jnp.where(first, halves[1], halves[0])], axis=0
            )
            far_m = jnp.concatenate(
                [jnp.where(first, masses[0], masses[1]), jnp.where(first, masses[1], masses[0])], axis=0
            )
            for i in range(4):
                rows = slice(i * BLK, (i + 1) * BLK)
                half = slice((i // 2) * BLK, (i // 2 + 1) * BLK)
                m0 = column(mass[rows, :], [g * GH + h])
                near_on = odd & (near_par == i % 2)
                m1 = column(near[half, GW:].astype(F32), [h, GH + h, 2 * GH + h])
                m1 = jnp.where(near_on, m1, LOW)
                o1 = jnp.where(near_on, near[half, cols].astype(F32), 0.0)
                far_on = far_here & (far_blk == i)
                m2 = jnp.where(far_on, far_m, LOW)
                o2 = jnp.where(far_on, far_o, 0.0)
                top = jnp.maximum(jnp.maximum(m0, m1), m2)
                e0, e1, e2 = jnp.exp2(m0 - top), jnp.exp2(m1 - top), jnp.exp2(m2 - top)
                mixed = (e0 * local_out[rows, place] + e1 * o1 + e2 * o2) / (e0 + e1 + e2)
                done[rows, place] = mixed.astype(BF)
        part = pl.ds(g * GW, GW)
        copies.append(pltpu.make_async_copy(done.at[:, part], out.at[:, part], sems.at[g]))
        copies[-1].start()
    for copy in copies:
        copy.wait()


def device_part(q, k, v, offsets):
    x, y, z, c = (lax.axis_index(a) for a in AXES)
    near_off, far_off = offsets[0], offsets[1]
    far_z = far_off // 8
    far_blk = far_off % 8
    info = jnp.concatenate(
        [
            jnp.stack([c, z % 2, (far_z[y] == z).astype(jnp.int32), y % 2]).astype(jnp.int32),
            near_off,
            far_blk,
            ((far_z == z) & (far_blk // 4 == c)).astype(jnp.int32),
        ]
    )

    vmem = pl.BlockSpec(memory_space=pltpu.VMEM)
    packed = pl.pallas_call(
        pack_first,
        out_shape=[jax.ShapeDtypeStruct((NSEL, GW), BF)] * GROUPS
        + [jax.ShapeDtypeStruct((GROUPS, 3, HALF, GW), BF)],
        in_specs=[SMEM] + [vmem] * 3,
        out_specs=[vmem] * (GROUPS + 1),
        compiler_params=pltpu.CompilerParams(**PARAMS),
        cost_estimate=cost(0, 4 << 20),
        name="pack_first",
    )(info, q, k, v)
    near_q, far_send = packed[:GROUPS], packed[GROUPS]

    far_recv = move(far_send, CORE)
    near_recv = [move(a, TO_EVEN) for a in near_q]
    ko, vo = move(k, CORE), move(v, CORE)

    far_pack = pl.pallas_call(
        pack_second,
        out_shape=jax.ShapeDtypeStruct((HEADS, 3, HALF, HD), BF),
        in_specs=[SMEM] + [vmem] * 4,
        out_specs=vmem,
        compiler_params=pltpu.CompilerParams(**PARAMS),
        cost_estimate=cost(0, 3 << 20),
        name="pack_second",
    )(info, q, k, v, far_recv)
    far_mine = lax.all_to_all(far_pack, ("x", "y"), 0, 0, tiled=True)
    far_other = move(far_mine, CORE)
    far_out = pl.pallas_call(
        far_kernel,
        out_shape=jax.ShapeDtypeStruct((HEADS, HALF + 16, HD), BF),
        in_specs=[SMEM, pl.BlockSpec(memory_space=pltpu.VMEM), pl.BlockSpec(memory_space=pltpu.VMEM)],
        out_specs=pl.BlockSpec(memory_space=pltpu.VMEM),
        compiler_params=pltpu.CompilerParams(**PARAMS),
        cost_estimate=cost(4 * 1024 * 1280 * 128, 2 << 20, 1024 * 1280),
        name="far",
    )(info, far_mine, far_other)
    far_back = lax.all_to_all(far_out, ("x", "y"), 0, 0, tiled=True)
    far_back_other = move(far_back, CORE)

    near_back = []
    for g in range(GROUPS):
        near_out = pl.pallas_call(
            functools.partial(near_kernel, g),
            out_shape=jax.ShapeDtypeStruct((NSEL, GW + HD), BF),
            in_specs=[SMEM] + [vmem] * 5,
            out_specs=vmem,
            compiler_params=pltpu.CompilerParams(**PARAMS),
            cost_estimate=cost(4 * 4 * NSEL * 512 * HD, 2 << 20, 4 * NSEL * 512),
            name="near",
        )(info, near_recv[g], k, ko, v, vo)
        near_back.append(move(near_out, TO_ODD))

    local_out, mass = pl.pallas_call(
        local_kernel,
        out_shape=[
            jax.ShapeDtypeStruct((ROWS, HEADS * HD), F32),
            jax.ShapeDtypeStruct((ROWS, HD), F32),
        ],
        in_specs=[SMEM] + [vmem] * 5,
        out_specs=[vmem] * 2,
        compiler_params=pltpu.CompilerParams(**PARAMS),
        cost_estimate=cost(4 * 16 * 512 * 832 * HD, 15 << 20, 16 * 512 * 832),
        name="local",
    )(info, q, k, v, ko, vo)

    return pl.pallas_call(
        merge_kernel,
        out_shape=jax.ShapeDtypeStruct((ROWS, HEADS * HD), BF),
        in_specs=[SMEM] + [vmem] * 8,
        out_specs=ANY,
        scratch_shapes=[pltpu.VMEM((ROWS, HEADS * HD), BF), pltpu.SemaphoreType.DMA((GROUPS,))],
        compiler_params=pltpu.CompilerParams(**PARAMS),
        cost_estimate=cost(1 << 22, 8 << 20),
        name="merge",
    )(info, local_out, mass, *near_back, far_back, far_back_other)


def solution(mesh):
    cube = Mesh(mesh.devices.reshape(SIZES), AXES)
    rows = P(AXES, None)
    return jax.shard_map(
        device_part, mesh=cube, in_specs=(rows, rows, rows, P()), out_specs=rows, check_vma=False
    )
```

time: 189 us -> 109 us (0.58)
  Pallas kernels: 131 us -> 55.3 us
  local copies, waits for them, and re-layouts: 9.67 us -> 4.62 us
  waiting for transfers between devices: 1.65 us -> 3.59 us
    pallas_call x1, Pallas kernels: 57.5 us -> 3.18 us  [device_part(): pl.pallas_call(pack_first, out_shape=[jax.ShapeDtypeStruct((NSEL, GW), BF...]
    pallas_call x1, Pallas kernels: 26.1 us -> 2.4 us  [device_part(): pl.pallas_call(pack_second, out_shape=jax.ShapeDtypeStruct((HEADS, 3, HAL...]
    pallas_call x4, Pallas kernels: 13.8 us -> 19.9 us  [device_part(): pl.pallas_call(functools.partial(near_kernel, g), out_shape=jax.ShapeDtyp...]
    unnamed x20 -> x4, local copies, waits for them, and re-layouts: 7.66 us -> 3.19 us
    pallas_call x1, Pallas kernels: 3.81 us -> 1.31 us  [device_part(): pl.pallas_call(far_kernel, out_shape=jax.ShapeDtypeStruct((HEADS, HALF +...]
    ppermute x13, waiting for transfers between devices: 1.64 us -> 3.59 us  [move(): return lax.ppermute(array, AXES, pairs)]
  transfers between devices with their start and end apart: 14 -> 14, of which waited for: 1 -> 2; matrix products, arithmetic and copies ran while one was open for 1% -> 0% of each run, Pallas kernels for 35% -> 43%
where the time goes in v2:
time: 109 us; the launch traced here: 107 us
  Pallas kernels  55.3 us (51%)
  starting transfers between devices  22.3 us (20%)
  blocking collectives  19.8 us (18%)
  local copies, waits for them, and re-layouts  4.62 us (4%)
  waiting for transfers between devices  3.59 us (3%)
    pallas_call x1, Pallas kernels, device_part(): pl.pallas_call(local_kernel, out_shape=[jax.ShapeDtypeStruct((ROWS, HEADS...  22.3 us
    pallas_call x4, Pallas kernels, device_part(): pl.pallas_call(functools.partial(near_kernel, g), out_shape=jax.ShapeDtyp...  19.9 us
    all_to_all x1, blocking collectives, device_part(): far_mine = lax.all_to_all(far_pack, ('x', 'y'), 0, 0, tiled=True)  19.8 us
    ppermute x13, starting transfers between devices, move(): return lax.ppermute(array, AXES, pairs)  18.7 us
    pallas_call x1, Pallas kernels, device_part(): pl.pallas_call(merge_kernel, out_shape=jax.ShapeDtypeStruct((ROWS, HEADS...  6.26 us
    ppermute x13, waiting for transfers between devices, move(): return lax.ppermute(array, AXES, pairs)  3.59 us
    all_to_all x1, starting transfers between devices, device_part(): far_back = lax.all_to_all(far_out, ('x', 'y'), 0, 0, tiled=True)  3.54 us
    unnamed x4, local copies, waits for them, and re-layouts  3.19 us
  transfers between devices with their start and end apart: 14, of which 2 were waited for; matrix products, arithmetic and copies ran while one was open for 0% of the time, Pallas kernels for 43%

profile of v2, /device:TPU:65, one launch (start us, length us, event | category | flops | bytes accessed | tf_op | source)
XLA Modules:
  0.0 107.4 jit_solution(9033389578891770880)
XLA Ops:
  2.9 1.6 %copy-done = bf16[512,2048]{1,0:T(8,128)(2,1)S(1)} copy-done((bf16[512,2048]{1,0:T(8,128)(2,1)S(1)}, bf16[512,2048]{1,0:T(8,128)(2,1)}, u32[]{:S(2)}) %copy-start) | copy-done | bytes 2097176
  4.5 3.2 %pack_first.1 = (bf16[256,512]{1,0:T(8,128)(2,1)S(1)}, bf16[256,512]{1,0:T(8,128)(2,1)}, bf16[256,512]{1,0:T(8,128)(2,1)}, bf16[256,512]{1,0:T(8,128)(2,1)}, bf16[4,3,64,512]{3,2,1,0:T(8,128)(2,1)S(1)}) custom-call(s32[16]{0:T(128)S(1)} %concatenate.3.info, bf16[512,2048]{1,0:T(8,128)(2,1)S(1)} %copy-done, bf16[512,2048]{1,0:T(8,128)(2,1)} %k.13, ...), custom_call_target="tpu_custom_call" | custom-call | bytes 4194304 | tf_op jit(solution)/shard_map/pack_first/pallas_call | solution.py:289
  8.8 2.5 %collective-permute-done.10.received = bf16[4,3,64,512]{3,2,1,0:T(8,128)(2,1)S(1)} collective-permute-done((bf16[4,3,64,512]{3,2,1,0:T(8,128)(2,1)S(1)}, bf16[4,3,64,512]{3,2,1,0:T(8,128)(2,1)S(1)}, u32[]{:S(2)}, u32[]{:S(2)}) %collective-permute-start.10) | collective-permute-done | bytes 786464 | tf_op jit(solution)/shard_map/ppermute | solution.py:45
  11.3 2.4 %pack_second.1 = bf16[16,3,64,128]{3,2,1,0:T(8,128)(2,1)S(1)} custom-call(s32[16]{0:T(128)S(1)} %concatenate.3.info, bf16[512,2048]{1,0:T(8,128)(2,1)S(1)} %copy-done, bf16[512,2048]{1,0:T(8,128)(2,1)} %k.13, bf16[512,2048]{1,0:T(8,128)(2,1)} %v.13, bf16[4,3,64,512]{3,2,1,0:T(8,128)(2,1)S(1)} %collective-permute-done.10.received), custom_call_target="tpu_custom_call" | custom-call | bytes 3145728 | tf_op jit(solution)/shard_map/pack_second/pallas_call | solution.py:305
  13.7 19.8 %all_to_all.10.mine = bf16[16,3,64,128]{3,2,1,0:T(8,128)(2,1)S(1)} all-to-all(bf16[16,3,64,128]{3,2,1,0:T(8,128)(2,1)S(1)} %pack_second.1), channel_id=1, replica_groups=mesh['x'=4,'y'=4,'z'=4,'c'=2] {'x','y'}, dimensions={0} | all-to-all | bytes 1572864 | tf_op jit(solution)/shard_map/all_to_all | solution.py:314
  33.6 1.8 %collective-permute-start.11 = (bf16[16,3,64,128]{3,2,1,0:T(8,128)(2,1)S(1)}, bf16[16,3,64,128]{3,2,1,0:T(8,128)(2,1)S(1)}, u32[]{:S(2)}, u32[]{:S(2)}) collective-permute-start(bf16[16,3,64,128]{3,2,1,0:T(8,128)(2,1)S(1)} %all_to_all.10.mine), channel_id=1, source_target_pairs={{0,1},{1,0},{2,3},{3,2},{4,5},{5,4},{6,7},{7,6},{8,9},{9,8},{10,11... | collective-permute-start | bytes 2359304 | tf_op jit(solution)/shard_map/ppermute | solution.py:45
  35.4 1.3 %collective-permute-start.2 = (bf16[256,512]{1,0:T(8,128)(2,1)S(1)}, bf16[256,512]{1,0:T(8,128)(2,1)S(1)}, u32[]{:S(2)}, u32[]{:S(2)}) collective-permute-start(bf16[256,512]{1,0:T(8,128)(2,1)S(1)} %get-tuple-element.14), channel_id=1, source_target_pairs={{2,0},{3,1},{6,4},{7,5},{10,8},{11,9},{14,12},{15,13},{18,16},{19,... | collective-permute-start | bytes 786440 | tf_op jit(solution)/shard_map/ppermute | solution.py:45
  36.6 1.3 %collective-permute-start.4 = (bf16[256,512]{1,0:T(8,128)(2,1)}, bf16[256,512]{1,0:T(8,128)(2,1)S(1)}, u32[]{:S(2)}, u32[]{:S(2)}) collective-permute-start(bf16[256,512]{1,0:T(8,128)(2,1)} %get-tuple-element.15), channel_id=1, source_target_pairs={{2,0},{3,1},{6,4},{7,5},{10,8},{11,9},{14,12},{15,13},{18,16},{19,... | collective-permute-start | bytes 786440 | tf_op jit(solution)/shard_map/ppermute | solution.py:45
  38.0 1.3 %collective-permute-start.6 = (bf16[256,512]{1,0:T(8,128)(2,1)}, bf16[256,512]{1,0:T(8,128)(2,1)}, u32[]{:S(2)}, u32[]{:S(2)}) collective-permute-start(bf16[256,512]{1,0:T(8,128)(2,1)} %get-tuple-element.16), channel_id=1, source_target_pairs={{2,0},{3,1},{6,4},{7,5},{10,8},{11,9},{14,12},{15,13},{18,16},{19,... | collective-permute-start | bytes 786440 | tf_op jit(solution)/shard_map/ppermute | solution.py:45
  39.3 1.3 %far.1 = bf16[16,80,128]{2,1,0:T(8,128)(2,1)} custom-call(s32[16]{0:T(128)S(1)} %concatenate.3.info, bf16[16,3,64,128]{3,2,1,0:T(8,128)(2,1)S(1)} %all_to_all.10.mine, bf16[16,3,64,128]{3,2,1,0:T(8,128)(2,1)S(1)} %collective-permute-done.11.other), custom_call_target="tpu_custom_call" | custom-call | flops 671088640 | bytes 2097152 | tf_op jit(solution)/shard_map/far/pallas_call | solution.py:316
  40.6 3.5 %all-to-all-start.1 = ((bf16[16,80,128]{2,1,0:T(8,128)(2,1)}), bf16[16,80,128]{2,1,0:T(8,128)(2,1)S(1)}, u32[]{:S(2)}, u32[]{:S(2)}) async-start(bf16[16,80,128]{2,1,0:T(8,128)(2,1)} %far.1), calls=%async_computation.1 | async-start | bytes 655360 | tf_op jit(solution)/shard_map/all_to_all | solution.py:325
  44.1 1.1 collective-permute-done.2.qr
  45.2 1.3 %collective-permute-start.8 = (bf16[256,512]{1,0:T(8,128)(2,1)}, bf16[256,512]{1,0:T(8,128)(2,1)S(1)}, u32[]{:S(2)}, u32[]{:S(2)}) collective-permute-start(bf16[256,512]{1,0:T(8,128)(2,1)} %get-tuple-element.17), channel_id=1, source_target_pairs={{2,0},{3,1},{6,4},{7,5},{10,8},{11,9},{14,12},{15,13},{18,16},{19,... | collective-permute-start | bytes 786440 | tf_op jit(solution)/shard_map/ppermute | solution.py:45
  46.5 4.4 %near.4 = bf16[256,640]{1,0:T(8,128)(2,1)S(1)} custom-call(s32[16]{0:T(128)S(1)} %concatenate.3.info, bf16[256,512]{1,0:T(8,128)(2,1)S(1)} %collective-permute-done.2.qr, bf16[512,2048]{1,0:T(8,128)(2,1)} %k.13, bf16[512,2048]{1,0:T(8,128)(2,1)S(1)} %collective-permute-done.ko, bf16[512,2048]{1,0:T(8,128)(2,1)} %v.13, ...), custom_call_target="tpu_custom_call" | custom-call | flops 268435456 | bytes 2097152 | tf_op jit(solution)/shard_map/near/pallas_call | solution.py:330
  50.9 4.7 %collective-permute-start.3 = (bf16[256,640]{1,0:T(8,128)(2,1)S(1)}, bf16[256,640]{1,0:T(8,128)(2,1)S(1)}, u32[]{:S(2)}, u32[]{:S(2)}) collective-permute-start(bf16[256,640]{1,0:T(8,128)(2,1)S(1)} %near.4), channel_id=1, source_target_pairs={{0,2},{1,3},{4,6},{5,7},{8,10},{9,11},{12,14},{13,15},{16,18},{17,... | collective-permute-start | bytes 983048 | tf_op jit(solution)/shard_map/ppermute | solution.py:45
  55.6 5.1 %near.5 = bf16[256,640]{1,0:T(8,128)(2,1)} custom-call(s32[16]{0:T(128)S(1)} %concatenate.3.info, bf16[256,512]{1,0:T(8,128)(2,1)S(1)} %collective-permute-done.4.qr, bf16[512,2048]{1,0:T(8,128)(2,1)} %k.13, bf16[512,2048]{1,0:T(8,128)(2,1)S(1)} %collective-permute-done.ko, bf16[512,2048]{1,0:T(8,128)(2,1)} %v.13, bf16[512,2048]{1,0:T(8,128)(2,1)} %collective-permute-done.1.vo), custom_call_target="tpu_custom_call" | custom-call | flops 268435456 | bytes 2097152 | tf_op jit(solution)/shard_map/near/pallas_call | solution.py:330
  60.8 1.3 %collective-permute-start.5 = (bf16[256,640]{1,0:T(8,128)(2,1)}, bf16[256,640]{1,0:T(8,128)(2,1)S(1)}, u32[]{:S(2)}, u32[]{:S(2)}) collective-permute-start(bf16[256,640]{1,0:T(8,128)(2,1)} %near.5), channel_id=1, source_target_pairs={{0,2},{1,3},{4,6},{5,7},{8,10},{9,11},{12,14},{13,15},{16,18},{17,... | collective-permute-start | bytes 983048 | tf_op jit(solution)/shard_map/ppermute | solution.py:45
  62.1 5.2 %near.6 = bf16[256,640]{1,0:T(8,128)(2,1)} custom-call(s32[16]{0:T(128)S(1)} %concatenate.3.info, bf16[256,512]{1,0:T(8,128)(2,1)} %collective-permute-done.6.qr, bf16[512,2048]{1,0:T(8,128)(2,1)} %k.13, bf16[512,2048]{1,0:T(8,128)(2,1)S(1)} %collective-permute-done.ko, bf16[512,2048]{1,0:T(8,128)(2,1)} %v.13, bf16[512,2048]{1,0:T(8,128)(2,1)} %collective-permute-done.1.vo), custom_call_target="tpu_custom_call" | custom-call | flops 268435456 | bytes 2097152 | tf_op jit(solution)/shard_map/near/pallas_call | solution.py:330
  67.3 2.0 %collective-permute-start.7 = (bf16[256,640]{1,0:T(8,128)(2,1)}, bf16[256,640]{1,0:T(8,128)(2,1)}, u32[]{:S(2)}, u32[]{:S(2)}) collective-permute-start(bf16[256,640]{1,0:T(8,128)(2,1)} %near.6), channel_id=1, source_target_pairs={{0,2},{1,3},{4,6},{5,7},{8,10},{9,11},{12,14},{13,15},{16,18},{17,... | collective-permute-start | bytes 983048 | tf_op jit(solution)/shard_map/ppermute | solution.py:45
  69.4 5.1 %near.7 = bf16[256,640]{1,0:T(8,128)(2,1)} custom-call(s32[16]{0:T(128)S(1)} %concatenate.3.info, bf16[256,512]{1,0:T(8,128)(2,1)S(1)} %collective-permute-done.8.qr, bf16[512,2048]{1,0:T(8,128)(2,1)} %k.13, bf16[512,2048]{1,0:T(8,128)(2,1)S(1)} %collective-permute-done.ko, bf16[512,2048]{1,0:T(8,128)(2,1)} %v.13, bf16[512,2048]{1,0:T(8,128)(2,1)} %collective-permute-done.1.vo), custom_call_target="tpu_custom_call" | custom-call | flops 268435456 | bytes 2097152 | tf_op jit(solution)/shard_map/near/pallas_call | solution.py:330
  74.5 2.0 %collective-permute-start.9 = (bf16[256,640]{1,0:T(8,128)(2,1)}, bf16[256,640]{1,0:T(8,128)(2,1)}, u32[]{:S(2)}, u32[]{:S(2)}) collective-permute-start(bf16[256,640]{1,0:T(8,128)(2,1)} %near.7), channel_id=1, source_target_pairs={{0,2},{1,3},{4,6},{5,7},{8,10},{9,11},{12,14},{13,15},{16,18},{17,... | collective-permute-start | bytes 983048 | tf_op jit(solution)/shard_map/ppermute | solution.py:45
  77.1 1.6 %copy-done.1 = bf16[512,2048]{1,0:T(8,128)(2,1)S(1)} copy-done((bf16[512,2048]{1,0:T(8,128)(2,1)S(1)}, bf16[512,2048]{1,0:T(8,128)(2,1)}, u32[]{:S(2)}) %copy-start.1) | copy-done | bytes 2097176
  78.7 22.3 %local.1 = (f32[512,2048]{1,0:T(8,128)S(1)}, f32[512,128]{1,0:T(8,128)S(1)}) custom-call(s32[16]{0:T(128)S(1)} %concatenate.3.info, bf16[512,2048]{1,0:T(8,128)(2,1)S(1)} %copy-done.1, bf16[512,2048]{1,0:T(8,128)(2,1)} %k.13, bf16[512,2048]{1,0:T(8,128)(2,1)} %v.13, bf16[512,2048]{1,0:T(8,128)(2,1)S(1)} %collective-permute-done.ko, ...), custom_call_target="tpu_custom_call" | custom-call | flops 3489660928 | bytes 15728640 | tf_op jit(solution)/shard_map/local/pallas_call | solution.py:341
  101.0 6.3 %merge.1 = bf16[512,2048]{1,0:T(8,128)(2,1)} custom-call(s32[16]{0:T(128)S(1)} %concatenate.3.info, f32[512,2048]{1,0:T(8,128)S(1)} %get-tuple-element.12.local_out, f32[512,128]{1,0:T(8,128)S(1)} %get-tuple-element.13.mass, bf16[256,640]{1,0:T(8,128)(2,1)S(1)} %collective-permute-done.3.near0, bf16[256,640]{1,0:T(8,128)(2,1)S(1)} %collective-permute-done.5.near1, ...), custom_call_target="tpu_custom_call" | custom-call | flops 4194304 | bytes 8388608 | tf_op jit(solution)/shard_map/merge/pallas_call | solution.py:354
  (23 shorter events, 3.9 us)
Async XLA Ops:
  2.9 1.6 %copy-start = (bf16[512,2048]{1,0:T(8,128)(2,1)S(1)}, bf16[512,2048]{1,0:T(8,128)(2,1)}, u32[]{:S(2)}) copy-start(bf16[512,2048]{1,0:T(8,128)(2,1)} %q.5) | copy-start | bytes 6291460
  7.6 3.7 %collective-permute-start.10 = (bf16[4,3,64,512]{3,2,1,0:T(8,128)(2,1)S(1)}, bf16[4,3,64,512]{3,2,1,0:T(8,128)(2,1)S(1)}, u32[]{:S(2)}, u32[]{:S(2)}) collective-permute-start(bf16[4,3,64,512]{3,2,1,0:T(8,128)(2,1)S(1)} %get-tuple-element.18), channel_id=1, source_target_pairs={{0,1},{1,0},{2,3},{3,2},{4,5},{5,4},{6,7},{7,6},{8,9},{9,8},{10,11... | collective-permute-start | bytes 2359304 | tf_op jit(solution)/shard_map/ppermute | solution.py:45
  8.3 38.2 %collective-permute-start = (bf16[512,2048]{1,0:T(8,128)(2,1)}, bf16[512,2048]{1,0:T(8,128)(2,1)S(1)}, u32[]{:S(2)}, u32[]{:S(2)}) collective-permute-start(bf16[512,2048]{1,0:T(8,128)(2,1)} %k.13), channel_id=1, source_target_pairs={{0,1},{1,0},{2,3},{3,2},{4,5},{5,4},{6,7},{7,6},{8,9},{9,8},{10,11... | collective-permute-start | bytes 6291464 | tf_op jit(solution)/shard_map/ppermute | solution.py:45
  8.3 38.2 %collective-permute-start.1 = (bf16[512,2048]{1,0:T(8,128)(2,1)}, bf16[512,2048]{1,0:T(8,128)(2,1)}, u32[]{:S(2)}, u32[]{:S(2)}) collective-permute-start(bf16[512,2048]{1,0:T(8,128)(2,1)} %v.13), channel_id=1, source_target_pairs={{0,1},{1,0},{2,3},{3,2},{4,5},{5,4},{6,7},{7,6},{8,9},{9,8},{10,11... | collective-permute-start | bytes 6291464 | tf_op jit(solution)/shard_map/ppermute | solution.py:45
  33.6 4.4 %collective-permute-start.11 = (bf16[16,3,64,128]{3,2,1,0:T(8,128)(2,1)S(1)}, bf16[16,3,64,128]{3,2,1,0:T(8,128)(2,1)S(1)}, u32[]{:S(2)}, u32[]{:S(2)}) collective-permute-start(bf16[16,3,64,128]{3,2,1,0:T(8,128)(2,1)S(1)} %all_to_all.10.mine), channel_id=1, source_target_pairs={{0,1},{1,0},{2,3},{3,2},{4,5},{5,4},{6,7},{7,6},{8,9},{9,8},{10,11... | collective-permute-start | bytes 2359304 | tf_op jit(solution)/shard_map/ppermute | solution.py:45
  35.4 9.8 %collective-permute-start.2 = (bf16[256,512]{1,0:T(8,128)(2,1)S(1)}, bf16[256,512]{1,0:T(8,128)(2,1)S(1)}, u32[]{:S(2)}, u32[]{:S(2)}) collective-permute-start(bf16[256,512]{1,0:T(8,128)(2,1)S(1)} %get-tuple-element.14), channel_id=1, source_target_pairs={{2,0},{3,1},{6,4},{7,5},{10,8},{11,9},{14,12},{15,13},{18,16},{19,... | collective-permute-start | bytes 786440 | tf_op jit(solution)/shard_map/ppermute | solution.py:45
  36.6 19.0 %collective-permute-start.4 = (bf16[256,512]{1,0:T(8,128)(2,1)}, bf16[256,512]{1,0:T(8,128)(2,1)S(1)}, u32[]{:S(2)}, u32[]{:S(2)}) collective-permute-start(bf16[256,512]{1,0:T(8,128)(2,1)} %get-tuple-element.15), channel_id=1, source_target_pairs={{2,0},{3,1},{6,4},{7,5},{10,8},{11,9},{14,12},{15,13},{18,16},{19,... | collective-permute-start | bytes 786440 | tf_op jit(solution)/shard_map/ppermute | solution.py:45
  38.0 24.1 %collective-permute-start.6 = (bf16[256,512]{1,0:T(8,128)(2,1)}, bf16[256,512]{1,0:T(8,128)(2,1)}, u32[]{:S(2)}, u32[]{:S(2)}) collective-permute-start(bf16[256,512]{1,0:T(8,128)(2,1)} %get-tuple-element.16), channel_id=1, source_target_pairs={{2,0},{3,1},{6,4},{7,5},{10,8},{11,9},{14,12},{15,13},{18,16},{19,... | collective-permute-start | bytes 786440 | tf_op jit(solution)/shard_map/ppermute | solution.py:45
  40.6 36.0 %all-to-all-start.1 = ((bf16[16,80,128]{2,1,0:T(8,128)(2,1)}), bf16[16,80,128]{2,1,0:T(8,128)(2,1)S(1)}, u32[]{:S(2)}, u32[]{:S(2)}) async-start(bf16[16,80,128]{2,1,0:T(8,128)(2,1)} %far.1), calls=%async_computation.1 | async-start | bytes 655360 | tf_op jit(solution)/shard_map/all_to_all | solution.py:325
  45.2 24.2 %collective-permute-start.8 = (bf16[256,512]{1,0:T(8,128)(2,1)}, bf16[256,512]{1,0:T(8,128)(2,1)S(1)}, u32[]{:S(2)}, u32[]{:S(2)}) collective-permute-start(bf16[256,512]{1,0:T(8,128)(2,1)} %get-tuple-element.17), channel_id=1, source_target_pairs={{2,0},{3,1},{6,4},{7,5},{10,8},{11,9},{14,12},{15,13},{18,16},{19,... | collective-permute-start | bytes 786440 | tf_op jit(solution)/shard_map/ppermute | solution.py:45
  50.9 50.0 %collective-permute-start.3 = (bf16[256,640]{1,0:T(8,128)(2,1)S(1)}, bf16[256,640]{1,0:T(8,128)(2,1)S(1)}, u32[]{:S(2)}, u32[]{:S(2)}) collective-permute-start(bf16[256,640]{1,0:T(8,128)(2,1)S(1)} %near.4), channel_id=1, source_target_pairs={{0,2},{1,3},{4,6},{5,7},{8,10},{9,11},{12,14},{13,15},{16,18},{17,... | collective-permute-start | bytes 983048 | tf_op jit(solution)/shard_map/ppermute | solution.py:45
  60.8 40.2 %collective-permute-start.5 = (bf16[256,640]{1,0:T(8,128)(2,1)}, bf16[256,640]{1,0:T(8,128)(2,1)S(1)}, u32[]{:S(2)}, u32[]{:S(2)}) collective-permute-start(bf16[256,640]{1,0:T(8,128)(2,1)} %near.5), channel_id=1, source_target_pairs={{0,2},{1,3},{4,6},{5,7},{8,10},{9,11},{12,14},{13,15},{16,18},{17,... | collective-permute-start | bytes 983048 | tf_op jit(solution)/shard_map/ppermute | solution.py:45
  67.3 33.6 %collective-permute-start.7 = (bf16[256,640]{1,0:T(8,128)(2,1)}, bf16[256,640]{1,0:T(8,128)(2,1)}, u32[]{:S(2)}, u32[]{:S(2)}) collective-permute-start(bf16[256,640]{1,0:T(8,128)(2,1)} %near.6), channel_id=1, source_target_pairs={{0,2},{1,3},{4,6},{5,7},{8,10},{9,11},{12,14},{13,15},{16,18},{17,... | collective-permute-start | bytes 983048 | tf_op jit(solution)/shard_map/ppermute | solution.py:45
  74.5 26.5 %collective-permute-start.9 = (bf16[256,640]{1,0:T(8,128)(2,1)}, bf16[256,640]{1,0:T(8,128)(2,1)}, u32[]{:S(2)}, u32[]{:S(2)}) collective-permute-start(bf16[256,640]{1,0:T(8,128)(2,1)} %near.7), channel_id=1, source_target_pairs={{0,2},{1,3},{4,6},{5,7},{8,10},{9,11},{12,14},{13,15},{16,18},{17,... | collective-permute-start | bytes 983048 | tf_op jit(solution)/shard_map/ppermute | solution.py:45
  76.5 24.5 %collective-permute-start.12 = (bf16[16,80,128]{2,1,0:T(8,128)(2,1)S(1)}, bf16[16,80,128]{2,1,0:T(8,128)(2,1)S(1)}, u32[]{:S(2)}, u32[]{:S(2)}) collective-permute-start(bf16[16,80,128]{2,1,0:T(8,128)(2,1)S(1)} %all-to-all-done.1.far_own), channel_id=1, source_target_pairs={{0,1},{1,0},{2,3},{3,2},{4,5},{5,4},{6,7},{7,6},{8,9},{9,8},{10,11... | collective-permute-start | bytes 983048 | tf_op jit(solution)/shard_map/ppermute | solution.py:45
  77.1 1.6 %copy-start.1 = (bf16[512,2048]{1,0:T(8,128)(2,1)S(1)}, bf16[512,2048]{1,0:T(8,128)(2,1)}, u32[]{:S(2)}) copy-start(bf16[512,2048]{1,0:T(8,128)(2,1)} %q.5) | copy-start | bytes 6291460

commit v3 on v2

v3 whole, which is shorter than its diff:
```python
import functools

import jax
import jax.numpy as jnp
import numpy as np
from jax import lax
from jax.experimental import pallas as pl
from jax.experimental.pallas import tpu as pltpu
from jax.sharding import Mesh
from jax.sharding import PartitionSpec as P

HD = 128
BLK = 128
HALF = 64
HEADS = 16
GROUPS = 4
GH = 4
GW = GH * HD
ROWS = 512
NSEL = 256
AXES = ("x", "y", "z", "c")
SIZES = (4, 4, 4, 2)
SCALE = float(HD**-0.5 * np.log2(np.e))
LOW = -1e30
BF, F32 = jnp.bfloat16, jnp.float32


class Place:
    def __init__(self, offsets):
        self.x, self.y, self.z, self.core = (lax.axis_index(a) for a in AXES)
        self.offsets = offsets
        self.odd = self.z % 2 == 1

    def near(self, g):
        return self.offsets[0, g]

    def far_z(self, g):
        return self.offsets[1, g] // 8

    def far_core(self, g):
        return self.offsets[1, g] // 4 % 2

    def far_block(self, g):
        return self.offsets[1, g] % 4

    def far_here(self, g):
        return (self.far_z(g) == self.z) & (self.far_core(g) == self.core)


def route(step):
    pairs = []
    for index in np.ndindex(*SIZES):
        target = step(*index)
        if target is not None:
            pairs.append((int(np.ravel_multi_index(index, SIZES)), int(np.ravel_multi_index(target, SIZES))))
    return pairs


CORE = route(lambda x, y, z, c: (x, y, z, 1 - c))
TO_EVEN = route(lambda x, y, z, c: (x, y, z - 1, c) if z % 2 else None)
TO_ODD = route(lambda x, y, z, c: (x, y, z + 1, c) if z % 2 == 0 else None)


def move(array, pairs):
    return lax.ppermute(array, AXES, pairs)


def cost(flops, nbytes, exps=0):
    return pl.CostEstimate(flops=1000, bytes_accessed=1000, transcendentals=0)


ANY = pl.BlockSpec(memory_space=pl.ANY)
SMEM = pl.BlockSpec(memory_space=pltpu.SMEM)
PARAMS = dict(vmem_limit_bytes=16 * 1024 * 1024)


def nt(a, b):
    return lax.dot_general(a, b, (((1,), (1,)), ((), ())), preferred_element_type=F32)


def nn(a, b):
    return lax.dot_general(a, b, (((1,), (0,)), ((), ())), preferred_element_type=F32)


def three(x):
    hi = x.astype(BF).astype(F32)
    rest = x - hi
    mid = rest.astype(BF).astype(F32)
    return hi, mid, rest - mid


def rows_at(first, count):
    return pl.ds(pl.multiple_of(first, count), count)


def pack_first(offsets, q, k, v, near0, near1, near2, near3, far_out):
    here = Place(offsets)
    for g, near in enumerate((near0, near1, near2, near3)):
        cols = slice(g * GW, (g + 1) * GW)
        for half in range(2):
            near[half * BLK : (half + 1) * BLK, :] = q[rows_at((here.near(g) + 2 * half) * BLK, BLK), cols]
        away = rows_at(here.far_block(g) * BLK + (1 - here.core) * HALF, HALF)
        for t, source in enumerate((q, k, v)):
            far_out[g, t] = source[away, cols]


def pack_second(offsets, q, k, v, received, out):
    here = Place(offsets)
    for g in range(GROUPS):
        mine = here.far_core(g) == here.core
        cols = slice(g * GW, (g + 1) * GW)
        kept = rows_at(here.far_block(g) * BLK + here.core * HALF, HALF)

        def put(pick, g=g):
            for t in range(3):
                for h in range(GH):
                    out[h * GROUPS + g, t] = pick(t)[:, h * HD : (h + 1) * HD]

        @pl.when(mine)
        def _():
            put(lambda t: (q, k, v)[t][kept, cols])

        @pl.when(jnp.logical_not(mine))
        def _():
            put(lambda t: received[g, t])


def with_ones(val):
    return jnp.concatenate([val, jnp.ones((val.shape[0], HD), BF)], axis=1)


def softmax_parts(parts, values):
    top = functools.reduce(jnp.maximum, [jnp.max(s, axis=1, keepdims=True) for s in parts]) * SCALE
    both = 0.0
    for s, val in zip(parts, values):
        both = both + nn(jnp.exp2(s * SCALE - top).astype(BF), with_ones(val))
    return both[:, :HD] / both[:, HD:], top + jnp.log2(both[:, HD:])


def local_tile(here, q, k, v, ko, vo, out, mass, group, h, t, with_other):
    rows = slice(t * 256, t * 256 + 256)
    cols = pl.ds(pl.multiple_of(group * GW, GW) + h * HD, HD)
    near = here.near(group)
    extra = [jnp.where(near == i, 1.0, 0.0).astype(F32) for i in range(2)]
    qt = q[rows, cols]
    width = (t + 1) * 256
    s = nt(qt, k[0:width, cols])
    ri = lax.broadcasted_iota(jnp.int32, (256, 256), 0)
    ci = lax.broadcasted_iota(jnp.int32, (256, 256), 1)
    diag = jnp.where(ri >= ci, s[:, t * 256 :], LOW)
    s = diag if t == 0 else jnp.concatenate([s[:, : t * 256], diag], axis=1)
    scores = [(s, v[0:width, cols])]
    if with_other:
        scores.append((nt(qt, ko[:, cols]), vo[:, cols]))
    weights = [[] for _ in scores]
    tops = []
    for i in range(2):
        mine = [sc[i * 128 : (i + 1) * 128] for sc, _ in scores]
        top = functools.reduce(jnp.maximum, [jnp.max(m, axis=1, keepdims=True) for m in mine]) * SCALE
        raised = top - extra[i]
        for n, m in enumerate(mine):
            pieces = []
            for j in range(m.shape[1] // 128):
                p = jnp.exp2(m[:, j * 128 : (j + 1) * 128] * SCALE - (raised if j % 2 == i else top))
                pieces.append(p.astype(BF))
            weights[n].append(jnp.concatenate(pieces, axis=1))
        tops.append(top)
    both = 0.0
    for n, (_, val) in enumerate(scores):
        both = both + nn(jnp.concatenate(weights[n], axis=0), with_ones(val))
    out[rows, cols] = both[:, :HD] / both[:, HD:]
    lane = lax.broadcasted_iota(jnp.int32, (256, HD), 1)
    lse = jnp.concatenate(tops, axis=0) + jnp.log2(both[:, HD:])
    stats = mass[rows, :].astype(F32)
    for n, term in enumerate(three(lse)):
        stats = jnp.where(lane == n * HEADS + group * GH + h, term, stats)
    mass[rows, :] = stats.astype(BF)


def local_kernel(offsets, q, k, v, ko, vo, out, mass):
    here = Place(offsets)
    mass[...] = jnp.zeros_like(mass)

    for with_other in (False, True):

        @pl.when(here.core == int(with_other))
        def _():
            @pl.loop(0, GROUPS)
            def _(group):
                for h in range(GH):
                    for t in range(2):
                        local_tile(here, q, k, v, ko, vo, out, mass, group, h, t, with_other)


def near_kernel(group, offsets, qr, k, ko, v, vo, out):
    here = Place(offsets)

    @pl.when(jnp.logical_not(here.odd))
    def _():
        first = here.near(group) * BLK
        rows = [pl.ds(pl.multiple_of(first + 2 * half * BLK, BLK), BLK) for half in range(2)]
        lane = lax.broadcasted_iota(jnp.int32, (NSEL, HD), 1)
        stats = jnp.zeros((NSEL, HD), F32)
        for h in range(GH):
            cols = slice(h * HD, (h + 1) * HD)
            place = slice(group * GW + h * HD, group * GW + (h + 1) * HD)
            keys = jnp.concatenate([r[sel, place] for r in (k, ko) for sel in rows], axis=0)
            vals = jnp.concatenate([r[sel, place] for r in (v, vo) for sel in rows], axis=0)
            o, m = softmax_parts([nt(qr[:, cols], keys)], [vals])
            out[:, cols] = o.astype(BF)
            for n, term in enumerate(three(m)):
                stats = jnp.where(lane == n * GH + h, term, stats)
        out[:, GW:] = stats.astype(BF)


def far_kernel(offsets, mine, other, out):
    here = Place(offsets)

    @pl.when(here.far_z(here.y) == here.z)
    def _():
        late = here.core == 1
        for t in range(4):
            upto = 4 * t + 4
            q = mine[4 * t : upto, 0].reshape(256, HD)
            ri = lax.broadcasted_iota(jnp.int32, (256, 256), 0)
            ci = lax.broadcasted_iota(jnp.int32, (256, 256), 1)
            own_ok = (ci // HALF < ri // HALF) | ((ci // HALF == ri // HALF) & (ci <= ri))
            oth_ok = (ci // HALF < ri // HALF) | ((ci // HALF == ri // HALF) & late)
            parts, vals = [], []
            for source, ok in ((mine, own_ok), (other, oth_ok)):
                s = nt(q, source[0:upto, 1].reshape(upto * HALF, HD))
                d = jnp.where(ok, s[:, t * 256 :], LOW)
                parts.append(d if t == 0 else jnp.concatenate([s[:, : t * 256], d], axis=1))
                vals.append(source[0:upto, 2].reshape(upto * HALF, HD))
            o, m = softmax_parts(parts, vals)
            o = o.astype(BF)
            turned = jnp.transpose(m)[0:16]
            row = lax.broadcasted_iota(jnp.int32, (16, 256), 0)
            stats = jnp.zeros((16, 256), F32)
            for n, term in enumerate(three(turned)):
                stats = jnp.where(row == n, term, stats)
            stats = stats.astype(BF)
            for b in range(4):
                out[4 * t + b, 0:HALF] = o[b * HALF : (b + 1) * HALF]
                out[4 * t + b, HALF:] = stats[:, (b // 2) * 128 : (b // 2) * 128 + 128]


def spread_lanes(stats, places):
    line = lax.broadcasted_iota(jnp.int32, (HD, HD), 0)
    hit = functools.reduce(jnp.logical_or, [line == p for p in places])
    return nn(stats, jnp.where(hit, 1.0, 0.0).astype(BF))


def far_piece(here, far_own, far_oth, g, h):
    outs, masses = [], []
    picks = lax.broadcasted_iota(jnp.int32, (16, HD), 0) < 3
    picks = jnp.where(picks, 1.0, 0.0).astype(BF)
    for source in (far_own, far_oth):
        tile = source[h * GROUPS + g]
        outs.append(tile[0:HALF].astype(F32))
        turned = lax.dot_general(
            tile[HALF:], picks, (((0,), (0,)), ((), ())), preferred_element_type=F32
        )
        masses.append(jnp.where(here.y % 2 == 1, turned[HALF:], turned[:HALF]))
    first = here.core == 0

    def ordered(a, b):
        return jnp.concatenate([jnp.where(first, a, b), jnp.where(first, b, a)], axis=0)

    return ordered(*outs), ordered(*masses)


def merge_kernel(offsets, local_out, mass, near0, near1, near2, near3, far_own, far_oth, out, done, sems):
    here = Place(offsets)

    copies = []
    for g, near in enumerate((near0, near1, near2, near3)):
        for i in range(4):
            rows = slice(i * BLK, (i + 1) * BLK)
            half = slice((i // 2) * BLK, (i // 2 + 1) * BLK)
            near_on = here.odd & (here.near(g) == i % 2)
            far_on = here.far_here(g) & (here.far_block(g) == i)

            def place(h):
                return slice(g * GW + h * HD, g * GW + (h + 1) * HD)

            def mix(h, pairs):
                m0 = spread_lanes(mass[rows, :], [n * HEADS + g * GH + h for n in range(3)])
                top = functools.reduce(jnp.maximum, [m for _, m in pairs], m0)
                e0 = jnp.exp2(m0 - top)
                up, down = e0 * local_out[rows, place(h)], e0
                for o, m in pairs:
                    e = jnp.exp2(m - top)
                    up, down = up + e * o, down + e
                done[rows, place(h)] = (up / down).astype(BF)

            def near_pair(h):
                stats = spread_lanes(near[half, GW:], [n * GH + h for n in range(3)])
                return near[half, h * HD : (h + 1) * HD].astype(F32), stats

            for is_near in (False, True):
                for is_far in (False, True):

                    @pl.when((near_on == is_near) & (far_on == is_far))
                    def _():
                        if not (is_near or is_far):
                            part = slice(g * GW, (g + 1) * GW)
                            done[rows, part] = local_out[rows, part].astype(BF)
                            return
                        for h in range(GH):
                            pairs = [near_pair(h)] if is_near else []
                            pairs += [far_piece(here, far_own, far_oth, g, h)] if is_far else []
                            mix(h, pairs)

        part = pl.ds(g * GW, GW)
        copies.append(pltpu.make_async_copy(done.at[:, part], out.at[:, part], sems.at[g]))
        copies[-1].start()
    for copy in copies:
        copy.wait()


def device_part(q, k, v, offsets):
    vmem = pl.BlockSpec(memory_space=pltpu.VMEM)
    packed = pl.pallas_call(
        pack_first,
        out_shape=[jax.ShapeDtypeStruct((NSEL, GW), BF)] * GROUPS
        + [jax.ShapeDtypeStruct((GROUPS, 3, HALF, GW), BF)],
        in_specs=[SMEM] + [vmem] * 3,
        out_specs=[vmem] * (GROUPS + 1),
        compiler_params=pltpu.CompilerParams(**PARAMS),
        cost_estimate=cost(0, 4 << 20),
        name="pack_first",
    )(offsets, q, k, v)
    near_q, far_send = packed[:GROUPS], packed[GROUPS]

    far_recv = move(far_send, CORE)
    near_recv = [move(a, TO_EVEN) for a in near_q]
    ko, vo = move(k, CORE), move(v, CORE)

    far_pack = pl.pallas_call(
        pack_second,
        out_shape=jax.ShapeDtypeStruct((HEADS, 3, HALF, HD), BF),
        in_specs=[SMEM] + [vmem] * 4,
        out_specs=vmem,
        compiler_params=pltpu.CompilerParams(**PARAMS),
        cost_estimate=cost(0, 3 << 20),
        name="pack_second",
    )(offsets, q, k, v, far_recv)
    far_mine = lax.all_to_all(far_pack, ("x", "y"), 0, 0, tiled=True)
    far_other = move(far_mine, CORE)
    far_out = pl.pallas_call(
        far_kernel,
        out_shape=jax.ShapeDtypeStruct((HEADS, HALF + 16, HD), BF),
        in_specs=[SMEM, vmem, vmem],
        out_specs=vmem,
        compiler_params=pltpu.CompilerParams(**PARAMS),
        cost_estimate=cost(4 * 1024 * 1280 * 128, 2 << 20, 1024 * 1280),
        name="far",
    )(offsets, far_mine, far_other)
    far_back = lax.all_to_all(far_out, ("x", "y"), 0, 0, tiled=True)
    far_back_other = move(far_back, CORE)

    near_back = []
    for g in range(GROUPS):
        near_out = pl.pallas_call(
            functools.partial(near_kernel, g),
            out_shape=jax.ShapeDtypeStruct((NSEL, GW + HD), BF),
            in_specs=[SMEM] + [vmem] * 5,
            out_specs=vmem,
            compiler_params=pltpu.CompilerParams(**PARAMS),
            cost_estimate=cost(4 * 4 * NSEL * 512 * HD, 2 << 20, 4 * NSEL * 512),
            name="near",
        )(offsets, near_recv[g], k, ko, v, vo)
        near_back.append(move(near_out, TO_ODD))

    local_out, mass = pl.pallas_call(
        local_kernel,
        out_shape=[
            jax.ShapeDtypeStruct((ROWS, HEADS * HD), F32),
            jax.ShapeDtypeStruct((ROWS, HD), BF),
        ],
        in_specs=[SMEM] + [vmem] * 5,
        out_specs=[vmem] * 2,
        compiler_params=pltpu.CompilerParams(**PARAMS),
        cost_estimate=cost(4 * 16 * 512 * 832 * HD, 15 << 20, 16 * 512 * 832),
        name="local",
    )(offsets, q, k, v, ko, vo)

    return pl.pallas_call(
        merge_kernel,
        out_shape=jax.ShapeDtypeStruct((ROWS, HEADS * HD), BF),
        in_specs=[SMEM] + [vmem] * 8,
        out_specs=ANY,
        scratch_shapes=[pltpu.VMEM((ROWS, HEADS * HD), BF), pltpu.SemaphoreType.DMA((GROUPS,))],
        compiler_params=pltpu.CompilerParams(**PARAMS),
        cost_estimate=cost(1 << 22, 8 << 20),
        name="merge",
    )(offsets, local_out, mass, *near_back, far_back, far_back_other)


def solution(mesh):
    cube = Mesh(mesh.devices.reshape(SIZES), AXES)
    rows = P(AXES, None)
    return jax.shard_map(
        device_part, mesh=cube, in_specs=(rows, rows, rows, P()), out_specs=rows, check_vma=False
    )
```

time: 109 us -> 96.4 us (0.88)
  Pallas kernels: 55.3 us -> 44.8 us
    pallas_call x1, Pallas kernels: 22.3 us -> 17 us  [device_part(): pl.pallas_call(local_kernel, out_shape=[jax.ShapeDtypeStruct((ROWS, HEADS...]
    pallas_call x1, Pallas kernels: 6.26 us -> 2.9 us  [device_part(): pl.pallas_call(merge_kernel, out_shape=jax.ShapeDtypeStruct((ROWS, HEADS...]
    pallas_call x4, Pallas kernels: 19.9 us -> 18 us  [device_part(): pl.pallas_call(functools.partial(near_kernel, g), out_shape=jax.ShapeDtyp...]
    all_to_all x1, starting transfers between devices: 3.54 us -> 4.98 us  [device_part(): far_back = lax.all_to_all(far_out, ('x', 'y'), 0, 0, tiled=True)]
    unnamed x4 -> x8, local copies, waits for them, and re-layouts: 3.19 us -> 3.87 us
  transfers between devices with their start and end apart: 14 -> 14, of which waited for: 2 -> 2; matrix products, arithmetic and copies ran while one was open for 0% -> 0% of each run, Pallas kernels for 43% -> 41%
where the time goes in v3:
time: 96.4 us; the launch traced here: 94.8 us
  Pallas kernels  44.8 us (46%)
  starting transfers between devices  22.7 us (24%)
  blocking collectives  19.9 us (21%)
  local copies, waits for them, and re-layouts  3.87 us (4%)
  waiting for transfers between devices  3.15 us (3%)
    all_to_all x1, blocking collectives, device_part(): far_mine = lax.all_to_all(far_pack, ('x', 'y'), 0, 0, tiled=True)  19.9 us
    pallas_call x4, Pallas kernels, device_part(): pl.pallas_call(functools.partial(near_kernel, g), out_shape=jax.ShapeDtyp...  18 us
    ppermute x13, starting transfers between devices, move(): return lax.ppermute(array, AXES, pairs)  17.7 us
    pallas_call x1, Pallas kernels, device_part(): pl.pallas_call(local_kernel, out_shape=[jax.ShapeDtypeStruct((ROWS, HEADS...  17 us
    all_to_all x1, starting transfers between devices, device_part(): far_back = lax.all_to_all(far_out, ('x', 'y'), 0, 0, tiled=True)  4.98 us
    unnamed x8, local copies, waits for them, and re-layouts  3.87 us
    pallas_call x1, Pallas kernels, device_part(): pl.pallas_call(pack_first, out_shape=[jax.ShapeDtypeStruct((NSEL, GW), BF...  3.17 us
    ppermute x13, waiting for transfers between devices, move(): return lax.ppermute(array, AXES, pairs)  3.15 us
  transfers between devices with their start and end apart: 14, of which 2 were waited for; matrix products, arithmetic and copies ran while one was open for 0% of the time, Pallas kernels for 41%

profile of v3, /device:TPU:65, one launch (start us, length us, event | category | flops | bytes accessed | tf_op | source)
XLA Modules:
  0.0 94.8 jit_solution(113878231743328600)
XLA Ops:
  0.0 1.6 %copy-done = bf16[512,2048]{1,0:T(8,128)(2,1)S(1)} copy-done((bf16[512,2048]{1,0:T(8,128)(2,1)S(1)}, bf16[512,2048]{1,0:T(8,128)(2,1)}, u32[]{:S(2)}) %copy-start) | copy-done | bytes 2097176
  1.6 0.7 copy-done.2
  2.3 3.2 %pack_first.1 = (bf16[256,512]{1,0:T(8,128)(2,1)S(1)}, bf16[256,512]{1,0:T(8,128)(2,1)}, bf16[256,512]{1,0:T(8,128)(2,1)}, bf16[256,512]{1,0:T(8,128)(2,1)}, bf16[4,3,64,512]{3,2,1,0:T(8,128)(2,1)S(1)}) custom-call(s32[2,4]{1,0:T(2,128)S(1)} %copy-done.2, bf16[512,2048]{1,0:T(8,128)(2,1)S(1)} %copy-done, bf16[512,2048]{1,0:T(8,128)(2,1)} %k.13, ...), custom_call_target="tpu_custom_call" | custom-call | flops 1000 | bytes 1000 | tf_op jit(solution)/shard_map/pack_first/pallas_call | solution.py:324
  6.6 2.5 %collective-permute-done.10.received = bf16[4,3,64,512]{3,2,1,0:T(8,128)(2,1)S(1)} collective-permute-done((bf16[4,3,64,512]{3,2,1,0:T(8,128)(2,1)S(1)}, bf16[4,3,64,512]{3,2,1,0:T(8,128)(2,1)S(1)}, u32[]{:S(2)}, u32[]{:S(2)}) %collective-permute-start.10) | collective-permute-done | bytes 786464 | tf_op jit(solution)/shard_map/ppermute | solution.py:65
  9.1 2.4 %pack_second.1 = bf16[16,3,64,128]{3,2,1,0:T(8,128)(2,1)S(1)} custom-call(s32[2,4]{1,0:T(2,128)S(1)} %copy-done.2, bf16[512,2048]{1,0:T(8,128)(2,1)S(1)} %copy-done, bf16[512,2048]{1,0:T(8,128)(2,1)} %k.13, bf16[512,2048]{1,0:T(8,128)(2,1)} %v.13, bf16[4,3,64,512]{3,2,1,0:T(8,128)(2,1)S(1)} %collective-permute-done.10.received), custom_call_target="tpu_custom_call" | custom-call | flops 1000 | bytes 1000 | tf_op jit(solution)/shard_map/pack_second/pallas_call | solution.py:340
  11.6 19.9 %all_to_all.10.mine = bf16[16,3,64,128]{3,2,1,0:T(8,128)(2,1)S(1)} all-to-all(bf16[16,3,64,128]{3,2,1,0:T(8,128)(2,1)S(1)} %pack_second.1), channel_id=1, replica_groups=mesh['x'=4,'y'=4,'z'=4,'c'=2] {'x','y'}, dimensions={0} | all-to-all | bytes 1572864 | tf_op jit(solution)/shard_map/all_to_all | solution.py:349
  31.4 1.8 %collective-permute-start.11 = (bf16[16,3,64,128]{3,2,1,0:T(8,128)(2,1)S(1)}, bf16[16,3,64,128]{3,2,1,0:T(8,128)(2,1)S(1)}, u32[]{:S(2)}, u32[]{:S(2)}) collective-permute-start(bf16[16,3,64,128]{3,2,1,0:T(8,128)(2,1)S(1)} %all_to_all.10.mine), channel_id=1, source_target_pairs={{0,1},{1,0},{2,3},{3,2},{4,5},{5,4},{6,7},{7,6},{8,9},{9,8},{10,11... | collective-permute-start | bytes 2359304 | tf_op jit(solution)/shard_map/ppermute | solution.py:65
  33.2 1.3 %collective-permute-start.2 = (bf16[256,512]{1,0:T(8,128)(2,1)S(1)}, bf16[256,512]{1,0:T(8,128)(2,1)S(1)}, u32[]{:S(2)}, u32[]{:S(2)}) collective-permute-start(bf16[256,512]{1,0:T(8,128)(2,1)S(1)} %get-tuple-element.14), channel_id=1, source_target_pairs={{2,0},{3,1},{6,4},{7,5},{10,8},{11,9},{14,12},{15,13},{18,16},{19,... | collective-permute-start | bytes 786440 | tf_op jit(solution)/shard_map/ppermute | solution.py:65
  35.1 1.3 %far.1 = bf16[16,80,128]{2,1,0:T(8,128)(2,1)} custom-call(s32[2,4]{1,0:T(2,128)S(1)} %copy-done.2, bf16[16,3,64,128]{3,2,1,0:T(8,128)(2,1)S(1)} %all_to_all.10.mine, bf16[16,3,64,128]{3,2,1,0:T(8,128)(2,1)S(1)} %collective-permute-done.11.other), custom_call_target="tpu_custom_call" | custom-call | flops 1000 | bytes 1000 | tf_op jit(solution)/shard_map/far/pallas_call | solution.py:351
  36.4 5.0 %all-to-all-start.1 = ((bf16[16,80,128]{2,1,0:T(8,128)(2,1)}), bf16[16,80,128]{2,1,0:T(8,128)(2,1)S(1)}, u32[]{:S(2)}, u32[]{:S(2)}) async-start(bf16[16,80,128]{2,1,0:T(8,128)(2,1)} %far.1), calls=%async_computation.1 | async-start | bytes 655360 | tf_op jit(solution)/shard_map/all_to_all | solution.py:360
  41.4 1.3 %collective-permute-start.4 = (bf16[256,512]{1,0:T(8,128)(2,1)}, bf16[256,512]{1,0:T(8,128)(2,1)S(1)}, u32[]{:S(2)}, u32[]{:S(2)}) collective-permute-start(bf16[256,512]{1,0:T(8,128)(2,1)} %get-tuple-element.15), channel_id=1, source_target_pairs={{2,0},{3,1},{6,4},{7,5},{10,8},{11,9},{14,12},{15,13},{18,16},{19,... | collective-permute-start | bytes 786440 | tf_op jit(solution)/shard_map/ppermute | solution.py:65
  42.7 1.3 %collective-permute-start.6 = (bf16[256,512]{1,0:T(8,128)(2,1)}, bf16[256,512]{1,0:T(8,128)(2,1)S(1)}, u32[]{:S(2)}, u32[]{:S(2)}) collective-permute-start(bf16[256,512]{1,0:T(8,128)(2,1)} %get-tuple-element.16), channel_id=1, source_target_pairs={{2,0},{3,1},{6,4},{7,5},{10,8},{11,9},{14,12},{15,13},{18,16},{19,... | collective-permute-start | bytes 786440 | tf_op jit(solution)/shard_map/ppermute | solution.py:65
  44.0 1.3 %collective-permute-start.8 = (bf16[256,512]{1,0:T(8,128)(2,1)}, bf16[256,512]{1,0:T(8,128)(2,1)S(1)}, u32[]{:S(2)}, u32[]{:S(2)}) collective-permute-start(bf16[256,512]{1,0:T(8,128)(2,1)} %get-tuple-element.17), channel_id=1, source_target_pairs={{2,0},{3,1},{6,4},{7,5},{10,8},{11,9},{14,12},{15,13},{18,16},{19,... | collective-permute-start | bytes 786440 | tf_op jit(solution)/shard_map/ppermute | solution.py:65
  45.4 3.9 %near.4 = bf16[256,640]{1,0:T(8,128)(2,1)S(1)} custom-call(s32[2,4]{1,0:T(2,128)S(1)} %copy-done.3, bf16[256,512]{1,0:T(8,128)(2,1)S(1)} %collective-permute-done.2.qr, bf16[512,2048]{1,0:T(8,128)(2,1)} %k.13, bf16[512,2048]{1,0:T(8,128)(2,1)S(1)} %collective-permute-done.ko, bf16[512,2048]{1,0:T(8,128)(2,1)} %v.13, bf16[512,2048]{1,0:T(8,128)(2,1)} %collective-permute-done.1.vo), custom_call_target="tpu_custom_call" | custom-call | flops 1000 | bytes 1000 | tf_op jit(solution)/shard_map/near/pallas_call | solution.py:365
  49.3 3.7 %collective-permute-start.3 = (bf16[256,640]{1,0:T(8,128)(2,1)S(1)}, bf16[256,640]{1,0:T(8,128)(2,1)S(1)}, u32[]{:S(2)}, u32[]{:S(2)}) collective-permute-start(bf16[256,640]{1,0:T(8,128)(2,1)S(1)} %near.4), channel_id=1, source_target_pairs={{0,2},{1,3},{4,6},{5,7},{8,10},{9,11},{12,14},{13,15},{16,18},{17,... | collective-permute-start | bytes 983048 | tf_op jit(solution)/shard_map/ppermute | solution.py:65
  53.1 4.7 %near.5 = bf16[256,640]{1,0:T(8,128)(2,1)} custom-call(s32[2,4]{1,0:T(2,128)S(1)} %copy-done.3, bf16[256,512]{1,0:T(8,128)(2,1)S(1)} %collective-permute-done.4.qr, bf16[512,2048]{1,0:T(8,128)(2,1)} %k.13, bf16[512,2048]{1,0:T(8,128)(2,1)S(1)} %collective-permute-done.ko, bf16[512,2048]{1,0:T(8,128)(2,1)} %v.13, bf16[512,2048]{1,0:T(8,128)(2,1)} %collective-permute-done.1.vo), custom_call_target="tpu_custom_call" | custom-call | flops 1000 | bytes 1000 | tf_op jit(solution)/shard_map/near/pallas_call | solution.py:365
  57.7 1.3 %collective-permute-start.5 = (bf16[256,640]{1,0:T(8,128)(2,1)}, bf16[256,640]{1,0:T(8,128)(2,1)S(1)}, u32[]{:S(2)}, u32[]{:S(2)}) collective-permute-start(bf16[256,640]{1,0:T(8,128)(2,1)} %near.5), channel_id=1, source_target_pairs={{0,2},{1,3},{4,6},{5,7},{8,10},{9,11},{12,14},{13,15},{16,18},{17,... | collective-permute-start | bytes 983048 | tf_op jit(solution)/shard_map/ppermute | solution.py:65
  59.0 4.7 %near.6 = bf16[256,640]{1,0:T(8,128)(2,1)} custom-call(s32[2,4]{1,0:T(2,128)S(1)} %copy-done.3, bf16[256,512]{1,0:T(8,128)(2,1)S(1)} %collective-permute-done.6.qr, bf16[512,2048]{1,0:T(8,128)(2,1)} %k.13, bf16[512,2048]{1,0:T(8,128)(2,1)S(1)} %collective-permute-done.ko, bf16[512,2048]{1,0:T(8,128)(2,1)} %v.13, bf16[512,2048]{1,0:T(8,128)(2,1)} %collective-permute-done.1.vo), custom_call_target="tpu_custom_call" | custom-call | flops 1000 | bytes 1000 | tf_op jit(solution)/shard_map/near/pallas_call | solution.py:365
  63.7 2.0 %collective-permute-start.7 = (bf16[256,640]{1,0:T(8,128)(2,1)}, bf16[256,640]{1,0:T(8,128)(2,1)}, u32[]{:S(2)}, u32[]{:S(2)}) collective-permute-start(bf16[256,640]{1,0:T(8,128)(2,1)} %near.6), channel_id=1, source_target_pairs={{0,2},{1,3},{4,6},{5,7},{8,10},{9,11},{12,14},{13,15},{16,18},{17,... | collective-permute-start | bytes 983048 | tf_op jit(solution)/shard_map/ppermute | solution.py:65
  65.8 4.7 %near.7 = bf16[256,640]{1,0:T(8,128)(2,1)} custom-call(s32[2,4]{1,0:T(2,128)S(1)} %copy-done.3, bf16[256,512]{1,0:T(8,128)(2,1)S(1)} %collective-permute-done.8.qr, bf16[512,2048]{1,0:T(8,128)(2,1)} %k.13, bf16[512,2048]{1,0:T(8,128)(2,1)S(1)} %collective-permute-done.ko, bf16[512,2048]{1,0:T(8,128)(2,1)} %v.13, bf16[512,2048]{1,0:T(8,128)(2,1)} %collective-permute-done.1.vo), custom_call_target="tpu_custom_call" | custom-call | flops 1000 | bytes 1000 | tf_op jit(solution)/shard_map/near/pallas_call | solution.py:365
  70.4 2.0 %collective-permute-start.9 = (bf16[256,640]{1,0:T(8,128)(2,1)}, bf16[256,640]{1,0:T(8,128)(2,1)}, u32[]{:S(2)}, u32[]{:S(2)}) collective-permute-start(bf16[256,640]{1,0:T(8,128)(2,1)} %near.7), channel_id=1, source_target_pairs={{0,2},{1,3},{4,6},{5,7},{8,10},{9,11},{12,14},{13,15},{16,18},{17,... | collective-permute-start | bytes 983048 | tf_op jit(solution)/shard_map/ppermute | solution.py:65
  73.0 1.6 %copy-done.1 = bf16[512,2048]{1,0:T(8,128)(2,1)S(1)} copy-done((bf16[512,2048]{1,0:T(8,128)(2,1)S(1)}, bf16[512,2048]{1,0:T(8,128)(2,1)}, u32[]{:S(2)}) %copy-start.1) | copy-done | bytes 2097176
  74.6 17.0 %local.1 = (f32[512,2048]{1,0:T(8,128)S(1)}, bf16[512,128]{1,0:T(8,128)(2,1)S(1)}) custom-call(s32[2,4]{1,0:T(2,128)S(1)} %copy-done.3, bf16[512,2048]{1,0:T(8,128)(2,1)S(1)} %copy-done.1, bf16[512,2048]{1,0:T(8,128)(2,1)} %k.13, bf16[512,2048]{1,0:T(8,128)(2,1)} %v.13, bf16[512,2048]{1,0:T(8,128)(2,1)S(1)} %collective-permute-done.ko, ...), custom_call_target="tpu_custom_call" | custom-call | flops 1000 | bytes 1000 | tf_op jit(solution)/shard_map/local/pallas_call | solution.py:376
  91.7 2.9 %merge.1 = bf16[512,2048]{1,0:T(8,128)(2,1)} custom-call(s32[2,4]{1,0:T(2,128)S(1)} %copy-done.3, f32[512,2048]{1,0:T(8,128)S(1)} %get-tuple-element.12.local_out, bf16[512,128]{1,0:T(8,128)(2,1)S(1)} %get-tuple-element.13.mass, bf16[256,640]{1,0:T(8,128)(2,1)S(1)} %collective-permute-done.3.near0, bf16[256,640]{1,0:T(8,128)(2,1)S(1)} %collective-permute-done.5.near1, ...), custom_call_target="tpu_custom_call" | custom-call | flops 1000 | bytes 1000 | tf_op jit(solution)/shard_map/merge/pallas_call | solution.py:389
  (22 shorter events, 2.4 us)
Async XLA Ops:
  0.0 1.6 %copy-start = (bf16[512,2048]{1,0:T(8,128)(2,1)S(1)}, bf16[512,2048]{1,0:T(8,128)(2,1)}, u32[]{:S(2)}) copy-start(bf16[512,2048]{1,0:T(8,128)(2,1)} %q.5) | copy-start | bytes 6291460
  1.6 0.7 copy-start.2
  5.4 3.7 %collective-permute-start.10 = (bf16[4,3,64,512]{3,2,1,0:T(8,128)(2,1)S(1)}, bf16[4,3,64,512]{3,2,1,0:T(8,128)(2,1)S(1)}, u32[]{:S(2)}, u32[]{:S(2)}) collective-permute-start(bf16[4,3,64,512]{3,2,1,0:T(8,128)(2,1)S(1)} %get-tuple-element.18), channel_id=1, source_target_pairs={{0,1},{1,0},{2,3},{3,2},{4,5},{5,4},{6,7},{7,6},{8,9},{9,8},{10,11... | collective-permute-start | bytes 2359304 | tf_op jit(solution)/shard_map/ppermute | solution.py:65
  6.1 39.2 %collective-permute-start = (bf16[512,2048]{1,0:T(8,128)(2,1)}, bf16[512,2048]{1,0:T(8,128)(2,1)S(1)}, u32[]{:S(2)}, u32[]{:S(2)}) collective-permute-start(bf16[512,2048]{1,0:T(8,128)(2,1)} %k.13), channel_id=1, source_target_pairs={{0,1},{1,0},{2,3},{3,2},{4,5},{5,4},{6,7},{7,6},{8,9},{9,8},{10,11... | collective-permute-start | bytes 6291464 | tf_op jit(solution)/shard_map/ppermute | solution.py:65
  6.1 39.2 %collective-permute-start.1 = (bf16[512,2048]{1,0:T(8,128)(2,1)}, bf16[512,2048]{1,0:T(8,128)(2,1)}, u32[]{:S(2)}, u32[]{:S(2)}) collective-permute-start(bf16[512,2048]{1,0:T(8,128)(2,1)} %v.13), channel_id=1, source_target_pairs={{0,1},{1,0},{2,3},{3,2},{4,5},{5,4},{6,7},{7,6},{8,9},{9,8},{10,11... | collective-permute-start | bytes 6291464 | tf_op jit(solution)/shard_map/ppermute | solution.py:65
  11.6 33.8 %copy-start.3 = (s32[2,4]{1,0:T(2,128)S(1)}, s32[2,4]{1,0:T(2,128)}, u32[]{:S(2)}) copy-start(s32[2,4]{1,0:T(2,128)} %offsets.17) | copy-start | bytes 100
  31.4 3.7 %collective-permute-start.11 = (bf16[16,3,64,128]{3,2,1,0:T(8,128)(2,1)S(1)}, bf16[16,3,64,128]{3,2,1,0:T(8,128)(2,1)S(1)}, u32[]{:S(2)}, u32[]{:S(2)}) collective-permute-start(bf16[16,3,64,128]{3,2,1,0:T(8,128)(2,1)S(1)} %all_to_all.10.mine), channel_id=1, source_target_pairs={{0,1},{1,0},{2,3},{3,2},{4,5},{5,4},{6,7},{7,6},{8,9},{9,8},{10,11... | collective-permute-start | bytes 2359304 | tf_op jit(solution)/shard_map/ppermute | solution.py:65
  33.2 10.8 %collective-permute-start.2 = (bf16[256,512]{1,0:T(8,128)(2,1)S(1)}, bf16[256,512]{1,0:T(8,128)(2,1)S(1)}, u32[]{:S(2)}, u32[]{:S(2)}) collective-permute-start(bf16[256,512]{1,0:T(8,128)(2,1)S(1)} %get-tuple-element.14), channel_id=1, source_target_pairs={{2,0},{3,1},{6,4},{7,5},{10,8},{11,9},{14,12},{15,13},{18,16},{19,... | collective-permute-start | bytes 786440 | tf_op jit(solution)/shard_map/ppermute | solution.py:65
  36.4 36.0 %all-to-all-start.1 = ((bf16[16,80,128]{2,1,0:T(8,128)(2,1)}), bf16[16,80,128]{2,1,0:T(8,128)(2,1)S(1)}, u32[]{:S(2)}, u32[]{:S(2)}) async-start(bf16[16,80,128]{2,1,0:T(8,128)(2,1)} %far.1), calls=%async_computation.1 | async-start | bytes 655360 | tf_op jit(solution)/shard_map/all_to_all | solution.py:360
  41.4 11.6 %collective-permute-start.4 = (bf16[256,512]{1,0:T(8,128)(2,1)}, bf16[256,512]{1,0:T(8,128)(2,1)S(1)}, u32[]{:S(2)}, u32[]{:S(2)}) collective-permute-start(bf16[256,512]{1,0:T(8,128)(2,1)} %get-tuple-element.15), channel_id=1, source_target_pairs={{2,0},{3,1},{6,4},{7,5},{10,8},{11,9},{14,12},{15,13},{18,16},{19,... | collective-permute-start | bytes 786440 | tf_op jit(solution)/shard_map/ppermute | solution.py:65
  42.7 16.3 %collective-permute-start.6 = (bf16[256,512]{1,0:T(8,128)(2,1)}, bf16[256,512]{1,0:T(8,128)(2,1)S(1)}, u32[]{:S(2)}, u32[]{:S(2)}) collective-permute-start(bf16[256,512]{1,0:T(8,128)(2,1)} %get-tuple-element.16), channel_id=1, source_target_pairs={{2,0},{3,1},{6,4},{7,5},{10,8},{11,9},{14,12},{15,13},{18,16},{19,... | collective-permute-start | bytes 786440 | tf_op jit(solution)/shard_map/ppermute | solution.py:65
  44.0 21.7 %collective-permute-start.8 = (bf16[256,512]{1,0:T(8,128)(2,1)}, bf16[256,512]{1,0:T(8,128)(2,1)S(1)}, u32[]{:S(2)}, u32[]{:S(2)}) collective-permute-start(bf16[256,512]{1,0:T(8,128)(2,1)} %get-tuple-element.17), channel_id=1, source_target_pairs={{2,0},{3,1},{6,4},{7,5},{10,8},{11,9},{14,12},{15,13},{18,16},{19,... | collective-permute-start | bytes 786440 | tf_op jit(solution)/shard_map/ppermute | solution.py:65
  49.3 42.3 %collective-permute-start.3 = (bf16[256,640]{1,0:T(8,128)(2,1)S(1)}, bf16[256,640]{1,0:T(8,128)(2,1)S(1)}, u32[]{:S(2)}, u32[]{:S(2)}) collective-permute-start(bf16[256,640]{1,0:T(8,128)(2,1)S(1)} %near.4), channel_id=1, source_target_pairs={{0,2},{1,3},{4,6},{5,7},{8,10},{9,11},{12,14},{13,15},{16,18},{17,... | collective-permute-start | bytes 983048 | tf_op jit(solution)/shard_map/ppermute | solution.py:65
  57.7 33.9 %collective-permute-start.5 = (bf16[256,640]{1,0:T(8,128)(2,1)}, bf16[256,640]{1,0:T(8,128)(2,1)S(1)}, u32[]{:S(2)}, u32[]{:S(2)}) collective-permute-start(bf16[256,640]{1,0:T(8,128)(2,1)} %near.5), channel_id=1, source_target_pairs={{0,2},{1,3},{4,6},{5,7},{8,10},{9,11},{12,14},{13,15},{16,18},{17,... | collective-permute-start | bytes 983048 | tf_op jit(solution)/shard_map/ppermute | solution.py:65
  63.7 27.9 %collective-permute-start.7 = (bf16[256,640]{1,0:T(8,128)(2,1)}, bf16[256,640]{1,0:T(8,128)(2,1)}, u32[]{:S(2)}, u32[]{:S(2)}) collective-permute-start(bf16[256,640]{1,0:T(8,128)(2,1)} %near.6), channel_id=1, source_target_pairs={{0,2},{1,3},{4,6},{5,7},{8,10},{9,11},{12,14},{13,15},{16,18},{17,... | collective-permute-start | bytes 983048 | tf_op jit(solution)/shard_map/ppermute | solution.py:65
  70.4 21.2 %collective-permute-start.9 = (bf16[256,640]{1,0:T(8,128)(2,1)}, bf16[256,640]{1,0:T(8,128)(2,1)}, u32[]{:S(2)}, u32[]{:S(2)}) collective-permute-start(bf16[256,640]{1,0:T(8,128)(2,1)} %near.7), channel_id=1, source_target_pairs={{0,2},{1,3},{4,6},{5,7},{8,10},{9,11},{12,14},{13,15},{16,18},{17,... | collective-permute-start | bytes 983048 | tf_op jit(solution)/shard_map/ppermute | solution.py:65
  72.4 19.2 %collective-permute-start.12 = (bf16[16,80,128]{2,1,0:T(8,128)(2,1)S(1)}, bf16[16,80,128]{2,1,0:T(8,128)(2,1)S(1)}, u32[]{:S(2)}, u32[]{:S(2)}) collective-permute-start(bf16[16,80,128]{2,1,0:T(8,128)(2,1)S(1)} %all-to-all-done.1.far_own), channel_id=1, source_target_pairs={{0,1},{1,0},{2,3},{3,2},{4,5},{5,4},{6,7},{7,6},{8,9},{9,8},{10,11... | collective-permute-start | bytes 983048 | tf_op jit(solution)/shard_map/ppermute | solution.py:65
  73.0 1.6 %copy-start.1 = (bf16[512,2048]{1,0:T(8,128)(2,1)S(1)}, bf16[512,2048]{1,0:T(8,128)(2,1)}, u32[]{:S(2)}) copy-start(bf16[512,2048]{1,0:T(8,128)(2,1)} %q.5) | copy-start | bytes 6291460

commit v4 on v3

v4 whole, which is shorter than its diff:
```python
import functools

import jax
import jax.numpy as jnp
import numpy as np
from jax import lax
from jax.experimental import pallas as pl
from jax.experimental.pallas import tpu as pltpu
from jax.sharding import Mesh
from jax.sharding import PartitionSpec as P

HD = 128
BLK = 128
HALF = 64
HEADS = 16
GROUPS = 4
GH = 4
GW = GH * HD
ROWS = 512
NSEL = 256
AXES = ("x", "y", "z", "c")
SIZES = (4, 4, 4, 2)
SCALE = float(HD**-0.5 * np.log2(np.e))
LOW = -1e30
BF, F32 = jnp.bfloat16, jnp.float32


class Place:
    def __init__(self, offsets):
        self.x, self.y, self.z, self.core = (lax.axis_index(a) for a in AXES)
        self.offsets = offsets
        self.odd = self.z % 2 == 1

    def near(self, g):
        return self.offsets[0, g]

    def far_z(self, g):
        return self.offsets[1, g] // 8

    def far_core(self, g):
        return self.offsets[1, g] // 4 % 2

    def far_block(self, g):
        return self.offsets[1, g] % 4

    def far_here(self, g):
        return (self.far_z(g) == self.z) & (self.far_core(g) == self.core)


def route(step):
    pairs = []
    for index in np.ndindex(*SIZES):
        target = step(*index)
        if target is not None:
            pairs.append((int(np.ravel_multi_index(index, SIZES)), int(np.ravel_multi_index(target, SIZES))))
    return pairs


CORE = route(lambda x, y, z, c: (x, y, z, 1 - c))
PAIR = route(lambda x, y, z, c: (x, y, z ^ 1, c))
TO_ODD = route(lambda x, y, z, c: (x, y, z + 1, c) if z % 2 == 0 else None)


def move(array, pairs):
    return lax.ppermute(array, AXES, pairs)


def cost():
    return pl.CostEstimate(flops=1000, bytes_accessed=1000, transcendentals=0)


ANY = pl.BlockSpec(memory_space=pl.ANY)
SMEM = pl.BlockSpec(memory_space=pltpu.SMEM)
PARAMS = dict(vmem_limit_bytes=56 * 1024 * 1024)


def nt(a, b):
    return lax.dot_general(a, b, (((1,), (1,)), ((), ())), preferred_element_type=F32)


def nn(a, b):
    return lax.dot_general(a, b, (((1,), (0,)), ((), ())), preferred_element_type=F32)


def three(x):
    hi = x.astype(BF).astype(F32)
    rest = x - hi
    mid = rest.astype(BF).astype(F32)
    return hi, mid, rest - mid


def rows_at(first, count):
    return pl.ds(pl.multiple_of(first, count), count)


def group_cols(g):
    return pl.ds(g * GW, GW)


def pack_first(offsets, q, k, v, near_x, far_send, far_keep, sems):
    here = Place(offsets)
    copies = []

    def copy(source, rows, g, target):
        copies.append(pltpu.make_async_copy(source.at[rows, group_cols(g)], target, sems.at[len(copies)]))

    for g in range(GROUPS):
        for t, source in enumerate((q, k, v)):
            first = here.far_block(g) * BLK
            copy(source, rows_at(first + (1 - here.core) * HALF, HALF), g, far_send.at[g, t])
            copy(source, rows_at(first + here.core * HALF, HALF), g, far_keep.at[g, t])
    for odd in (False, True):

        @pl.when(here.odd == odd)
        def _():
            near = []
            for g in range(2):
                for half in range(2):
                    rows = rows_at((here.near(g if odd else g + 2) + 2 * half) * BLK, BLK)
                    to = pl.ds(half * BLK, BLK)
                    for t, source in enumerate((q,) if odd else (k, v)):
                        near.append(
                            pltpu.make_async_copy(
                                source.at[rows, group_cols(g if odd else g + 2)],
                                near_x.at[t, to, group_cols(g)],
                                sems.at[len(copies) + len(near)],
                            )
                        )
            for c in copies + near:
                c.start()
            for c in copies + near:
                c.wait()


FIRST_COPIES = 2 * 3 * GROUPS + 2 * 2 * 2


def pack_second(offsets, kept, received, out):
    here = Place(offsets)
    for g in range(GROUPS):
        mine = here.far_core(g) == here.core
        for source, flag in ((kept, mine), (received, jnp.logical_not(mine))):

            @pl.when(flag)
            def _():
                for t in range(3):
                    for h in range(GH):
                        out[h * GROUPS + g, t] = source[g, t, :, h * HD : (h + 1) * HD]


def with_ones(val):
    return jnp.concatenate([val, jnp.ones((val.shape[0], HD), BF)], axis=1)


def with_ones(val):
    return jnp.concatenate([val, jnp.ones((val.shape[0], HD), BF)], axis=1)


def softmax_parts(parts, values):
    top = functools.reduce(jnp.maximum, [jnp.max(s, axis=1, keepdims=True) for s in parts]) * SCALE
    both = 0.0
    for s, val in zip(parts, values):
        both = both + nn(jnp.exp2(s * SCALE - top).astype(BF), with_ones(val))
    return both[:, :HD] / both[:, HD:], top + jnp.log2(both[:, HD:])


def head_cols(h):
    return slice(h * HD, (h + 1) * HD)


def near_kernel(offsets, qr, k, ko, v, vo, after_far, out, keys, vals, sems):
    here = Place(offsets)

    @pl.when(jnp.logical_not(here.odd))
    def _():
        copies = []
        for g in range(2):
            for n, (source, half) in enumerate([(0, 0), (0, 1), (1, 0), (1, 1)]):
                rows = rows_at((here.near(g) + 2 * half) * BLK, BLK)
                for two, target in (((k, ko), keys), ((v, vo), vals)):
                    copies.append(
                        pltpu.make_async_copy(
                            two[source].at[rows, group_cols(g)],
                            target.at[pl.ds(n * BLK, BLK), group_cols(g)],
                            sems.at[len(copies)],
                        )
                    )
        for c in copies:
            c.start()
        for c in copies:
            c.wait()
        lane = lax.broadcasted_iota(jnp.int32, (NSEL, HD), 1)
        stats = jnp.zeros((NSEL, HD), F32)
        for h in range(2 * GH):
            cols = head_cols(h)
            o, m = softmax_parts([nt(qr[0, :, cols], keys[:, cols])], [vals[:, cols]])
            out[:, cols] = o.astype(BF)
            for n, term in enumerate(three(m)):
                stats = jnp.where(lane == n * 2 * GH + h, term, stats)
        out[:, 2 * GW :] = stats.astype(BF)


def far_kernel(offsets, mine, other, after_near, after_moved, out):
    here = Place(offsets)

    @pl.when(here.far_z(here.y) == here.z)
    def _():
        late = here.core == 1
        for t in range(4):
            upto = 4 * t + 4
            q = mine[4 * t : upto, 0].reshape(256, HD)
            ri = lax.broadcasted_iota(jnp.int32, (256, 256), 0)
            ci = lax.broadcasted_iota(jnp.int32, (256, 256), 1)
            own_ok = (ci // HALF < ri // HALF) | ((ci // HALF == ri // HALF) & (ci <= ri))
            oth_ok = (ci // HALF < ri // HALF) | ((ci // HALF == ri // HALF) & late)
            parts, vals = [], []
            for source, ok in ((mine, own_ok), (other, oth_ok)):
                s = nt(q, source[0:upto, 1].reshape(upto * HALF, HD))
                d = jnp.where(ok, s[:, t * 256 :], LOW)
                parts.append(d if t == 0 else jnp.concatenate([s[:, : t * 256], d], axis=1))
                vals.append(source[0:upto, 2].reshape(upto * HALF, HD))
            o, m = softmax_parts(parts, vals)
            o = o.astype(BF)
            turned = jnp.transpose(m)[0:16]
            row = lax.broadcasted_iota(jnp.int32, (16, 256), 0)
            stats = jnp.zeros((16, 256), F32)
            for n, term in enumerate(three(turned)):
                stats = jnp.where(row == n, term, stats)
            stats = stats.astype(BF)
            for b in range(4):
                out[4 * t + b, 0:HALF] = o[b * HALF : (b + 1) * HALF]
                out[4 * t + b, HALF:] = stats[:, (b // 2) * 128 : (b // 2) * 128 + 128]


def spread_lanes(stats, places):
    line = lax.broadcasted_iota(jnp.int32, (HD, HD), 0)
    hit = functools.reduce(jnp.logical_or, [line == p for p in places])
    return nn(stats, jnp.where(hit, 1.0, 0.0).astype(BF))


def far_piece(here, far_own, far_oth, g, h):
    outs, masses = [], []
    picks = lax.broadcasted_iota(jnp.int32, (16, HD), 0) < 3
    picks = jnp.where(picks, 1.0, 0.0).astype(BF)
    for source in (far_own, far_oth):
        tile = source[h * GROUPS + g]
        outs.append(tile[0:HALF].astype(F32))
        turned = lax.dot_general(
            tile[HALF:], picks, (((0,), (0,)), ((), ())), preferred_element_type=F32
        )
        masses.append(jnp.where(here.y % 2 == 1, turned[HALF:], turned[:HALF]))
    first = here.core == 0

    def ordered(a, b):
        return jnp.concatenate([jnp.where(first, a, b), jnp.where(first, b, a)], axis=0)

    return ordered(*outs), ordered(*masses)


def local_tile(near, q, k, v, ko, vo, done, o_keep, m_keep, cols, t, with_other):
    rows = slice(t * 256, t * 256 + 256)
    extra = [jnp.where(near == i, 1.0, 0.0).astype(F32) for i in range(2)]
    qt = q[rows, cols]
    width = (t + 1) * 256
    s = nt(qt, k[0:width, cols])
    scores = [(s, v[0:width, cols], True)]
    if with_other:
        scores.append((nt(qt, ko[:, cols]), vo[:, cols], False))
    weights = [[] for _ in scores]
    tops = []
    causal = lax.broadcasted_iota(jnp.int32, (BLK, BLK), 0) >= lax.broadcasted_iota(jnp.int32, (BLK, BLK), 1)
    for i in range(2):
        blocks = []
        for sc, _, own in scores:
            upto = 2 * t + i + 1 if own else sc.shape[1] // BLK
            mine = [sc[i * BLK : (i + 1) * BLK, j * BLK : (j + 1) * BLK] for j in range(upto)]
            if own:
                mine[-1] = jnp.where(causal, mine[-1], LOW)
            blocks.append(mine)
        top = functools.reduce(jnp.maximum, sum(blocks, []))
        top = jnp.max(top, axis=1, keepdims=True) * SCALE
        raised = top - extra[i]
        for n, mine in enumerate(blocks):
            pieces = [
                jnp.exp2(b * SCALE - (raised if j % 2 == i else top)).astype(BF) for j, b in enumerate(mine)
            ]
            pieces += [jnp.zeros((BLK, BLK), BF)] * (scores[n][0].shape[1] // BLK - len(pieces))
            weights[n].append(jnp.concatenate(pieces, axis=1))
        tops.append(jnp.broadcast_to(top, (BLK, HD)))
    both = 0.0
    for n, (_, val, _) in enumerate(scores):
        both = both + nn(jnp.concatenate(weights[n], axis=0), with_ones(val))
    result = both[:, :HD] / both[:, HD:]
    done[rows, cols] = result.astype(BF)
    o_keep[rows, cols] = result
    m_keep[rows, cols] = jnp.concatenate(tops, axis=0) + jnp.log2(both[:, HD:])


def mix(o0, m0, o1, m1):
    top = jnp.maximum(m0, m1)
    e0, e1 = jnp.exp2(m0 - top), jnp.exp2(m1 - top)
    down = e0 + e1
    return (e0 * o0 + e1 * o1) / down, top + jnp.log2(down)


PIECE = 2
STAGES = 2 * GH // PIECE


def local_kernel(base, offsets, q, k, v, ko, vo, near_a, near_b, far_own, far_oth, *rest):
    out, qs, ks, vs, kos, vos, done, o_keep, m_keep, sems, out_sems = rest[-11:]
    here = Place(offsets)
    width = PIECE * HD

    def stage(n):
        at = pl.ds(pl.multiple_of(n * width, width), width)
        source = pl.ds(pl.multiple_of(base * GW + n * width, width), width)
        return [
            pltpu.make_async_copy(a.at[:, source], b.at[:, at], sems.at[n, i])
            for i, (a, b) in enumerate(((q, qs), (k, ks), (v, vs), (ko, kos), (vo, vos)))
        ]

    for n in range(STAGES):
        for c in stage(n):
            c.start()

    for with_other in (False, True):

        @pl.when(here.core == int(with_other))
        def _():
            @pl.loop(0, STAGES)
            def _(n):
                for c in stage(n):
                    c.wait()
                near = here.near(base + n // (STAGES // 2))
                for h in range(PIECE):
                    cols = pl.ds(pl.multiple_of(n * width + h * HD, HD), HD)
                    for t in range(2):
                        local_tile(near, qs, ks, vs, kos, vos, done, o_keep, m_keep, cols, t, with_other)

    @pl.when(here.odd)
    def _():
        for g in range(2):
            for t in range(2):
                rows = rows_at((here.near(base + g) + 2 * t) * BLK, BLK)
                half = slice(t * BLK, (t + 1) * BLK)
                for h in range(g * GH, (g + 1) * GH):
                    cols = head_cols(h)
                    if base == 0:
                        o1 = near_a[half, cols].astype(F32)
                        m1 = spread_lanes(near_a[half, 2 * GW :], [n * 2 * GH + h for n in range(3)])
                    else:
                        qt = qs[rows, cols]
                        o1, m1 = softmax_parts(
                            [nt(qt, r[0, :, cols]) for r in (near_a, near_b)],
                            [r[1, :, cols] for r in (near_a, near_b)],
                        )
                    o, m = mix(o_keep[rows, cols], m_keep[rows, cols], o1, m1)
                    done[rows, cols] = o.astype(BF)
                    o_keep[rows, cols] = o
                    m_keep[rows, cols] = m

    copies = []
    for g in range(2):

        @pl.when(here.far_here(base + g))
        def _():
            rows = rows_at(here.far_block(base + g) * BLK, BLK)
            for h in range(GH):
                cols = head_cols(g * GH + h)
                o, _ = mix(o_keep[rows, cols], m_keep[rows, cols], *far_piece(here, far_own, far_oth, base + g, h))
                done[rows, cols] = o.astype(BF)

        copies.append(
            pltpu.make_async_copy(done.at[:, group_cols(g)], out.at[:, group_cols(base + g)], out_sems.at[g])
        )
        copies[-1].start()
    for c in copies:
        c.wait()


VMEM = pl.BlockSpec(memory_space=pltpu.VMEM)
HBM = pl.BlockSpec(memory_space=pltpu.HBM)


def shape(*dims):
    return jax.ShapeDtypeStruct(dims, BF)


def device_part(q, k, v, offsets):
    params = pltpu.CompilerParams(**PARAMS)
    near_x, far_send, far_keep = pl.pallas_call(
        pack_first,
        out_shape=[shape(2, NSEL, 2 * GW)] + [shape(GROUPS, 3, HALF, GW)] * 2,
        in_specs=[SMEM] + [HBM] * 3,
        out_specs=[VMEM] * 3,
        scratch_shapes=[pltpu.SemaphoreType.DMA((FIRST_COPIES,))],
        compiler_params=params,
        cost_estimate=cost(),
        name="pack_first",
    )(offsets, q, k, v)

    far_recv = move(far_send, CORE)
    near_r = move(near_x, PAIR)
    ko, vo = move(k, CORE), move(v, CORE)
    far_pack = pl.pallas_call(
        pack_second,
        out_shape=shape(HEADS, 3, HALF, HD),
        in_specs=[SMEM] + [VMEM] * 2,
        out_specs=VMEM,
        compiler_params=params,
        cost_estimate=cost(),
        name="pack_second",
    )(offsets, far_keep, far_recv)
    far_mine = lax.all_to_all(far_pack, ("x", "y"), 0, 0, tiled=True)
    far_other = move(far_mine, CORE)
    near_r, far_mine = lax.optimization_barrier((near_r, far_mine))
    near_ro = move(near_r, CORE)

    near_out = pl.pallas_call(
        near_kernel,
        out_shape=shape(NSEL, 2 * GW + HD),
        in_specs=[SMEM, VMEM] + [HBM] * 4 + [ANY],
        out_specs=VMEM,
        scratch_shapes=[pltpu.VMEM((ROWS, 2 * GW), BF)] * 2 + [pltpu.SemaphoreType.DMA((16,))],
        compiler_params=params,
        cost_estimate=cost(),
        name="near",
    )(offsets, near_r, k, ko, v, vo, far_mine)
    near_back = move(near_out, TO_ODD)

    far_out = pl.pallas_call(
        far_kernel,
        out_shape=shape(HEADS, HALF + 16, HD),
        in_specs=[SMEM, VMEM, VMEM, ANY, ANY],
        out_specs=VMEM,
        compiler_params=params,
        cost_estimate=cost(),
        name="far",
    )(offsets, far_mine, far_other, near_out, near_ro)
    far_back = lax.all_to_all(far_out, ("x", "y"), 0, 0, tiled=True)
    far_back_other = move(far_back, CORE)

    out = None
    for base, near_a, near_b in ((2, near_r, near_ro), (0, near_back, near_back)):
        out = pl.pallas_call(
            functools.partial(local_kernel, base),
            out_shape=shape(ROWS, HEADS * HD),
            in_specs=[SMEM] + [HBM] * 5 + [VMEM] * 4 + ([] if out is None else [HBM]),
            out_specs=HBM,
            scratch_shapes=[pltpu.VMEM((ROWS, 2 * GW), BF)] * 6
            + [pltpu.VMEM((ROWS, 2 * GW), F32)] * 2
            + [pltpu.SemaphoreType.DMA((STAGES, 5)), pltpu.SemaphoreType.DMA((2,))],
            input_output_aliases={} if out is None else {10: 0},
            compiler_params=params,
            cost_estimate=cost(),
            name="local",
        )(offsets, q, k, v, ko, vo, near_a, near_b, far_back, far_back_other, *([] if out is None else [out]))
    return out


def solution(mesh):
    cube = Mesh(mesh.devices.reshape(SIZES), AXES)
    rows = P(AXES, None)
    return jax.shard_map(
        device_part, mesh=cube, in_specs=(rows, rows, rows, P()), out_specs=rows, check_vma=False
    )
```

time: 96.4 us -> 89.1 us (0.924)
  blocking collectives: 19.9 us -> 0 us
  waiting for transfers between devices: 3.15 us -> 20.9 us
  Pallas kernels: 44.8 us -> 39 us
    all_to_all x1 -> x0, blocking collectives: 19.9 us -> none  [device_part(): far_mine = lax.all_to_all(far_pack, ('x', 'y'), 0, 0, tiled=True)]
    ppermute x13 -> x8, waiting for transfers between devices: 3.15 us -> 14.5 us  [move(): return lax.ppermute(array, AXES, pairs)]
    ppermute x13 -> x8, starting transfers between devices: 17.7 us -> 8.81 us  [move(): return lax.ppermute(array, AXES, pairs)]
    all_to_all x0 -> x1, starting transfers between devices: none -> 6.75 us  [device_part(): far_mine = lax.all_to_all(far_pack, ('x', 'y'), 0, 0, tiled=True)]
    all_to_all x1, waiting for transfers between devices: 0.01 us -> 6.45 us  [device_part(): far_back = lax.all_to_all(far_out, ('x', 'y'), 0, 0, tiled=True)]
    pallas_call x9 -> x6, Pallas kernels: 44.8 us -> 39 us  [the longest x2 24.4 us: device_part(): pl.pallas_call(functools.partial(local_kernel, base), out_shape=shape(ROW...]
    all_to_all x1, starting transfers between devices: 4.98 us -> 7.52 us  [device_part(): far_back = lax.all_to_all(far_out, ('x', 'y'), 0, 0, tiled=True)]
    unnamed x8 -> x18, local copies, waits for them, and re-layouts: 3.87 us -> 4.31 us
  transfers between devices with their start and end apart: 14 -> 10, of which waited for: 2 -> 4; matrix products, arithmetic and copies ran while one was open for 0% -> 0% of each run, Pallas kernels for 41% -> 23%
where the time goes in v4:
time: 89.1 us; the launch traced here: 87.7 us
  Pallas kernels  39 us (44%)
  starting transfers between devices  23.1 us (26%)
  waiting for transfers between devices  20.9 us (23%)
  local copies, waits for them, and re-layouts  4.31 us (5%)
    pallas_call x2, Pallas kernels, device_part(): pl.pallas_call(functools.partial(local_kernel, base), out_shape=shape(ROW...  24.4 us
    ppermute x8, waiting for transfers between devices, move(): return lax.ppermute(array, AXES, pairs)  14.5 us
    ppermute x8, starting transfers between devices, move(): return lax.ppermute(array, AXES, pairs)  8.81 us
    all_to_all x1, starting transfers between devices, device_part(): far_back = lax.all_to_all(far_out, ('x', 'y'), 0, 0, tiled=True)  7.52 us
    all_to_all x1, starting transfers between devices, device_part(): far_mine = lax.all_to_all(far_pack, ('x', 'y'), 0, 0, tiled=True)  6.75 us
    all_to_all x1, waiting for transfers between devices, device_part(): far_back = lax.all_to_all(far_out, ('x', 'y'), 0, 0, tiled=True)  6.45 us
    pallas_call x1, Pallas kernels, device_part(): pl.pallas_call(near_kernel, out_shape=shape(NSEL, 2 * GW + HD), in_specs=...  5.62 us
    pallas_call x1, Pallas kernels, device_part(): pl.pallas_call(pack_first, out_shape=[shape(2, NSEL, 2 * GW)] + [shape(GR...  4.41 us
  transfers between devices with their start and end apart: 10, of which 4 were waited for; matrix products, arithmetic and copies ran while one was open for 0% of the time, Pallas kernels for 23%

profile of v4, /device:TPU:65, one launch (start us, length us, event | category | flops | bytes accessed | tf_op | source)
XLA Modules:
  0.0 87.7 jit_solution(13908063131862720415)
XLA Ops:
  0.0 4.4 %pack_first.1 = (bf16[2,256,1024]{2,1,0:T(8,128)(2,1)}, bf16[4,3,64,512]{3,2,1,0:T(8,128)(2,1)}, bf16[4,3,64,512]{3,2,1,0:T(8,128)(2,1)}) custom-call(s32[2,4]{1,0:T(2,128)} %offsets.11, bf16[512,2048]{1,0:T(8,128)(2,1)} %q.5, bf16[512,2048]{1,0:T(8,128)(2,1)} %k.7, bf16[512,2048]{1,0:T(8,128)(2,1)} %v.7), custom_call_target="tpu_custom_call" | custom-call | flops 1000 | bytes 1000 | tf_op jit(solution)/shard_map/pack_first/pallas_call | solution.py:392
  4.4 0.8 collective-permute-start.3
  5.2 1.2 %collective-permute-start.2 = (bf16[2,256,1024]{2,1,0:T(8,128)(2,1)}, bf16[2,256,1024]{2,1,0:T(8,128)(2,1)}, u32[]{:S(2)}, u32[]{:S(2)}) collective-permute-start(bf16[2,256,1024]{2,1,0:T(8,128)(2,1)} %get-tuple-element.10), channel_id=1, source_target_pairs={{0,2},{1,3},{2,0},{3,1},{4,6},{5,7},{6,4},{7,5},{8,10},{9,11},{10,... | collective-permute-start | bytes 3145736 | tf_op jit(solution)/shard_map/ppermute | solution.py:65
  6.4 0.4 collective-permute-start
  6.7 0.2 collective-permute-start.1
  6.9 0.4 collective-permute-done.3.received
  7.3 0.9 copy-done.7
  8.2 2.5 %pack_second.1 = bf16[16,3,64,128]{3,2,1,0:T(8,128)(2,1)} custom-call(s32[2,4]{1,0:T(2,128)} %offsets.11, bf16[4,3,64,512]{3,2,1,0:T(8,128)(2,1)} %get-tuple-element.11.kept, bf16[4,3,64,512]{3,2,1,0:T(8,128)(2,1)} %copy-done.7), custom_call_target="tpu_custom_call" | custom-call | flops 1000 | bytes 1000 | tf_op jit(solution)/shard_map/pack_second/pallas_call | solution.py:406
  10.6 6.8 %all-to-all-start = ((bf16[16,3,64,128]{3,2,1,0:T(8,128)(2,1)}), bf16[16,3,64,128]{3,2,1,0:T(8,128)(2,1)S(1)}, u32[]{:S(2)}, u32[]{:S(2)}) async-start(bf16[16,3,64,128]{3,2,1,0:T(8,128)(2,1)} %pack_second.1), calls=%async_computation | async-start | bytes 1572864 | tf_op jit(solution)/shard_map/all_to_all | solution.py:415
  17.4 12.8 %collective-permute-done.2.qr.near_a = bf16[2,256,1024]{2,1,0:T(8,128)(2,1)} collective-permute-done((bf16[2,256,1024]{2,1,0:T(8,128)(2,1)}, bf16[2,256,1024]{2,1,0:T(8,128)(2,1)}, u32[]{:S(2)}, u32[]{:S(2)}) %collective-permute-start.2) | collective-permute-done | bytes 1048608 | tf_op jit(solution)/shard_map/ppermute | solution.py:65
  30.2 2.7 %collective-permute-start.6 = (bf16[2,256,1024]{2,1,0:T(8,128)(2,1)}, bf16[2,256,1024]{2,1,0:T(8,128)(2,1)S(1)}, u32[]{:S(2)}, u32[]{:S(2)}) collective-permute-start(bf16[2,256,1024]{2,1,0:T(8,128)(2,1)} %collective-permute-done.2.qr.near_a), channel_id=1, source_target_pairs={{0,1},{1,0},{2,3},{3,2},{4,5},{5,4},{6,7},{7,6},{8,9},{9,8},{10,11... | collective-permute-start | bytes 3145736 | tf_op jit(solution)/shard_map/ppermute | solution.py:65
  32.9 5.6 %near.1.after_near = bf16[256,1152]{1,0:T(8,128)(2,1)} custom-call(s32[2,4]{1,0:T(2,128)} %offsets.11, bf16[2,256,1024]{2,1,0:T(8,128)(2,1)} %collective-permute-done.2.qr.near_a, bf16[512,2048]{1,0:T(8,128)(2,1)} %k.7, bf16[512,2048]{1,0:T(8,128)(2,1)} %collective-permute-done.ko, bf16[512,2048]{1,0:T(8,128)(2,1)} %v.7, ...), custom_call_target="tpu_custom_call" | custom-call | flops 1000 | bytes 1000 | tf_op jit(solution)/shard_map/near/pallas_call | solution.py:420
  38.6 0.9 %copy-done.8 = bf16[16,3,64,128]{3,2,1,0:T(8,128)(2,1)} copy-done((bf16[16,3,64,128]{3,2,1,0:T(8,128)(2,1)}, bf16[16,3,64,128]{3,2,1,0:T(8,128)(2,1)S(1)}, u32[]{:S(2)}) %copy-start.8) | copy-done | bytes 786456
  39.5 1.0 %copy-done.2 = bf16[2,256,1024]{2,1,0:T(8,128)(2,1)} copy-done((bf16[2,256,1024]{2,1,0:T(8,128)(2,1)}, bf16[2,256,1024]{2,1,0:T(8,128)(2,1)S(1)}, u32[]{:S(2)}) %copy-start.2) | copy-done | bytes 1048600
  40.5 2.1 %far.1 = bf16[16,80,128]{2,1,0:T(8,128)(2,1)} custom-call(s32[2,4]{1,0:T(2,128)} %offsets.11, bf16[16,3,64,128]{3,2,1,0:T(8,128)(2,1)} %copy-done.1, bf16[16,3,64,128]{3,2,1,0:T(8,128)(2,1)} %copy-done.8, bf16[256,1152]{1,0:T(8,128)(2,1)} %near.1.after_near, bf16[2,256,1024]{2,1,0:T(8,128)(2,1)} %copy-done.2), custom_call_target="tpu_custom_call" | custom-call | flops 1000 | bytes 1000 | tf_op jit(solution)/shard_map/far/pallas_call | solution.py:432
  42.6 7.5 %all-to-all-start.1 = ((bf16[16,80,128]{2,1,0:T(8,128)(2,1)}), bf16[16,80,128]{2,1,0:T(8,128)(2,1)S(1)}, u32[]{:S(2)}, u32[]{:S(2)}) async-start(bf16[16,80,128]{2,1,0:T(8,128)(2,1)} %far.1), calls=%async_computation.1 | async-start | bytes 655360 | tf_op jit(solution)/shard_map/all_to_all | solution.py:441
  50.2 1.3 %collective-permute-start.4 = (bf16[256,1152]{1,0:T(8,128)(2,1)S(1)}, bf16[256,1152]{1,0:T(8,128)(2,1)S(1)}, u32[]{:S(2)}, u32[]{:S(2)}) collective-permute-start(bf16[256,1152]{1,0:T(8,128)(2,1)S(1)} %copy-done.5), channel_id=1, source_target_pairs={{0,2},{1,3},{4,6},{5,7},{8,10},{9,11},{12,14},{13,15},{16,18},{17,... | collective-permute-start | bytes 1769480 | tf_op jit(solution)/shard_map/ppermute | solution.py:65
  51.5 6.5 %all-to-all-done.1.far_own = bf16[16,80,128]{2,1,0:T(8,128)(2,1)S(1)} async-done(((bf16[16,80,128]{2,1,0:T(8,128)(2,1)}), bf16[16,80,128]{2,1,0:T(8,128)(2,1)S(1)}, u32[]{:S(2)}, u32[]{:S(2)}) %all-to-all-start.1) | async-done | bytes 327712 | tf_op jit(solution)/shard_map/all_to_all | solution.py:441
  57.9 2.3 %collective-permute-start.7 = (bf16[16,80,128]{2,1,0:T(8,128)(2,1)S(1)}, bf16[16,80,128]{2,1,0:T(8,128)(2,1)S(1)}, u32[]{:S(2)}, u32[]{:S(2)}) collective-permute-start(bf16[16,80,128]{2,1,0:T(8,128)(2,1)S(1)} %all-to-all-done.1.far_own), channel_id=1, source_target_pairs={{0,1},{1,0},{2,3},{3,2},{4,5},{5,4},{6,7},{7,6},{8,9},{9,8},{10,11... | collective-permute-start | bytes 983048 | tf_op jit(solution)/shard_map/ppermute | solution.py:65
  60.3 1.3 %collective-permute-done.7.far_oth = bf16[16,80,128]{2,1,0:T(8,128)(2,1)S(1)} collective-permute-done((bf16[16,80,128]{2,1,0:T(8,128)(2,1)S(1)}, bf16[16,80,128]{2,1,0:T(8,128)(2,1)S(1)}, u32[]{:S(2)}, u32[]{:S(2)}) %collective-permute-start.7) | collective-permute-done | bytes 327712 | tf_op jit(solution)/shard_map/ppermute | solution.py:65
  61.5 0.7 copy-done.6
  62.3 12.4 %local.2.rest_0_ = bf16[512,2048]{1,0:T(8,128)(2,1)} custom-call(s32[2,4]{1,0:T(2,128)} %offsets.11, bf16[512,2048]{1,0:T(8,128)(2,1)} %q.5, bf16[512,2048]{1,0:T(8,128)(2,1)} %k.7, bf16[512,2048]{1,0:T(8,128)(2,1)} %v.7, bf16[512,2048]{1,0:T(8,128)(2,1)} %collective-permute-done.ko, bf16[512,2048]{1,0:T(8,128)(2,1)} %collective-permute-done.1.vo, ...), custom_call_target="tpu_custom_call" | custom-call | flops 1000 | bytes 1000 | tf_op jit(solution)/shard_map/local/pallas_call | solution.py:446
  74.7 0.8 copy-done.4
  75.5 12.0 %local.3 = bf16[512,2048]{1,0:T(8,128)(2,1)} custom-call(s32[2,4]{1,0:T(2,128)} %offsets.11, bf16[512,2048]{1,0:T(8,128)(2,1)} %q.5, bf16[512,2048]{1,0:T(8,128)(2,1)} %k.7, bf16[512,2048]{1,0:T(8,128)(2,1)} %v.7, bf16[512,2048]{1,0:T(8,128)(2,1)} %collective-permute-done.ko, ...), custom_call_target="tpu_custom_call", output_to_operand_aliasing={{}: (10, {})} | custom-call | flops 1000 | bytes 1000 | tf_op jit(solution)/shard_map/local/pallas_call | solution.py:446
  (20 shorter events, 0.0 us)
Async XLA Ops:
  0.0 6.4 %copy-start = (bf16[512,2048]{1,0:T(8,128)(2,1)S(1)}, bf16[512,2048]{1,0:T(8,128)(2,1)}, u32[]{:S(2)}) copy-start(bf16[512,2048]{1,0:T(8,128)(2,1)} %k.7) | copy-start | bytes 6291460
  4.4 2.9 %collective-permute-start.3 = (bf16[4,3,64,512]{3,2,1,0:T(8,128)(2,1)}, bf16[4,3,64,512]{3,2,1,0:T(8,128)(2,1)S(1)}, u32[]{:S(2)}, u32[]{:S(2)}) collective-permute-start(bf16[4,3,64,512]{3,2,1,0:T(8,128)(2,1)} %get-tuple-element.12), channel_id=1, source_target_pairs={{0,1},{1,0},{2,3},{3,2},{4,5},{5,4},{6,7},{7,6},{8,9},{9,8},{10,11... | collective-permute-start | bytes 2359304 | tf_op jit(solution)/shard_map/ppermute | solution.py:65
  5.2 25.0 %collective-permute-start.2 = (bf16[2,256,1024]{2,1,0:T(8,128)(2,1)}, bf16[2,256,1024]{2,1,0:T(8,128)(2,1)}, u32[]{:S(2)}, u32[]{:S(2)}) collective-permute-start(bf16[2,256,1024]{2,1,0:T(8,128)(2,1)} %get-tuple-element.10), channel_id=1, source_target_pairs={{0,2},{1,3},{2,0},{3,1},{4,6},{5,7},{6,4},{7,5},{8,10},{9,11},{10,... | collective-permute-start | bytes 3145736 | tf_op jit(solution)/shard_map/ppermute | solution.py:65
  6.4 26.5 %collective-permute-start = (bf16[512,2048]{1,0:T(8,128)(2,1)S(1)}, bf16[512,2048]{1,0:T(8,128)(2,1)}, u32[]{:S(2)}, u32[]{:S(2)}) collective-permute-start(bf16[512,2048]{1,0:T(8,128)(2,1)S(1)} %copy-done), channel_id=1, source_target_pairs={{0,1},{1,0},{2,3},{3,2},{4,5},{5,4},{6,7},{7,6},{8,9},{9,8},{10,11... | collective-permute-start | bytes 6291464 | tf_op jit(solution)/shard_map/ppermute | solution.py:65
  6.7 26.2 %collective-permute-start.1 = (bf16[512,2048]{1,0:T(8,128)(2,1)}, bf16[512,2048]{1,0:T(8,128)(2,1)}, u32[]{:S(2)}, u32[]{:S(2)}) collective-permute-start(bf16[512,2048]{1,0:T(8,128)(2,1)} %v.7), channel_id=1, source_target_pairs={{0,1},{1,0},{2,3},{3,2},{4,5},{5,4},{6,7},{7,6},{8,9},{9,8},{10,11... | collective-permute-start | bytes 6291464 | tf_op jit(solution)/shard_map/ppermute | solution.py:65
  7.3 0.9 %copy-start.7 = (bf16[4,3,64,512]{3,2,1,0:T(8,128)(2,1)}, bf16[4,3,64,512]{3,2,1,0:T(8,128)(2,1)S(1)}, u32[]{:S(2)}) copy-start(bf16[4,3,64,512]{3,2,1,0:T(8,128)(2,1)S(1)} %collective-permute-done.3.received) | copy-start | bytes 2359300
  10.6 19.6 %all-to-all-start = ((bf16[16,3,64,128]{3,2,1,0:T(8,128)(2,1)}), bf16[16,3,64,128]{3,2,1,0:T(8,128)(2,1)S(1)}, u32[]{:S(2)}, u32[]{:S(2)}) async-start(bf16[16,3,64,128]{3,2,1,0:T(8,128)(2,1)} %pack_second.1), calls=%async_computation | async-start | bytes 1572864 | tf_op jit(solution)/shard_map/all_to_all | solution.py:415
  30.2 2.7 %copy-start.1 = (bf16[16,3,64,128]{3,2,1,0:T(8,128)(2,1)}, bf16[16,3,64,128]{3,2,1,0:T(8,128)(2,1)S(1)}, u32[]{:S(2)}) copy-start(bf16[16,3,64,128]{3,2,1,0:T(8,128)(2,1)S(1)} %all-to-all-done.after_far.mine) | copy-start | bytes 2359300
  30.2 8.4 %collective-permute-start.6 = (bf16[2,256,1024]{2,1,0:T(8,128)(2,1)}, bf16[2,256,1024]{2,1,0:T(8,128)(2,1)S(1)}, u32[]{:S(2)}, u32[]{:S(2)}) collective-permute-start(bf16[2,256,1024]{2,1,0:T(8,128)(2,1)} %collective-permute-done.2.qr.near_a), channel_id=1, source_target_pairs={{0,1},{1,0},{2,3},{3,2},{4,5},{5,4},{6,7},{7,6},{8,9},{9,8},{10,11... | collective-permute-start | bytes 3145736 | tf_op jit(solution)/shard_map/ppermute | solution.py:65
  32.9 5.7 %collective-permute-start.5 = (bf16[16,3,64,128]{3,2,1,0:T(8,128)(2,1)S(1)}, bf16[16,3,64,128]{3,2,1,0:T(8,128)(2,1)S(1)}, u32[]{:S(2)}, u32[]{:S(2)}) collective-permute-start(bf16[16,3,64,128]{3,2,1,0:T(8,128)(2,1)S(1)} %all-to-all-done.after_far.mine), channel_id=1, source_target_pairs={{0,1},{1,0},{2,3},{3,2},{4,5},{5,4},{6,7},{7,6},{8,9},{9,8},{10,11... | collective-permute-start | bytes 2359304 | tf_op jit(solution)/shard_map/ppermute | solution.py:65
  38.6 11.6 %copy-start.5 = (bf16[256,1152]{1,0:T(8,128)(2,1)S(1)}, bf16[256,1152]{1,0:T(8,128)(2,1)}, u32[]{:S(2)}) copy-start(bf16[256,1152]{1,0:T(8,128)(2,1)} %near.1.after_near) | copy-start | bytes 1769476
  38.6 0.9 %copy-start.8 = (bf16[16,3,64,128]{3,2,1,0:T(8,128)(2,1)}, bf16[16,3,64,128]{3,2,1,0:T(8,128)(2,1)S(1)}, u32[]{:S(2)}) copy-start(bf16[16,3,64,128]{3,2,1,0:T(8,128)(2,1)S(1)} %collective-permute-done.5.other) | copy-start | bytes 2359300
  39.5 1.0 %copy-start.2 = (bf16[2,256,1024]{2,1,0:T(8,128)(2,1)}, bf16[2,256,1024]{2,1,0:T(8,128)(2,1)S(1)}, u32[]{:S(2)}) copy-start(bf16[2,256,1024]{2,1,0:T(8,128)(2,1)S(1)} %collective-permute-done.6.after_moved.near_b) | copy-start | bytes 3145732
  42.6 15.3 %all-to-all-start.1 = ((bf16[16,80,128]{2,1,0:T(8,128)(2,1)}), bf16[16,80,128]{2,1,0:T(8,128)(2,1)S(1)}, u32[]{:S(2)}, u32[]{:S(2)}) async-start(bf16[16,80,128]{2,1,0:T(8,128)(2,1)} %far.1), calls=%async_computation.1 | async-start | bytes 655360 | tf_op jit(solution)/shard_map/all_to_all | solution.py:441
  50.2 24.6 %collective-permute-start.4 = (bf16[256,1152]{1,0:T(8,128)(2,1)S(1)}, bf16[256,1152]{1,0:T(8,128)(2,1)S(1)}, u32[]{:S(2)}, u32[]{:S(2)}) collective-permute-start(bf16[256,1152]{1,0:T(8,128)(2,1)S(1)} %copy-done.5), channel_id=1, source_target_pairs={{0,2},{1,3},{4,6},{5,7},{8,10},{9,11},{12,14},{13,15},{16,18},{17,... | collective-permute-start | bytes 1769480 | tf_op jit(solution)/shard_map/ppermute | solution.py:65
  57.9 3.6 %copy-start.3 = (bf16[16,80,128]{2,1,0:T(8,128)(2,1)}, bf16[16,80,128]{2,1,0:T(8,128)(2,1)S(1)}, u32[]{:S(2)}) copy-start(bf16[16,80,128]{2,1,0:T(8,128)(2,1)S(1)} %all-to-all-done.1.far_own) | copy-start | bytes 983044
  57.9 3.6 %collective-permute-start.7 = (bf16[16,80,128]{2,1,0:T(8,128)(2,1)S(1)}, bf16[16,80,128]{2,1,0:T(8,128)(2,1)S(1)}, u32[]{:S(2)}, u32[]{:S(2)}) collective-permute-start(bf16[16,80,128]{2,1,0:T(8,128)(2,1)S(1)} %all-to-all-done.1.far_own), channel_id=1, source_target_pairs={{0,1},{1,0},{2,3},{3,2},{4,5},{5,4},{6,7},{7,6},{8,9},{9,8},{10,11... | collective-permute-start | bytes 983048 | tf_op jit(solution)/shard_map/ppermute | solution.py:65
  61.5 0.7 copy-start.6
  74.7 0.8 copy-start.4

commit v5 on v4

v5 whole, which is shorter than its diff:
```python
import functools

import jax
import jax.numpy as jnp
import numpy as np
from jax import lax
from jax.experimental import pallas as pl
from jax.experimental.pallas import tpu as pltpu
from jax.sharding import Mesh
from jax.sharding import PartitionSpec as P

HD = 128
BLK = 128
HALF = 64
HEADS = 16
GROUPS = 4
GH = 4
GW = GH * HD
ROWS = 512
NSEL = 256
AXES = ("x", "y", "z", "c")
SIZES = (4, 4, 4, 2)
SCALE = float(HD**-0.5 * np.log2(np.e))
LOW = -1e30
BF, F32 = jnp.bfloat16, jnp.float32


class Place:
    def __init__(self, offsets):
        self.x, self.y, self.z, self.core = (lax.axis_index(a) for a in AXES)
        self.offsets = offsets
        self.odd = self.z % 2 == 1

    def near(self, g):
        return self.offsets[0, g]

    def far_z(self, g):
        return self.offsets[1, g] // 8

    def far_core(self, g):
        return self.offsets[1, g] // 4 % 2

    def far_block(self, g):
        return self.offsets[1, g] % 4

    def far_here(self, g):
        return (self.far_z(g) == self.z) & (self.far_core(g) == self.core)


def route(step):
    pairs = []
    for index in np.ndindex(*SIZES):
        target = step(*index)
        if target is not None:
            pairs.append((int(np.ravel_multi_index(index, SIZES)), int(np.ravel_multi_index(target, SIZES))))
    return pairs


CORE = route(lambda x, y, z, c: (x, y, z, 1 - c))
PAIR = route(lambda x, y, z, c: (x, y, z ^ 1, c))
TO_ODD = route(lambda x, y, z, c: (x, y, z + 1, c) if z % 2 == 0 else None)


def move(array, pairs):
    return lax.ppermute(array, AXES, pairs)


def cost(flops=1000):
    return pl.CostEstimate(flops=flops, bytes_accessed=1000, transcendentals=0)


ANY = pl.BlockSpec(memory_space=pl.ANY)
SMEM = pl.BlockSpec(memory_space=pltpu.SMEM)
PARAMS = dict(vmem_limit_bytes=28 * 1024 * 1024)


def nt(a, b):
    return lax.dot_general(a, b, (((1,), (1,)), ((), ())), preferred_element_type=F32)


def nn(a, b):
    return lax.dot_general(a, b, (((1,), (0,)), ((), ())), preferred_element_type=F32)


def three(x):
    hi = x.astype(BF).astype(F32)
    rest = x - hi
    mid = rest.astype(BF).astype(F32)
    return hi, mid, rest - mid


def rows_at(first, count):
    return pl.ds(pl.multiple_of(first, count), count)


def group_cols(g):
    return pl.ds(g * GW, GW)


def run_copies(copies):
    for c in copies:
        c.start()
    for c in copies:
        c.wait()


def pack_far(offsets, q, k, v, send, keep, sems):
    here = Place(offsets)
    copies = []
    for g in range(GROUPS):
        for t, source in enumerate((q, k, v)):
            first = here.far_block(g) * BLK
            for half, target in ((1 - here.core, send), (here.core, keep)):
                rows = rows_at(first + half * HALF, HALF)
                copies.append(
                    pltpu.make_async_copy(source.at[rows, group_cols(g)], target.at[g, t], sems.at[len(copies)])
                )
    run_copies(copies)


def pack_near(offsets, q, k, v, near_q, near_kv, sems):
    here = Place(offsets)
    for odd in (False, True):

        @pl.when(here.odd == odd)
        def _():
            copies = []
            for g in range(2):
                for half in range(2):
                    rows = rows_at((here.near(g if odd else g + 2) + 2 * half) * BLK, BLK)
                    to = pl.ds(half * BLK, BLK)
                    for t, source in enumerate((q,) if odd else (k, v)):
                        target = near_q if odd else near_kv.at[t]
                        copies.append(
                            pltpu.make_async_copy(
                                source.at[rows, group_cols(g if odd else g + 2)],
                                target.at[to, group_cols(g)],
                                sems.at[len(copies)],
                            )
                        )
            run_copies(copies)


def pack_second(offsets, kept, received, after_near, out):
    here = Place(offsets)
    for g in range(GROUPS):
        mine = here.far_core(g) == here.core
        for source, flag in ((kept, mine), (received, jnp.logical_not(mine))):

            @pl.when(flag)
            def _():
                for t in range(3):
                    for h in range(GH):
                        out[h * GROUPS + g, t] = source[g, t, :, h * HD : (h + 1) * HD]


def with_ones(val):
    return jnp.concatenate([val, jnp.ones((val.shape[0], HD), BF)], axis=1)


def with_ones(val):
    return jnp.concatenate([val, jnp.ones((val.shape[0], HD), BF)], axis=1)


def softmax_parts(parts, values):
    top = functools.reduce(jnp.maximum, [jnp.max(s, axis=1, keepdims=True) for s in parts]) * SCALE
    both = 0.0
    for s, val in zip(parts, values):
        both = both + nn(jnp.exp2(s * SCALE - top).astype(BF), with_ones(val))
    return both[:, :HD] / both[:, HD:], top + jnp.log2(both[:, HD:])


def head_cols(h):
    return slice(h * HD, (h + 1) * HD)


def near_part(heads, q_of, keys_of, vals_of, out):
    lane = lax.broadcasted_iota(jnp.int32, (NSEL, HD), 1)
    stats = jnp.zeros((NSEL, HD), F32)
    for h in range(heads):
        keys = jnp.concatenate(keys_of(h), axis=0)
        vals = jnp.concatenate(vals_of(h), axis=0)
        o, m = softmax_parts([nt(q_of(h), keys)], [vals])
        out[:, head_cols(h)] = o.astype(BF)
        for n, term in enumerate(three(m)):
            stats = jnp.where(lane == n * heads + h, term, stats)
    out[:, heads * HD :] = stats.astype(BF)


def near_even(offsets, qr, k, ko, v, vo, out, keys, vals, sems):
    here = Place(offsets)

    @pl.when(jnp.logical_not(here.odd))
    def _():
        copies = []
        for g in range(2):
            for n, (source, half) in enumerate([(0, 0), (0, 1), (1, 0), (1, 1)]):
                rows = rows_at((here.near(g) + 2 * half) * BLK, BLK)
                for two, target in (((k, ko), keys), ((v, vo), vals)):
                    copies.append(
                        pltpu.make_async_copy(
                            two[source].at[rows, group_cols(g)],
                            target.at[pl.ds(n * BLK, BLK), group_cols(g)],
                            sems.at[len(copies)],
                        )
                    )
        run_copies(copies)
        near_part(
            2 * GH,
            lambda h: qr[:, head_cols(h)],
            lambda h: [keys[:, head_cols(h)]],
            lambda h: [vals[:, head_cols(h)]],
            out,
        )


def near_odd(offsets, q, kv_a, kv_b, out, queries, sems):
    here = Place(offsets)

    @pl.when(here.odd)
    def _():
        copies = []
        for g in range(2):
            for half in range(2):
                rows = rows_at((here.near(2 + g) + 2 * half) * BLK, BLK)
                copies.append(
                    pltpu.make_async_copy(
                        q.at[rows, group_cols(2 + g)],
                        queries.at[pl.ds(half * BLK, BLK), group_cols(g)],
                        sems.at[len(copies)],
                    )
                )
        run_copies(copies)
        near_part(
            2 * GH,
            lambda h: queries[:, head_cols(h)],
            lambda h: [r[0, :, head_cols(h)] for r in (kv_a, kv_b)],
            lambda h: [r[1, :, head_cols(h)] for r in (kv_a, kv_b)],
            out,
        )


def far_kernel(offsets, mine, other, out):
    here = Place(offsets)

    @pl.when(here.far_z(here.y) == here.z)
    def _():
        late = here.core == 1
        for t in range(4):
            upto = 4 * t + 4
            q = mine[4 * t : upto, 0].reshape(256, HD)
            ri = lax.broadcasted_iota(jnp.int32, (256, 256), 0)
            ci = lax.broadcasted_iota(jnp.int32, (256, 256), 1)
            own_ok = (ci // HALF < ri // HALF) | ((ci // HALF == ri // HALF) & (ci <= ri))
            oth_ok = (ci // HALF < ri // HALF) | ((ci // HALF == ri // HALF) & late)
            parts, vals = [], []
            for source, ok in ((mine, own_ok), (other, oth_ok)):
                s = nt(q, source[0:upto, 1].reshape(upto * HALF, HD))
                d = jnp.where(ok, s[:, t * 256 :], LOW)
                parts.append(d if t == 0 else jnp.concatenate([s[:, : t * 256], d], axis=1))
                vals.append(source[0:upto, 2].reshape(upto * HALF, HD))
            o, m = softmax_parts(parts, vals)
            o = o.astype(BF)
            turned = jnp.transpose(m)[0:16]
            row = lax.broadcasted_iota(jnp.int32, (16, 256), 0)
            stats = jnp.zeros((16, 256), F32)
            for n, term in enumerate(three(turned)):
                stats = jnp.where(row == n, term, stats)
            stats = stats.astype(BF)
            for b in range(4):
                out[4 * t + b, 0:HALF] = o[b * HALF : (b + 1) * HALF]
                out[4 * t + b, HALF:] = stats[:, (b // 2) * 128 : (b // 2) * 128 + 128]


def spread_lanes(stats, places):
    line = lax.broadcasted_iota(jnp.int32, (HD, HD), 0)
    hit = functools.reduce(jnp.logical_or, [line == p for p in places])
    return nn(stats, jnp.where(hit, 1.0, 0.0).astype(BF))


def far_piece(here, far_own, far_oth, g, h):
    outs, masses = [], []
    picks = lax.broadcasted_iota(jnp.int32, (16, HD), 0) < 3
    picks = jnp.where(picks, 1.0, 0.0).astype(BF)
    for source in (far_own, far_oth):
        tile = source[h * GROUPS + g]
        outs.append(tile[0:HALF].astype(F32))
        turned = lax.dot_general(
            tile[HALF:], picks, (((0,), (0,)), ((), ())), preferred_element_type=F32
        )
        masses.append(jnp.where(here.y % 2 == 1, turned[HALF:], turned[:HALF]))
    first = here.core == 0

    def ordered(a, b):
        return jnp.concatenate([jnp.where(first, a, b), jnp.where(first, b, a)], axis=0)

    return ordered(*outs), ordered(*masses)


def local_parts(core):
    if core == 0:
        return [[("own", 256, True)], [("own", 512, False), ("oth", 512, True)]]
    return [[("oth", 512, False), ("own", 256, True)], [("oth", 512, True)]]


def local_weights(near, parts, scores):
    extra = [jnp.where(near == i, 1.0, 0.0).astype(F32) for i in range(2)]
    causal = lax.broadcasted_iota(jnp.int32, (BLK, BLK), 0) >= lax.broadcasted_iota(jnp.int32, (BLK, BLK), 1)
    weights, tops = [[] for _ in scores], []
    for i in range(2):
        blocks = []
        for (_, count, diagonal), sc in zip(parts, scores):
            upto = count // BLK - (1 - i if diagonal else 0)
            mine = [sc[i * BLK : (i + 1) * BLK, j * BLK : (j + 1) * BLK] for j in range(upto)]
            if diagonal:
                mine[-1] = jnp.where(causal, mine[-1], LOW)
            blocks.append(mine)
        top = functools.reduce(jnp.maximum, sum(blocks, []))
        top = jnp.max(top, axis=1, keepdims=True) * SCALE
        raised = top - extra[i]
        for n, mine in enumerate(blocks):
            pieces = [
                jnp.exp2(b * SCALE - (raised if j % 2 == i else top)).astype(BF) for j, b in enumerate(mine)
            ]
            pieces += [jnp.zeros((BLK, BLK), BF)] * (parts[n][1] // BLK - len(pieces))
            weights[n].append(jnp.concatenate(pieces, axis=1))
        tops.append(jnp.broadcast_to(top, (BLK, HD)))
    return [jnp.concatenate(w, axis=0) for w in weights], jnp.concatenate(tops, axis=0)


UNROLL = GH


def local_kernel(offsets, q_in, qo_in, k_in, ko_in, v_in, vo_in, after_near, mine, away, q, qo, k, ko, v, vo, sems):
    here = Place(offsets)
    keys, vals = {"own": k, "oth": ko}, {"own": v, "oth": vo}
    for target in (mine, away):
        target[:, HEADS * HD :] = jnp.zeros((NSEL, HD), BF)

    for core in range(2):
        tiles = local_parts(core)
        own = 512 if core == 0 else 256

        def stage(g, own=own):
            cols = pl.ds(pl.multiple_of(g * GW, GW), GW)
            pieces = (
                (q_in, 0, q, 256),
                (k_in, 0, k, own),
                (ko_in, 0, ko, 512),
                (qo_in, 256, qo, 256),
                (v_in, 0, v, own),
                (vo_in, 0, vo, 512),
            )
            return [
                pltpu.make_async_copy(a.at[pl.ds(first, n), cols], b.at[pl.ds(0, n), cols], sems.at[g, i])
                for i, (a, first, b, n) in enumerate(pieces)
            ]

        @pl.when(here.core == core)
        def _():
            for g in range(GROUPS):
                for c in stage(g):
                    c.start()

            @pl.loop(0, HEADS // UNROLL)
            def _(turn):
                for c in stage(turn):
                    c.wait()
                items = [(h, t) for h in range(UNROLL) for t in range(2)]

                def cols(h):
                    return pl.ds(pl.multiple_of(turn * (UNROLL * HD), HD) + h * HD, HD)

                def score(h, t):
                    queries = (qo if t else q)[:, cols(h)]
                    return [nt(queries, keys[w][0:n, cols(h)]) for w, n, _ in tiles[t]]

                def finish(h, t, weights, top):
                    target = (mine, away)[t]
                    both = 0.0
                    for (w, n, _), p in zip(tiles[t], weights):
                        both = both + nn(p, with_ones(vals[w][0:n, cols(h)]))
                    target[:, cols(h)] = (both[:, :HD] / both[:, HD:]).astype(BF)
                    lane = lax.broadcasted_iota(jnp.int32, (256, HD), 1)
                    stats = target[:, HEADS * HD :].astype(F32)
                    for n, term in enumerate(three(top + jnp.log2(both[:, HD:]))):
                        stats = jnp.where(lane == n * HEADS + turn * UNROLL + h, term, stats)
                    target[:, HEADS * HD :] = stats.astype(BF)

                scores = score(*items[0])
                last = None
                for n, (h, t) in enumerate(items):
                    ahead = score(*items[n + 1]) if n + 1 < len(items) else None
                    current = local_weights(here.near((turn * UNROLL + h) // GH), tiles[t], scores)
                    if last is not None:
                        finish(*last)
                    last = (h, t, *current)
                    scores = ahead
                finish(*last)


def mix(parts):
    top = functools.reduce(jnp.maximum, [m for _, m in parts])
    up = down = 0.0
    for o, m in parts:
        e = jnp.exp2(m - top)
        up, down = up + e * o, down + e
    return (up / down).astype(BF)


def merge_kernel(offsets, mine, back, near_a, near_b, far_own, far_oth, out, done, sems):
    here = Place(offsets)
    nears = (near_a, near_b)
    halves = (mine, back)

    def own_part(half, rows, g, h):
        source = halves[half]
        return (
            source[rows, pl.ds(g * GW + h * HD, HD)].astype(F32),
            spread_lanes(source[rows, HEADS * HD :], [n * HEADS + g * GH + h for n in range(3)]),
        )

    def next_part(half, g, h):
        rows = slice(half * BLK, (half + 1) * BLK)
        source, place = nears[g // 2], (g % 2) * GH + h
        return (
            source[rows, head_cols(place)].astype(F32),
            spread_lanes(source[rows, 2 * GW :], [n * 2 * GH + place for n in range(3)]),
        )

    def put(half, rows, g, h, parts):
        start = rows.start + half * NSEL
        done[pl.ds(pl.multiple_of(start, BLK), BLK), pl.ds(g * GW + h * HD, HD)] = mix(parts)

    copies = []
    for g in range(GROUPS):
        for half in range(2):
            done[half * NSEL : (half + 1) * NSEL, group_cols(g)] = halves[half][:, group_cols(g)]

        near_rows = rows_at(here.near(g) * BLK, BLK)
        far_rows = rows_at(here.far_block(g) % 2 * BLK, BLK)
        near_too = here.odd & (here.far_block(g) % 2 == here.near(g))

        @pl.when(here.odd)
        def _():
            for half in range(2):
                for h in range(GH):
                    put(half, near_rows, g, h, [own_part(half, near_rows, g, h), next_part(half, g, h)])

        for half in range(2):
            for both in (False, True):

                @pl.when(here.far_here(g) & (here.far_block(g) // 2 == half) & (near_too == both))
                def _():
                    for h in range(GH):
                        parts = [own_part(half, far_rows, g, h), far_piece(here, far_own, far_oth, g, h)]
                        if both:
                            parts.append(next_part(half, g, h))
                        put(half, far_rows, g, h, parts)

        copies.append(pltpu.make_async_copy(done.at[:, group_cols(g)], out.at[:, group_cols(g)], sems.at[g]))
        copies[-1].start()
    for c in copies:
        c.wait()


VMEM = pl.BlockSpec(memory_space=pltpu.VMEM)
HBM = pl.BlockSpec(memory_space=pltpu.HBM)


def shape(*dims):
    return jax.ShapeDtypeStruct(dims, BF)


def hbm(array):
    return pltpu.with_memory_space_constraint(array, pltpu.HBM)


def device_part(q, k, v, offsets):
    params = pltpu.CompilerParams(**PARAMS)

    def call(kernel, outs, operands, places, sems=None, scratch=(), out_places=VMEM, flops=1000):
        return pl.pallas_call(
            kernel,
            out_shape=outs,
            in_specs=[SMEM] + places,
            out_specs=out_places,
            scratch_shapes=list(scratch) + ([] if sems is None else [pltpu.SemaphoreType.DMA((sems,))]),
            compiler_params=params,
            cost_estimate=cost(flops),
            name=kernel.__name__,
        )(hbm(offsets), *operands)

    qh, kh, vh = hbm(q), hbm(k), hbm(v)
    half_shape = shape(GROUPS, 3, HALF, GW)
    far_send, far_keep = call(
        pack_far, [half_shape] * 2, (qh, kh, vh), [HBM] * 3, sems=6 * GROUPS, out_places=[VMEM] * 2
    )
    far_recv = move(far_send, CORE)
    near_q, near_kv = call(
        pack_near,
        [shape(NSEL, 2 * GW), shape(2, NSEL, 2 * GW)],
        (qh, kh, vh),
        [HBM] * 3,
        sems=8,
        out_places=[VMEM] * 2,
    )
    near_qr, near_kvr = move(near_q, PAIR), move(near_kv, TO_ODD)
    qo, ko, vo = hbm(move(q, CORE)), hbm(move(k, CORE)), hbm(move(v, CORE))
    far_pack = call(pack_second, shape(HEADS, 3, HALF, HD), (far_keep, far_recv, near_q), [VMEM] * 2 + [ANY])
    far_mine = lax.all_to_all(far_pack, ("x", "y"), 0, 0, tiled=True)

    near_out = call(
        near_even,
        shape(NSEL, 2 * GW + HD),
        (near_qr, kh, ko, vh, vo),
        [VMEM] + [HBM] * 4,
        sems=16,
        scratch=[pltpu.VMEM((ROWS, 2 * GW), BF)] * 2,
    )
    near_back = move(near_out, TO_ODD)
    rows = HEADS * HD
    mine, away = call(
        local_kernel,
        [shape(NSEL, rows + HD)] * 2,
        (qh, qo, kh, ko, vh, vo, near_out),
        [HBM] * 6 + [ANY],
        scratch=[pltpu.VMEM((n, rows), BF) for n in (NSEL, NSEL, ROWS, ROWS, ROWS, ROWS)]
        + [pltpu.SemaphoreType.DMA((GROUPS, 6))],
        out_places=[VMEM] * 2,
        flops=10**10,
    )
    back = move(away, CORE)
    far_mine, near_kvr, mine = lax.optimization_barrier((far_mine, near_kvr, mine))
    far_other = move(far_mine, CORE)
    far_out = call(far_kernel, shape(HEADS, HALF + 16, HD), (far_mine, far_other), [VMEM] * 2)
    far_back = lax.all_to_all(far_out, ("x", "y"), 0, 0, tiled=True)
    near_here = call(
        near_odd,
        shape(NSEL, 2 * GW + HD),
        (qh, near_kvr, move(near_kvr, CORE)),
        [HBM] + [VMEM] * 2,
        sems=4,
        scratch=[pltpu.VMEM((NSEL, 2 * GW), BF)],
    )
    far_back, near_back = lax.optimization_barrier((far_back, near_back))
    far_back_other = move(far_back, CORE)

    return call(
        merge_kernel,
        shape(ROWS, HEADS * HD),
        (mine, back, near_back, near_here, far_back, far_back_other),
        [VMEM] * 6,
        sems=GROUPS,
        scratch=[pltpu.VMEM((ROWS, HEADS * HD), BF)],
        out_places=HBM,
    )


def solution(mesh):
    cube = Mesh(mesh.devices.reshape(SIZES), AXES)
    rows = P(AXES, None)
    return jax.shard_map(
        device_part, mesh=cube, in_specs=(rows, rows, rows, P()), out_specs=rows, check_vma=False
    )
```

time: 89.1 us -> 77.6 us (0.87)
  the two profiles are of different devices: /device:TPU:65 before, /device:TPU:97 now
where the time goes in v5:
time: 77.6 us; the launch traced here: 77 us
  Pallas kernels  33.1 us (43%)
  starting transfers between devices  22.3 us (29%)
  waiting for transfers between devices  19 us (24%)
  local copies, waits for them, and re-layouts  2.22 us (3%)
    pallas_call x8, Pallas kernels, call(): pl.pallas_call(kernel, out_shape=outs, in_specs=[SMEM] + places, out_spec...  33.1 us
    ppermute x11, waiting for transfers between devices, move(): return lax.ppermute(array, AXES, pairs)  15.4 us
    ppermute x11, starting transfers between devices, move(): return lax.ppermute(array, AXES, pairs)  8.79 us
    all_to_all x1, starting transfers between devices, device_part(): far_back = lax.all_to_all(far_out, ('x', 'y'), 0, 0, tiled=True)  6.76 us
    all_to_all x1, starting transfers between devices, device_part(): far_mine = lax.all_to_all(far_pack, ('x', 'y'), 0, 0, tiled=True)  6.75 us
    all_to_all x1, waiting for transfers between devices, device_part(): far_back = lax.all_to_all(far_out, ('x', 'y'), 0, 0, tiled=True)  3.67 us
    unnamed x8, local copies, waits for them, and re-layouts  2.22 us
  transfers between devices with their start and end apart: 13, of which 5 were waited for; matrix products, arithmetic and copies ran while one was open for 0% of the time, Pallas kernels for 37%

profile of v5, /device:TPU:97, one launch (start us, length us, event | category | flops | bytes accessed | tf_op | source)
XLA Modules:
  0.0 77.0 jit_solution(2522467716081800339)
XLA Ops:
  0.0 0.7 collective-permute-start.3
  0.7 0.5 collective-permute-start.2
  1.2 2.3 %pack_far.1 = (bf16[4,3,64,512]{3,2,1,0:T(8,128)(2,1)S(1)}, bf16[4,3,64,512]{3,2,1,0:T(8,128)(2,1)S(1)}) custom-call(s32[2,4]{1,0:T(2,128)} %offsets.15, bf16[512,2048]{1,0:T(8,128)(2,1)} %q.5, bf16[512,2048]{1,0:T(8,128)(2,1)} %k_in.1, bf16[512,2048]{1,0:T(8,128)(2,1)} %v_in.1), custom_call_target="tpu_custom_call" | custom-call | flops 1000 | bytes 1000 | tf_op jit(solution)/shard_map/pack_far/pallas_call | solution.py:483
  3.6 2.9 %pack_near.1 = (bf16[256,1024]{1,0:T(8,128)(2,1)S(1)}, bf16[2,256,1024]{2,1,0:T(8,128)(2,1)}) custom-call(s32[2,4]{1,0:T(2,128)} %offsets.15, bf16[512,2048]{1,0:T(8,128)(2,1)} %q.5, bf16[512,2048]{1,0:T(8,128)(2,1)} %k_in.1, bf16[512,2048]{1,0:T(8,128)(2,1)} %v_in.1), custom_call_target="tpu_custom_call" | custom-call | flops 1000 | bytes 1000 | tf_op jit(solution)/shard_map/pack_near/pallas_call | solution.py:483
  6.5 0.4 collective-permute-start.5
  6.9 2.7 %collective-permute-done.received = bf16[4,3,64,512]{3,2,1,0:T(8,128)(2,1)S(1)} collective-permute-done((bf16[4,3,64,512]{3,2,1,0:T(8,128)(2,1)S(1)}, bf16[4,3,64,512]{3,2,1,0:T(8,128)(2,1)S(1)}, u32[]{:S(2)}, u32[]{:S(2)}) %collective-permute-start) | collective-permute-done | bytes 786464 | tf_op jit(solution)/shard_map/ppermute | solution.py:65
  9.6 1.3 %collective-permute-start.1 = (bf16[2,256,1024]{2,1,0:T(8,128)(2,1)}, bf16[2,256,1024]{2,1,0:T(8,128)(2,1)S(1)}, u32[]{:S(2)}, u32[]{:S(2)}) collective-permute-start(bf16[2,256,1024]{2,1,0:T(8,128)(2,1)} %get-tuple-element.19), channel_id=1, source_target_pairs={{0,2},{1,3},{4,6},{5,7},{8,10},{9,11},{12,14},{13,15},{16,18},{17,... | collective-permute-start | bytes 3145736 | tf_op jit(solution)/shard_map/ppermute | solution.py:65
  10.9 1.8 %pack_second.1 = bf16[16,3,64,128]{3,2,1,0:T(8,128)(2,1)} custom-call(s32[2,4]{1,0:T(2,128)} %offsets.15, bf16[4,3,64,512]{3,2,1,0:T(8,128)(2,1)S(1)} %get-tuple-element.16.kept, bf16[4,3,64,512]{3,2,1,0:T(8,128)(2,1)S(1)} %collective-permute-done.received, bf16[256,1024]{1,0:T(8,128)(2,1)S(1)} %get-tuple-element.18.after_near), custom_call_target="tpu_custom_call" | custom-call | flops 1000 | bytes 1000 | tf_op jit(solution)/shard_map/pack_second/pallas_call | solution.py:483
  12.7 6.8 %all-to-all-start = ((bf16[16,3,64,128]{3,2,1,0:T(8,128)(2,1)}), bf16[16,3,64,128]{3,2,1,0:T(8,128)(2,1)S(1)}, u32[]{:S(2)}, u32[]{:S(2)}) async-start(bf16[16,3,64,128]{3,2,1,0:T(8,128)(2,1)} %pack_second.1), calls=%async_computation | async-start | bytes 1572864 | tf_op jit(solution)/shard_map/all_to_all | solution.py:511
  19.6 0.8 %near_even.1.after_near = bf16[256,1152]{1,0:T(8,128)(2,1)S(1)} custom-call(s32[2,4]{1,0:T(2,128)} %offsets.15, bf16[256,1024]{1,0:T(8,128)(2,1)S(1)} %collective-permute-done.5.qr, bf16[512,2048]{1,0:T(8,128)(2,1)} %k_in.1, bf16[512,2048]{1,0:T(8,128)(2,1)} %collective-permute-done.3.ko.ko_in, bf16[512,2048]{1,0:T(8,128)(2,1)} %v_in.1, ...), custom_call_target="tpu_custom_call" | custom-call | flops 1000 | bytes 1000 | tf_op jit(solution)/shard_map/near_even/pallas_call | solution.py:483
  20.5 12.2 %local_kernel.1 = (bf16[256,2176]{1,0:T(8,128)(2,1)S(1)}, bf16[256,2176]{1,0:T(8,128)(2,1)S(1)}) custom-call(s32[2,4]{1,0:T(2,128)} %offsets.15, bf16[512,2048]{1,0:T(8,128)(2,1)} %q.5, bf16[512,2048]{1,0:T(8,128)(2,1)} %collective-permute-done.2.qo_in, bf16[512,2048]{1,0:T(8,128)(2,1)} %k_in.1, bf16[512,2048]{1,0:T(8,128)(2,1)} %collective-permute-done.3.ko.ko_in, ...), custom_call_target="tpu_custom_call" | custom-call | flops 10000000000 | bytes 1000 | tf_op jit(solution)/shard_map/local_kernel/pallas_call | solution.py:483
  32.7 1.0 %copy-done.3 = bf16[256,2176]{1,0:T(8,128)(2,1)} copy-done((bf16[256,2176]{1,0:T(8,128)(2,1)}, bf16[256,2176]{1,0:T(8,128)(2,1)S(1)}, u32[]{:S(2)}) %copy-start.3) | copy-done | bytes 1114136
  33.7 8.4 %collective-permute-done.1.kv_a = bf16[2,256,1024]{2,1,0:T(8,128)(2,1)S(1)} collective-permute-done((bf16[2,256,1024]{2,1,0:T(8,128)(2,1)}, bf16[2,256,1024]{2,1,0:T(8,128)(2,1)S(1)}, u32[]{:S(2)}, u32[]{:S(2)}) %collective-permute-start.1) | collective-permute-done | bytes 1048608 | tf_op jit(solution)/shard_map/ppermute | solution.py:65
  42.0 1.3 %collective-permute-start.7 = (bf16[16,3,64,128]{3,2,1,0:T(8,128)(2,1)S(1)}, bf16[16,3,64,128]{3,2,1,0:T(8,128)(2,1)S(1)}, u32[]{:S(2)}, u32[]{:S(2)}) collective-permute-start(bf16[16,3,64,128]{3,2,1,0:T(8,128)(2,1)S(1)} %all-to-all-done.mine), channel_id=1, source_target_pairs={{0,1},{1,0},{2,3},{3,2},{4,5},{5,4},{6,7},{7,6},{8,9},{9,8},{10,11... | collective-permute-start | bytes 2359304 | tf_op jit(solution)/shard_map/ppermute | solution.py:65
  43.4 1.0 %collective-permute-start.6 = (bf16[256,2176]{1,0:T(8,128)(2,1)}, bf16[256,2176]{1,0:T(8,128)(2,1)S(1)}, u32[]{:S(2)}, u32[]{:S(2)}) collective-permute-start(bf16[256,2176]{1,0:T(8,128)(2,1)} %copy-done.3), channel_id=1, source_target_pairs={{0,1},{1,0},{2,3},{3,2},{4,5},{5,4},{6,7},{7,6},{8,9},{9,8},{10,11... | collective-permute-start | bytes 3342344 | tf_op jit(solution)/shard_map/ppermute | solution.py:65
  44.4 1.3 %collective-permute-start.8 = (bf16[256,1152]{1,0:T(8,128)(2,1)}, bf16[256,1152]{1,0:T(8,128)(2,1)}, u32[]{:S(2)}, u32[]{:S(2)}) collective-permute-start(bf16[256,1152]{1,0:T(8,128)(2,1)} %copy-done.2), channel_id=1, source_target_pairs={{0,2},{1,3},{4,6},{5,7},{8,10},{9,11},{12,14},{13,15},{16,18},{17,... | collective-permute-start | bytes 1769480 | tf_op jit(solution)/shard_map/ppermute | solution.py:65
  45.7 4.3 %far_kernel.1 = bf16[16,80,128]{2,1,0:T(8,128)(2,1)} custom-call(s32[2,4]{1,0:T(2,128)} %offsets.15, bf16[16,3,64,128]{3,2,1,0:T(8,128)(2,1)S(1)} %all-to-all-done.mine, bf16[16,3,64,128]{3,2,1,0:T(8,128)(2,1)S(1)} %collective-permute-done.7.other), custom_call_target="tpu_custom_call" | custom-call | flops 1000 | bytes 1000 | tf_op jit(solution)/shard_map/far_kernel/pallas_call | solution.py:483
  50.0 6.8 %all-to-all-start.1 = ((bf16[16,80,128]{2,1,0:T(8,128)(2,1)}), bf16[16,80,128]{2,1,0:T(8,128)(2,1)S(1)}, u32[]{:S(2)}, u32[]{:S(2)}) async-start(bf16[16,80,128]{2,1,0:T(8,128)(2,1)} %far_kernel.1), calls=%async_computation.1 | async-start | bytes 655360 | tf_op jit(solution)/shard_map/all_to_all | solution.py:537
  56.8 4.2 %collective-permute-done.8.near_a = bf16[256,1152]{1,0:T(8,128)(2,1)} collective-permute-done((bf16[256,1152]{1,0:T(8,128)(2,1)}, bf16[256,1152]{1,0:T(8,128)(2,1)}, u32[]{:S(2)}, u32[]{:S(2)}) %collective-permute-start.8) | collective-permute-done | bytes 589856 | tf_op jit(solution)/shard_map/ppermute | solution.py:65
  60.9 3.7 %all-to-all-done.1.far_own = bf16[16,80,128]{2,1,0:T(8,128)(2,1)S(1)} async-done(((bf16[16,80,128]{2,1,0:T(8,128)(2,1)}), bf16[16,80,128]{2,1,0:T(8,128)(2,1)S(1)}, u32[]{:S(2)}, u32[]{:S(2)}) %all-to-all-start.1) | async-done | bytes 327712 | tf_op jit(solution)/shard_map/all_to_all | solution.py:537
  64.6 2.3 %collective-permute-start.10 = (bf16[16,80,128]{2,1,0:T(8,128)(2,1)S(1)}, bf16[16,80,128]{2,1,0:T(8,128)(2,1)S(1)}, u32[]{:S(2)}, u32[]{:S(2)}) collective-permute-start(bf16[16,80,128]{2,1,0:T(8,128)(2,1)S(1)} %all-to-all-done.1.far_own), channel_id=1, source_target_pairs={{0,1},{1,0},{2,3},{3,2},{4,5},{5,4},{6,7},{7,6},{8,9},{9,8},{10,11... | collective-permute-start | bytes 983048 | tf_op jit(solution)/shard_map/ppermute | solution.py:65
  66.9 1.2 %copy-done.1 = bf16[2,256,1024]{2,1,0:T(8,128)(2,1)S(1)} copy-done((bf16[2,256,1024]{2,1,0:T(8,128)(2,1)S(1)}, bf16[2,256,1024]{2,1,0:T(8,128)(2,1)}, u32[]{:S(2)}) %copy-start.1) | copy-done | bytes 1048600
  68.1 4.2 %near_odd.1.near_b = bf16[256,1152]{1,0:T(8,128)(2,1)S(1)} custom-call(s32[2,4]{1,0:T(2,128)} %offsets.15, bf16[512,2048]{1,0:T(8,128)(2,1)} %q.5, bf16[2,256,1024]{2,1,0:T(8,128)(2,1)S(1)} %copy-done.1, bf16[2,256,1024]{2,1,0:T(8,128)(2,1)} %collective-permute-done.9.kv_b), custom_call_target="tpu_custom_call" | custom-call | flops 1000 | bytes 1000 | tf_op jit(solution)/shard_map/near_odd/pallas_call | solution.py:483
  72.4 4.5 %merge_kernel.1 = bf16[512,2048]{1,0:T(8,128)(2,1)} custom-call(s32[2,4]{1,0:T(2,128)} %offsets.15, bf16[256,2176]{1,0:T(8,128)(2,1)S(1)} %get-tuple-element.21.mine, bf16[256,2176]{1,0:T(8,128)(2,1)S(1)} %collective-permute-done.6.back, bf16[256,1152]{1,0:T(8,128)(2,1)} %collective-permute-done.8.near_a, bf16[256,1152]{1,0:T(8,128)(2,1)S(1)} %near_odd.1.near_b, ...), custom_call_target="tpu_custom_call" | custom-call | flops 1000 | bytes 1000 | tf_op jit(solution)/shard_map/merge_kernel/pallas_call | solution.py:483
  (18 shorter events, 0.2 us)
Async XLA Ops:
  0.0 19.6 %collective-permute-start.3 = (bf16[512,2048]{1,0:T(8,128)(2,1)}, bf16[512,2048]{1,0:T(8,128)(2,1)}, u32[]{:S(2)}, u32[]{:S(2)}) collective-permute-start(bf16[512,2048]{1,0:T(8,128)(2,1)} %k_in.1), channel_id=1, source_target_pairs={{0,1},{1,0},{2,3},{3,2},{4,5},{5,4},{6,7},{7,6},{8,9},{9,8},{10,11... | collective-permute-start | bytes 6291464 | tf_op jit(solution)/shard_map/ppermute | solution.py:65
  0.7 18.9 %collective-permute-start.4 = (bf16[512,2048]{1,0:T(8,128)(2,1)}, bf16[512,2048]{1,0:T(8,128)(2,1)}, u32[]{:S(2)}, u32[]{:S(2)}) collective-permute-start(bf16[512,2048]{1,0:T(8,128)(2,1)} %v_in.1), channel_id=1, source_target_pairs={{0,1},{1,0},{2,3},{3,2},{4,5},{5,4},{6,7},{7,6},{8,9},{9,8},{10,11... | collective-permute-start | bytes 6291464 | tf_op jit(solution)/shard_map/ppermute | solution.py:65
  0.7 19.8 %collective-permute-start.2 = (bf16[512,2048]{1,0:T(8,128)(2,1)}, bf16[512,2048]{1,0:T(8,128)(2,1)}, u32[]{:S(2)}, u32[]{:S(2)}) collective-permute-start(bf16[512,2048]{1,0:T(8,128)(2,1)} %q.5), channel_id=1, source_target_pairs={{0,1},{1,0},{2,3},{3,2},{4,5},{5,4},{6,7},{7,6},{8,9},{9,8},{10,11... | collective-permute-start | bytes 6291464 | tf_op jit(solution)/shard_map/ppermute | solution.py:65
  3.5 6.1 %collective-permute-start = (bf16[4,3,64,512]{3,2,1,0:T(8,128)(2,1)S(1)}, bf16[4,3,64,512]{3,2,1,0:T(8,128)(2,1)S(1)}, u32[]{:S(2)}, u32[]{:S(2)}) collective-permute-start(bf16[4,3,64,512]{3,2,1,0:T(8,128)(2,1)S(1)} %get-tuple-element.17), channel_id=1, source_target_pairs={{0,1},{1,0},{2,3},{3,2},{4,5},{5,4},{6,7},{7,6},{8,9},{9,8},{10,11... | collective-permute-start | bytes 2359304 | tf_op jit(solution)/shard_map/ppermute | solution.py:65
  6.5 13.1 %collective-permute-start.5 = (bf16[256,1024]{1,0:T(8,128)(2,1)S(1)}, bf16[256,1024]{1,0:T(8,128)(2,1)S(1)}, u32[]{:S(2)}, u32[]{:S(2)}) collective-permute-start(bf16[256,1024]{1,0:T(8,128)(2,1)S(1)} %get-tuple-element.18.after_near), channel_id=1, source_target_pairs={{0,2},{1,3},{2,0},{3,1},{4,6},{5,7},{6,4},{7,5},{8,10},{9,11},{10,... | collective-permute-start | bytes 1572872 | tf_op jit(solution)/shard_map/ppermute | solution.py:65
  9.6 32.5 %collective-permute-start.1 = (bf16[2,256,1024]{2,1,0:T(8,128)(2,1)}, bf16[2,256,1024]{2,1,0:T(8,128)(2,1)S(1)}, u32[]{:S(2)}, u32[]{:S(2)}) collective-permute-start(bf16[2,256,1024]{2,1,0:T(8,128)(2,1)} %get-tuple-element.19), channel_id=1, source_target_pairs={{0,2},{1,3},{4,6},{5,7},{8,10},{9,11},{12,14},{13,15},{16,18},{17,... | collective-permute-start | bytes 3145736 | tf_op jit(solution)/shard_map/ppermute | solution.py:65
  12.7 29.3 %all-to-all-start = ((bf16[16,3,64,128]{3,2,1,0:T(8,128)(2,1)}), bf16[16,3,64,128]{3,2,1,0:T(8,128)(2,1)S(1)}, u32[]{:S(2)}, u32[]{:S(2)}) async-start(bf16[16,3,64,128]{3,2,1,0:T(8,128)(2,1)} %pack_second.1), calls=%async_computation | async-start | bytes 1572864 | tf_op jit(solution)/shard_map/all_to_all | solution.py:511
  20.4 12.2 %copy-start.2 = (bf16[256,1152]{1,0:T(8,128)(2,1)}, bf16[256,1152]{1,0:T(8,128)(2,1)S(1)}, u32[]{:S(2)}) copy-start(bf16[256,1152]{1,0:T(8,128)(2,1)S(1)} %near_even.1.after_near) | copy-start | bytes 1769476
  32.7 1.0 %copy-start.3 = (bf16[256,2176]{1,0:T(8,128)(2,1)}, bf16[256,2176]{1,0:T(8,128)(2,1)S(1)}, u32[]{:S(2)}) copy-start(bf16[256,2176]{1,0:T(8,128)(2,1)S(1)} %get-tuple-element.22) | copy-start | bytes 3342340
  42.0 1.3 %copy-start = (bf16[2,256,1024]{2,1,0:T(8,128)(2,1)}, bf16[2,256,1024]{2,1,0:T(8,128)(2,1)S(1)}, u32[]{:S(2)}) copy-start(bf16[2,256,1024]{2,1,0:T(8,128)(2,1)S(1)} %collective-permute-done.1.kv_a) | copy-start | bytes 3145732
  42.0 3.6 %collective-permute-start.7 = (bf16[16,3,64,128]{3,2,1,0:T(8,128)(2,1)S(1)}, bf16[16,3,64,128]{3,2,1,0:T(8,128)(2,1)S(1)}, u32[]{:S(2)}, u32[]{:S(2)}) collective-permute-start(bf16[16,3,64,128]{3,2,1,0:T(8,128)(2,1)S(1)} %all-to-all-done.mine), channel_id=1, source_target_pairs={{0,1},{1,0},{2,3},{3,2},{4,5},{5,4},{6,7},{7,6},{8,9},{9,8},{10,11... | collective-permute-start | bytes 2359304 | tf_op jit(solution)/shard_map/ppermute | solution.py:65
  43.4 28.9 %collective-permute-start.6 = (bf16[256,2176]{1,0:T(8,128)(2,1)}, bf16[256,2176]{1,0:T(8,128)(2,1)S(1)}, u32[]{:S(2)}, u32[]{:S(2)}) collective-permute-start(bf16[256,2176]{1,0:T(8,128)(2,1)} %copy-done.3), channel_id=1, source_target_pairs={{0,1},{1,0},{2,3},{3,2},{4,5},{5,4},{6,7},{7,6},{8,9},{9,8},{10,11... | collective-permute-start | bytes 3342344 | tf_op jit(solution)/shard_map/ppermute | solution.py:65
  44.4 22.5 %collective-permute-start.9 = (bf16[2,256,1024]{2,1,0:T(8,128)(2,1)}, bf16[2,256,1024]{2,1,0:T(8,128)(2,1)}, u32[]{:S(2)}, u32[]{:S(2)}) collective-permute-start(bf16[2,256,1024]{2,1,0:T(8,128)(2,1)} %copy-done), channel_id=1, source_target_pairs={{0,1},{1,0},{2,3},{3,2},{4,5},{5,4},{6,7},{7,6},{8,9},{9,8},{10,11... | collective-permute-start | bytes 3145736 | tf_op jit(solution)/shard_map/ppermute | solution.py:65
  44.4 16.6 %collective-permute-start.8 = (bf16[256,1152]{1,0:T(8,128)(2,1)}, bf16[256,1152]{1,0:T(8,128)(2,1)}, u32[]{:S(2)}, u32[]{:S(2)}) collective-permute-start(bf16[256,1152]{1,0:T(8,128)(2,1)} %copy-done.2), channel_id=1, source_target_pairs={{0,2},{1,3},{4,6},{5,7},{8,10},{9,11},{12,14},{13,15},{16,18},{17,... | collective-permute-start | bytes 1769480 | tf_op jit(solution)/shard_map/ppermute | solution.py:65
  50.0 14.6 %all-to-all-start.1 = ((bf16[16,80,128]{2,1,0:T(8,128)(2,1)}), bf16[16,80,128]{2,1,0:T(8,128)(2,1)S(1)}, u32[]{:S(2)}, u32[]{:S(2)}) async-start(bf16[16,80,128]{2,1,0:T(8,128)(2,1)} %far_kernel.1), calls=%async_computation.1 | async-start | bytes 655360 | tf_op jit(solution)/shard_map/all_to_all | solution.py:537
  64.6 7.7 %collective-permute-start.10 = (bf16[16,80,128]{2,1,0:T(8,128)(2,1)S(1)}, bf16[16,80,128]{2,1,0:T(8,128)(2,1)S(1)}, u32[]{:S(2)}, u32[]{:S(2)}) collective-permute-start(bf16[16,80,128]{2,1,0:T(8,128)(2,1)S(1)} %all-to-all-done.1.far_own), channel_id=1, source_target_pairs={{0,1},{1,0},{2,3},{3,2},{4,5},{5,4},{6,7},{7,6},{8,9},{9,8},{10,11... | collective-permute-start | bytes 983048 | tf_op jit(solution)/shard_map/ppermute | solution.py:65
  66.9 1.2 %copy-start.1 = (bf16[2,256,1024]{2,1,0:T(8,128)(2,1)S(1)}, bf16[2,256,1024]{2,1,0:T(8,128)(2,1)}, u32[]{:S(2)}) copy-start(bf16[2,256,1024]{2,1,0:T(8,128)(2,1)} %copy-done) | copy-start | bytes 3145732

commit v6 on v5

--- a/solution.py
+++ b/solution.py
@@ -104,7 +104,7 @@
         c.wait()
 
 
-def pack_far(offsets, q, k, v, send, keep, sems):
+def pack_first(offsets, q, k, v, near, send, keep, sems):
     here = Place(offsets)
     copies = []
     for g in range(GROUPS):
@@ -115,33 +115,27 @@
                 copies.append(
                     pltpu.make_async_copy(source.at[rows, group_cols(g)], target.at[g, t], sems.at[len(copies)])
                 )
-    run_copies(copies)
-
-
-def pack_near(offsets, q, k, v, near_q, near_kv, sems):
-    here = Place(offsets)
     for odd in (False, True):
 
         @pl.when(here.odd == odd)
         def _():
-            copies = []
+            nears = []
             for g in range(2):
                 for half in range(2):
                     rows = rows_at((here.near(g if odd else g + 2) + 2 * half) * BLK, BLK)
                     to = pl.ds(half * BLK, BLK)
                     for t, source in enumerate((q,) if odd else (k, v)):
-                        target = near_q if odd else near_kv.at[t]
-                        copies.append(
+                        nears.append(
                             pltpu.make_async_copy(
                                 source.at[rows, group_cols(g if odd else g + 2)],
-                                target.at[to, group_cols(g)],
-                                sems.at[len(copies)],
+                                near.at[t, to, group_cols(g)],
+                                sems.at[len(copies) + len(nears)],
                             )
                         )
-            run_copies(copies)
-
-
-def pack_second(offsets, kept, received, after_near, out):
+            run_copies(copies + nears)
+
+
+def pack_second(offsets, kept, received, out):
     here = Place(offsets)
     for g in range(GROUPS):
         mine = here.far_core(g) == here.core
@@ -207,7 +201,7 @@
         run_copies(copies)
         near_part(
             2 * GH,
-            lambda h: qr[:, head_cols(h)],
+            lambda h: qr[0, :, head_cols(h)],
             lambda h: [keys[:, head_cols(h)]],
             lambda h: [vals[:, head_cols(h)]],
             out,
@@ -331,7 +325,7 @@
 UNROLL = GH
 
 
-def local_kernel(offsets, q_in, qo_in, k_in, ko_in, v_in, vo_in, after_near, mine, away, q, qo, k, ko, v, vo, sems):
+def local_kernel(offsets, q_in, qo_in, k_in, ko_in, v_in, vo_in, mine, away, q, qo, k, ko, v, vo, sems):
     here = Place(offsets)
     keys, vals = {"own": k, "oth": ko}, {"own": v, "oth": vo}
     for target in (mine, away):
@@ -493,57 +487,57 @@
 
     qh, kh, vh = hbm(q), hbm(k), hbm(v)
     half_shape = shape(GROUPS, 3, HALF, GW)
-    far_send, far_keep = call(
-        pack_far, [half_shape] * 2, (qh, kh, vh), [HBM] * 3, sems=6 * GROUPS, out_places=[VMEM] * 2
+    near_x, far_send, far_keep = call(
+        pack_first,
+        [pltpu.HBM((2, NSEL, 2 * GW), BF), half_shape, half_shape],
+        (qh, kh, vh),
+        [HBM] * 3,
+        sems=6 * GROUPS + 8,
+        out_places=[HBM] + [VMEM] * 2,
     )
     far_recv = move(far_send, CORE)
-    near_q, near_kv = call(
-        pack_near,
-        [shape(NSEL, 2 * GW), shape(2, NSEL, 2 * GW)],
-        (qh, kh, vh),
-        [HBM] * 3,
-        sems=8,
-        out_places=[VMEM] * 2,
-    )
-    near_qr, near_kvr = move(near_q, PAIR), move(near_kv, TO_ODD)
+    near_r = move(near_x, PAIR)
     qo, ko, vo = hbm(move(q, CORE)), hbm(move(k, CORE)), hbm(move(v, CORE))
-    far_pack = call(pack_second, shape(HEADS, 3, HALF, HD), (far_keep, far_recv, near_q), [VMEM] * 2 + [ANY])
+    far_pack = call(pack_second, shape(HEADS, 3, HALF, HD), (far_keep, far_recv), [VMEM] * 2)
     far_mine = lax.all_to_all(far_pack, ("x", "y"), 0, 0, tiled=True)
 
-    near_out = call(
-        near_even,
-        shape(NSEL, 2 * GW + HD),
-        (near_qr, kh, ko, vh, vo),
-        [VMEM] + [HBM] * 4,
-        sems=16,
-        scratch=[pltpu.VMEM((ROWS, 2 * GW), BF)] * 2,
-    )
-    near_back = move(near_out, TO_ODD)
     rows = HEADS * HD
     mine, away = call(
         local_kernel,
-        [shape(NSEL, rows + HD)] * 2,
-        (qh, qo, kh, ko, vh, vo, near_out),
-        [HBM] * 6 + [ANY],
+        [shape(NSEL, rows + HD), pltpu.HBM((NSEL, rows + HD), BF)],
+        (qh, qo, kh, ko, vh, vo),
+        [HBM] * 6,
         scratch=[pltpu.VMEM((n, rows), BF) for n in (NSEL, NSEL, ROWS, ROWS, ROWS, ROWS)]
         + [pltpu.SemaphoreType.DMA((GROUPS, 6))],
         out_places=[VMEM] * 2,
         flops=10**10,
     )
     back = move(away, CORE)
-    far_mine, near_kvr, mine = lax.optimization_barrier((far_mine, near_kvr, mine))
+    far_mine, mine = lax.optimization_barrier((far_mine, mine))
     far_other = move(far_mine, CORE)
     far_out = call(far_kernel, shape(HEADS, HALF + 16, HD), (far_mine, far_other), [VMEM] * 2)
+    near_r, far_out = lax.optimization_barrier((near_r, far_out))
+    near_ro = move(near_r, CORE)
+    near_out = call(
+        near_even,
+        shape(NSEL, 2 * GW + HD),
+        (near_r, kh, ko, vh, vo),
+        [VMEM] + [HBM] * 4,
+        sems=16,
+        scratch=[pltpu.VMEM((ROWS, 2 * GW), BF)] * 2,
+    )
+    near_back = move(near_out, TO_ODD)
+    far_out, near_out = lax.optimization_barrier((far_out, near_out))
     far_back = lax.all_to_all(far_out, ("x", "y"), 0, 0, tiled=True)
     near_here = call(
         near_odd,
         shape(NSEL, 2 * GW + HD),
-        (qh, near_kvr, move(near_kvr, CORE)),
+        (qh, near_r, near_ro),
         [HBM] + [VMEM] * 2,
         sems=4,
         scratch=[pltpu.VMEM((NSEL, 2 * GW), BF)],
     )
-    far_back, near_back = lax.optimization_barrier((far_back, near_back))
+    far_back, near_back, near_here = lax.optimization_barrier((far_back, near_back, near_here))
     far_back_other = move(far_back, CORE)
 
     return call(

time: 77.6 us -> 97.5 us (1.26)
  the two profiles are of different devices: /device:TPU:97 before, /device:TPU:1 now
where the time goes in v6:
time: 97.5 us; the launch traced here: 96.8 us
  Pallas kernels  59.8 us (61%)
  starting transfers between devices  24.7 us (25%)
  waiting for transfers between devices  12 us (12%)
    pallas_call x7, Pallas kernels, call(): pl.pallas_call(kernel, out_shape=outs, in_specs=[SMEM] + places, out_spec...  59.8 us
    ppermute x10, starting transfers between devices, move(): return lax.ppermute(array, AXES, pairs)  9.24 us
    all_to_all x1, starting transfers between devices, device_part(): far_back = lax.all_to_all(far_out, ('x', 'y'), 0, 0, tiled=True)  8.67 us
    all_to_all x1, starting transfers between devices, device_part(): far_mine = lax.all_to_all(far_pack, ('x', 'y'), 0, 0, tiled=True)  6.84 us
    all_to_all x1, waiting for transfers between devices, device_part(): far_back = lax.all_to_all(far_out, ('x', 'y'), 0, 0, tiled=True)  6.62 us
    ppermute x10, waiting for transfers between devices, move(): return lax.ppermute(array, AXES, pairs)  5.36 us
  transfers between devices with their start and end apart: 12, of which 4 were waited for; matrix products, arithmetic and copies ran while one was open for 0% of the time, Pallas kernels for 59%

profile of v6, /device:TPU:1, one launch (start us, length us, event | category | flops | bytes accessed | tf_op | source)
XLA Modules:
  0.0 96.8 jit_solution(13496528003400416844)
XLA Ops:
  0.0 1.4 %collective-permute-start.1 = (bf16[512,2048]{1,0:T(8,128)(2,1)}, bf16[512,2048]{1,0:T(8,128)(2,1)}, u32[]{:S(2)}, u32[]{:S(2)}) collective-permute-start(bf16[512,2048]{1,0:T(8,128)(2,1)} %q.3), channel_id=1, source_target_pairs={{0,1},{1,0},{2,3},{3,2},{4,5},{5,4},{6,7},{7,6},{8,9},{9,8},{10,11... | collective-permute-start | bytes 6291464 | tf_op jit(solution)/shard_map/ppermute | solution.py:65
  1.4 0.0 collective-permute-start.2
  1.4 0.5 collective-permute-start.3
  1.9 33.9 %pack_first.1 = (bf16[2,256,1024]{2,1,0:T(8,128)(2,1)}, bf16[4,3,64,512]{3,2,1,0:T(8,128)(2,1)S(1)}, bf16[4,3,64,512]{3,2,1,0:T(8,128)(2,1)S(1)}) custom-call(s32[2,4]{1,0:T(2,128)} %offsets.13, bf16[512,2048]{1,0:T(8,128)(2,1)} %q.3, bf16[512,2048]{1,0:T(8,128)(2,1)} %k.3, bf16[512,2048]{1,0:T(8,128)(2,1)} %v.3), custom_call_target="tpu_custom_call" | custom-call | flops 1000 | bytes 1000 | tf_op jit(solution)/shard_map/pack_first/pallas_call | solution.py:477
  35.9 0.1 collective-permute-start
  35.9 0.1 collective-permute-start.5
  36.0 2.2 %collective-permute-done.received = bf16[4,3,64,512]{3,2,1,0:T(8,128)(2,1)S(1)} collective-permute-done((bf16[4,3,64,512]{3,2,1,0:T(8,128)(2,1)S(1)}, bf16[4,3,64,512]{3,2,1,0:T(8,128)(2,1)S(1)}, u32[]{:S(2)}, u32[]{:S(2)}) %collective-permute-start) | collective-permute-done | bytes 786464 | tf_op jit(solution)/shard_map/ppermute | solution.py:65
  38.2 1.8 %pack_second.1 = bf16[16,3,64,128]{3,2,1,0:T(8,128)(2,1)} custom-call(s32[2,4]{1,0:T(2,128)} %offsets.13, bf16[4,3,64,512]{3,2,1,0:T(8,128)(2,1)S(1)} %get-tuple-element.18.kept, bf16[4,3,64,512]{3,2,1,0:T(8,128)(2,1)S(1)} %collective-permute-done.received), custom_call_target="tpu_custom_call" | custom-call | flops 1000 | bytes 1000 | tf_op jit(solution)/shard_map/pack_second/pallas_call | solution.py:477
  40.0 6.8 %all-to-all-start = ((bf16[16,3,64,128]{3,2,1,0:T(8,128)(2,1)}), bf16[16,3,64,128]{3,2,1,0:T(8,128)(2,1)S(1)}, u32[]{:S(2)}, u32[]{:S(2)}) async-start(bf16[16,3,64,128]{3,2,1,0:T(8,128)(2,1)} %pack_second.1), calls=%async_computation | async-start | bytes 1572864 | tf_op jit(solution)/shard_map/all_to_all | solution.py:502
  46.9 0.0 collective-permute-done.1.qo_in
  46.9 13.2 %local_kernel.1 = (bf16[256,2176]{1,0:T(8,128)(2,1)S(1)}, bf16[256,2176]{1,0:T(8,128)(2,1)}) custom-call(s32[2,4]{1,0:T(2,128)} %offsets.13, bf16[512,2048]{1,0:T(8,128)(2,1)} %q.3, bf16[512,2048]{1,0:T(8,128)(2,1)} %collective-permute-done.1.qo_in, bf16[512,2048]{1,0:T(8,128)(2,1)} %k.3, bf16[512,2048]{1,0:T(8,128)(2,1)} %collective-permute-done.2.ko_in.ko, ...), custom_call_target="tpu_custom_call" | custom-call | flops 10000000000 | bytes 1000 | tf_op jit(solution)/shard_map/local_kernel/pallas_call | solution.py:477
  60.1 2.3 %collective-permute-start.6 = (bf16[16,3,64,128]{3,2,1,0:T(8,128)(2,1)S(1)}, bf16[16,3,64,128]{3,2,1,0:T(8,128)(2,1)S(1)}, u32[]{:S(2)}, u32[]{:S(2)}) collective-permute-start(bf16[16,3,64,128]{3,2,1,0:T(8,128)(2,1)S(1)} %all-to-all-done.mine), channel_id=1, source_target_pairs={{0,1},{1,0},{2,3},{3,2},{4,5},{5,4},{6,7},{7,6},{8,9},{9,8},{10,11... | collective-permute-start | bytes 2359304 | tf_op jit(solution)/shard_map/ppermute | solution.py:65
  62.4 1.9 %collective-permute-done.6.other = bf16[16,3,64,128]{3,2,1,0:T(8,128)(2,1)S(1)} collective-permute-done((bf16[16,3,64,128]{3,2,1,0:T(8,128)(2,1)S(1)}, bf16[16,3,64,128]{3,2,1,0:T(8,128)(2,1)S(1)}, u32[]{:S(2)}, u32[]{:S(2)}) %collective-permute-start.6) | collective-permute-done | bytes 786464 | tf_op jit(solution)/shard_map/ppermute | solution.py:65
  64.3 1.4 %far_kernel.1 = bf16[16,80,128]{2,1,0:T(8,128)(2,1)} custom-call(s32[2,4]{1,0:T(2,128)} %offsets.13, bf16[16,3,64,128]{3,2,1,0:T(8,128)(2,1)S(1)} %all-to-all-done.mine, bf16[16,3,64,128]{3,2,1,0:T(8,128)(2,1)S(1)} %collective-permute-done.6.other), custom_call_target="tpu_custom_call" | custom-call | flops 1000 | bytes 1000 | tf_op jit(solution)/shard_map/far_kernel/pallas_call | solution.py:477
  65.8 0.4 collective-permute-start.8
  66.2 0.1 collective-permute-start.4
  66.3 5.3 %near_even.1 = bf16[256,1152]{1,0:T(8,128)(2,1)} custom-call(s32[2,4]{1,0:T(2,128)} %offsets.13, bf16[2,256,1024]{2,1,0:T(8,128)(2,1)S(1)} %collective-permute-done.5.qr.kv_a, bf16[512,2048]{1,0:T(8,128)(2,1)} %k.3, bf16[512,2048]{1,0:T(8,128)(2,1)} %collective-permute-done.2.ko_in.ko, bf16[512,2048]{1,0:T(8,128)(2,1)} %v.3, ...), custom_call_target="tpu_custom_call" | custom-call | flops 1000 | bytes 1000 | tf_op jit(solution)/shard_map/near_even/pallas_call | solution.py:477
  71.6 2.1 %collective-permute-start.7 = (bf16[256,1152]{1,0:T(8,128)(2,1)}, bf16[256,1152]{1,0:T(8,128)(2,1)}, u32[]{:S(2)}, u32[]{:S(2)}) collective-permute-start(bf16[256,1152]{1,0:T(8,128)(2,1)} %near_even.1), channel_id=1, source_target_pairs={{0,2},{1,3},{4,6},{5,7},{8,10},{9,11},{12,14},{13,15},{16,18},{17,... | collective-permute-start | bytes 1769480 | tf_op jit(solution)/shard_map/ppermute | solution.py:65
  73.7 8.7 %all-to-all-start.1 = ((bf16[16,80,128]{2,1,0:T(8,128)(2,1)}), bf16[16,80,128]{2,1,0:T(8,128)(2,1)S(1)}, u32[]{:S(2)}, u32[]{:S(2)}) async-start(bf16[16,80,128]{2,1,0:T(8,128)(2,1)} %far_kernel.1), calls=%async_computation.1 | async-start | bytes 655360 | tf_op jit(solution)/shard_map/all_to_all | solution.py:531
  82.4 1.3 %near_odd.1.near_b = bf16[256,1152]{1,0:T(8,128)(2,1)S(1)} custom-call(s32[2,4]{1,0:T(2,128)} %offsets.13, bf16[512,2048]{1,0:T(8,128)(2,1)} %q.3, bf16[2,256,1024]{2,1,0:T(8,128)(2,1)S(1)} %collective-permute-done.5.qr.kv_a, bf16[2,256,1024]{2,1,0:T(8,128)(2,1)} %collective-permute-done.8.kv_b), custom_call_target="tpu_custom_call" | custom-call | flops 1000 | bytes 1000 | tf_op jit(solution)/shard_map/near_odd/pallas_call | solution.py:477
  83.7 6.6 %all-to-all-done.1.far_own = bf16[16,80,128]{2,1,0:T(8,128)(2,1)S(1)} async-done(((bf16[16,80,128]{2,1,0:T(8,128)(2,1)}), bf16[16,80,128]{2,1,0:T(8,128)(2,1)S(1)}, u32[]{:S(2)}, u32[]{:S(2)}) %all-to-all-start.1) | async-done | bytes 327712 | tf_op jit(solution)/shard_map/all_to_all | solution.py:531
  90.3 2.2 %collective-permute-start.9 = (bf16[16,80,128]{2,1,0:T(8,128)(2,1)S(1)}, bf16[16,80,128]{2,1,0:T(8,128)(2,1)S(1)}, u32[]{:S(2)}, u32[]{:S(2)}) collective-permute-start(bf16[16,80,128]{2,1,0:T(8,128)(2,1)S(1)} %all-to-all-done.1.far_own), channel_id=1, source_target_pairs={{0,1},{1,0},{2,3},{3,2},{4,5},{5,4},{6,7},{7,6},{8,9},{9,8},{10,11... | collective-permute-start | bytes 983048 | tf_op jit(solution)/shard_map/ppermute | solution.py:65
  92.5 1.3 %collective-permute-done.9.far_oth = bf16[16,80,128]{2,1,0:T(8,128)(2,1)S(1)} collective-permute-done((bf16[16,80,128]{2,1,0:T(8,128)(2,1)S(1)}, bf16[16,80,128]{2,1,0:T(8,128)(2,1)S(1)}, u32[]{:S(2)}, u32[]{:S(2)}) %collective-permute-start.9) | collective-permute-done | bytes 327712 | tf_op jit(solution)/shard_map/ppermute | solution.py:65
  93.7 2.9 %merge_kernel.1 = bf16[512,2048]{1,0:T(8,128)(2,1)} custom-call(s32[2,4]{1,0:T(2,128)} %offsets.13, bf16[256,2176]{1,0:T(8,128)(2,1)S(1)} %get-tuple-element.21.mine, bf16[256,2176]{1,0:T(8,128)(2,1)} %collective-permute-done.4.back, bf16[256,1152]{1,0:T(8,128)(2,1)} %collective-permute-done.7.near_a, bf16[256,1152]{1,0:T(8,128)(2,1)S(1)} %near_odd.1.near_b, ...), custom_call_target="tpu_custom_call" | custom-call | flops 1000 | bytes 1000 | tf_op jit(solution)/shard_map/merge_kernel/pallas_call | solution.py:477
  (7 shorter events, 0.0 us)
Async XLA Ops:
  0.0 46.9 %collective-permute-start.1 = (bf16[512,2048]{1,0:T(8,128)(2,1)}, bf16[512,2048]{1,0:T(8,128)(2,1)}, u32[]{:S(2)}, u32[]{:S(2)}) collective-permute-start(bf16[512,2048]{1,0:T(8,128)(2,1)} %q.3), channel_id=1, source_target_pairs={{0,1},{1,0},{2,3},{3,2},{4,5},{5,4},{6,7},{7,6},{8,9},{9,8},{10,11... | collective-permute-start | bytes 6291464 | tf_op jit(solution)/shard_map/ppermute | solution.py:65
  1.4 45.4 %collective-permute-start.2 = (bf16[512,2048]{1,0:T(8,128)(2,1)}, bf16[512,2048]{1,0:T(8,128)(2,1)}, u32[]{:S(2)}, u32[]{:S(2)}) collective-permute-start(bf16[512,2048]{1,0:T(8,128)(2,1)} %k.3), channel_id=1, source_target_pairs={{0,1},{1,0},{2,3},{3,2},{4,5},{5,4},{6,7},{7,6},{8,9},{9,8},{10,11... | collective-permute-start | bytes 6291464 | tf_op jit(solution)/shard_map/ppermute | solution.py:65
  1.4 45.5 %collective-permute-start.3 = (bf16[512,2048]{1,0:T(8,128)(2,1)}, bf16[512,2048]{1,0:T(8,128)(2,1)}, u32[]{:S(2)}, u32[]{:S(2)}) collective-permute-start(bf16[512,2048]{1,0:T(8,128)(2,1)} %v.3), channel_id=1, source_target_pairs={{0,1},{1,0},{2,3},{3,2},{4,5},{5,4},{6,7},{7,6},{8,9},{9,8},{10,11... | collective-permute-start | bytes 6291464 | tf_op jit(solution)/shard_map/ppermute | solution.py:65
  35.9 2.4 %collective-permute-start = (bf16[4,3,64,512]{3,2,1,0:T(8,128)(2,1)S(1)}, bf16[4,3,64,512]{3,2,1,0:T(8,128)(2,1)S(1)}, u32[]{:S(2)}, u32[]{:S(2)}) collective-permute-start(bf16[4,3,64,512]{3,2,1,0:T(8,128)(2,1)S(1)} %get-tuple-element.19), channel_id=1, source_target_pairs={{0,1},{1,0},{2,3},{3,2},{4,5},{5,4},{6,7},{7,6},{8,9},{9,8},{10,11... | collective-permute-start | bytes 2359304 | tf_op jit(solution)/shard_map/ppermute | solution.py:65
  35.9 29.8 %collective-permute-start.5 = (bf16[2,256,1024]{2,1,0:T(8,128)(2,1)}, bf16[2,256,1024]{2,1,0:T(8,128)(2,1)S(1)}, u32[]{:S(2)}, u32[]{:S(2)}) collective-permute-start(bf16[2,256,1024]{2,1,0:T(8,128)(2,1)} %get-tuple-element.23), channel_id=1, source_target_pairs={{0,2},{1,3},{2,0},{3,1},{4,6},{5,7},{6,4},{7,5},{8,10},{9,11},{10,... | collective-permute-start | bytes 3145736 | tf_op jit(solution)/shard_map/ppermute | solution.py:65
  40.0 20.1 %all-to-all-start = ((bf16[16,3,64,128]{3,2,1,0:T(8,128)(2,1)}), bf16[16,3,64,128]{3,2,1,0:T(8,128)(2,1)S(1)}, u32[]{:S(2)}, u32[]{:S(2)}) async-start(bf16[16,3,64,128]{3,2,1,0:T(8,128)(2,1)} %pack_second.1), calls=%async_computation | async-start | bytes 1572864 | tf_op jit(solution)/shard_map/all_to_all | solution.py:502
  60.1 4.2 %collective-permute-start.6 = (bf16[16,3,64,128]{3,2,1,0:T(8,128)(2,1)S(1)}, bf16[16,3,64,128]{3,2,1,0:T(8,128)(2,1)S(1)}, u32[]{:S(2)}, u32[]{:S(2)}) collective-permute-start(bf16[16,3,64,128]{3,2,1,0:T(8,128)(2,1)S(1)} %all-to-all-done.mine), channel_id=1, source_target_pairs={{0,1},{1,0},{2,3},{3,2},{4,5},{5,4},{6,7},{7,6},{8,9},{9,8},{10,11... | collective-permute-start | bytes 2359304 | tf_op jit(solution)/shard_map/ppermute | solution.py:65
  65.8 16.6 %collective-permute-start.8 = (bf16[2,256,1024]{2,1,0:T(8,128)(2,1)S(1)}, bf16[2,256,1024]{2,1,0:T(8,128)(2,1)}, u32[]{:S(2)}, u32[]{:S(2)}) collective-permute-start(bf16[2,256,1024]{2,1,0:T(8,128)(2,1)S(1)} %collective-permute-done.5.qr.kv_a), channel_id=1, source_target_pairs={{0,1},{1,0},{2,3},{3,2},{4,5},{5,4},{6,7},{7,6},{8,9},{9,8},{10,11... | collective-permute-start | bytes 3145736 | tf_op jit(solution)/shard_map/ppermute | solution.py:65
  66.2 26.3 %collective-permute-start.4 = (bf16[256,2176]{1,0:T(8,128)(2,1)}, bf16[256,2176]{1,0:T(8,128)(2,1)}, u32[]{:S(2)}, u32[]{:S(2)}) collective-permute-start(bf16[256,2176]{1,0:T(8,128)(2,1)} %get-tuple-element.22), channel_id=1, source_target_pairs={{0,1},{1,0},{2,3},{3,2},{4,5},{5,4},{6,7},{7,6},{8,9},{9,8},{10,11... | collective-permute-start | bytes 3342344 | tf_op jit(solution)/shard_map/ppermute | solution.py:65
  71.6 18.7 %collective-permute-start.7 = (bf16[256,1152]{1,0:T(8,128)(2,1)}, bf16[256,1152]{1,0:T(8,128)(2,1)}, u32[]{:S(2)}, u32[]{:S(2)}) collective-permute-start(bf16[256,1152]{1,0:T(8,128)(2,1)} %near_even.1), channel_id=1, source_target_pairs={{0,2},{1,3},{4,6},{5,7},{8,10},{9,11},{12,14},{13,15},{16,18},{17,... | collective-permute-start | bytes 1769480 | tf_op jit(solution)/shard_map/ppermute | solution.py:65
  73.7 16.6 %all-to-all-start.1 = ((bf16[16,80,128]{2,1,0:T(8,128)(2,1)}), bf16[16,80,128]{2,1,0:T(8,128)(2,1)S(1)}, u32[]{:S(2)}, u32[]{:S(2)}) async-start(bf16[16,80,128]{2,1,0:T(8,128)(2,1)} %far_kernel.1), calls=%async_computation.1 | async-start | bytes 655360 | tf_op jit(solution)/shard_map/all_to_all | solution.py:531
  90.3 3.4 %collective-permute-start.9 = (bf16[16,80,128]{2,1,0:T(8,128)(2,1)S(1)}, bf16[16,80,128]{2,1,0:T(8,128)(2,1)S(1)}, u32[]{:S(2)}, u32[]{:S(2)}) collective-permute-start(bf16[16,80,128]{2,1,0:T(8,128)(2,1)S(1)} %all-to-all-done.1.far_own), channel_id=1, source_target_pairs={{0,1},{1,0},{2,3},{3,2},{4,5},{5,4},{6,7},{7,6},{8,9},{9,8},{10,11... | collective-permute-start | bytes 983048 | tf_op jit(solution)/shard_map/ppermute | solution.py:65

commit v7 on v6

--- a/solution.py
+++ b/solution.py
@@ -489,11 +489,11 @@
     half_shape = shape(GROUPS, 3, HALF, GW)
     near_x, far_send, far_keep = call(
         pack_first,
-        [pltpu.HBM((2, NSEL, 2 * GW), BF), half_shape, half_shape],
+        [shape(2, NSEL, 2 * GW), half_shape, half_shape],
         (qh, kh, vh),
         [HBM] * 3,
         sems=6 * GROUPS + 8,
-        out_places=[HBM] + [VMEM] * 2,
+        out_places=[VMEM] * 3,
     )
     far_recv = move(far_send, CORE)
     near_r = move(near_x, PAIR)
@@ -513,11 +513,8 @@
         flops=10**10,
     )
     back = move(away, CORE)
-    far_mine, mine = lax.optimization_barrier((far_mine, mine))
-    far_other = move(far_mine, CORE)
-    far_out = call(far_kernel, shape(HEADS, HALF + 16, HD), (far_mine, far_other), [VMEM] * 2)
-    near_r, far_out = lax.optimization_barrier((near_r, far_out))
-    near_ro = move(near_r, CORE)
+    near_r, far_mine, mine = lax.optimization_barrier((near_r, far_mine, mine))
+    far_other, near_ro = move(far_mine, CORE), move(near_r, CORE)
     near_out = call(
         near_even,
         shape(NSEL, 2 * GW + HD),
@@ -527,7 +524,8 @@
         scratch=[pltpu.VMEM((ROWS, 2 * GW), BF)] * 2,
     )
     near_back = move(near_out, TO_ODD)
-    far_out, near_out = lax.optimization_barrier((far_out, near_out))
+    far_other, near_out = lax.optimization_barrier((far_other, near_out))
+    far_out = call(far_kernel, shape(HEADS, HALF + 16, HD), (far_mine, far_other), [VMEM] * 2)
     far_back = lax.all_to_all(far_out, ("x", "y"), 0, 0, tiled=True)
     near_here = call(
         near_odd,

time: 97.5 us -> 67 us (0.69)
  the two profiles are of different devices: /device:TPU:1 before, /device:TPU:65 now
where the time goes in v7:
time: 67 us; the launch traced here: 66.2 us
  Pallas kernels  32.3 us (48%)
  starting transfers between devices  22 us (33%)
  waiting for transfers between devices  11.6 us (17%)
    pallas_call x7, Pallas kernels, call(): pl.pallas_call(kernel, out_shape=outs, in_specs=[SMEM] + places, out_spec...  32.3 us
    ppermute x10, starting transfers between devices, move(): return lax.ppermute(array, AXES, pairs)  9.25 us
    all_to_all x1, starting transfers between devices, device_part(): far_mine = lax.all_to_all(far_pack, ('x', 'y'), 0, 0, tiled=True)  6.75 us
    all_to_all x1, waiting for transfers between devices, device_part(): far_back = lax.all_to_all(far_out, ('x', 'y'), 0, 0, tiled=True)  6.14 us
    all_to_all x1, starting transfers between devices, device_part(): far_back = lax.all_to_all(far_out, ('x', 'y'), 0, 0, tiled=True)  6 us
    ppermute x10, waiting for transfers between devices, move(): return lax.ppermute(array, AXES, pairs)  5.46 us
  transfers between devices with their start and end apart: 12, of which 4 were waited for; matrix products, arithmetic and copies ran while one was open for 0% of the time, Pallas kernels for 44%

profile of v7, /device:TPU:65, one launch (start us, length us, event | category | flops | bytes accessed | tf_op | source)
XLA Modules:
  0.0 66.2 jit_solution(4287591105637212696)
XLA Ops:
  0.0 0.7 %collective-permute-start.2 = (bf16[512,2048]{1,0:T(8,128)(2,1)}, bf16[512,2048]{1,0:T(8,128)(2,1)}, u32[]{:S(2)}, u32[]{:S(2)}) collective-permute-start(bf16[512,2048]{1,0:T(8,128)(2,1)} %q.3), channel_id=1, source_target_pairs={{0,1},{1,0},{2,3},{3,2},{4,5},{5,4},{6,7},{7,6},{8,9},{9,8},{10,11... | collective-permute-start | bytes 6291464 | tf_op jit(solution)/shard_map/ppermute | solution.py:65
  0.7 0.0 collective-permute-start.3
  0.7 0.5 collective-permute-start.4
  1.2 3.8 %pack_first.1 = (bf16[2,256,1024]{2,1,0:T(8,128)(2,1)}, bf16[4,3,64,512]{3,2,1,0:T(8,128)(2,1)S(1)}, bf16[4,3,64,512]{3,2,1,0:T(8,128)(2,1)S(1)}) custom-call(s32[2,4]{1,0:T(2,128)} %offsets.13, bf16[512,2048]{1,0:T(8,128)(2,1)} %q.3, bf16[512,2048]{1,0:T(8,128)(2,1)} %k.3, bf16[512,2048]{1,0:T(8,128)(2,1)} %v.3), custom_call_target="tpu_custom_call" | custom-call | flops 1000 | bytes 1000 | tf_op jit(solution)/shard_map/pack_first/pallas_call | solution.py:477
  5.0 0.1 collective-permute-start.1
  5.1 1.3 %collective-permute-start = (bf16[2,256,1024]{2,1,0:T(8,128)(2,1)}, bf16[2,256,1024]{2,1,0:T(8,128)(2,1)S(1)}, u32[]{:S(2)}, u32[]{:S(2)}) collective-permute-start(bf16[2,256,1024]{2,1,0:T(8,128)(2,1)} %get-tuple-element.17), channel_id=1, source_target_pairs={{0,2},{1,3},{2,0},{3,1},{4,6},{5,7},{6,4},{7,5},{8,10},{9,11},{10,... | collective-permute-start | bytes 3145736 | tf_op jit(solution)/shard_map/ppermute | solution.py:65
  6.3 3.4 %collective-permute-done.1.received = bf16[4,3,64,512]{3,2,1,0:T(8,128)(2,1)S(1)} collective-permute-done((bf16[4,3,64,512]{3,2,1,0:T(8,128)(2,1)S(1)}, bf16[4,3,64,512]{3,2,1,0:T(8,128)(2,1)S(1)}, u32[]{:S(2)}, u32[]{:S(2)}) %collective-permute-start.1) | collective-permute-done | bytes 786464 | tf_op jit(solution)/shard_map/ppermute | solution.py:65
  9.7 1.8 %pack_second.1 = bf16[16,3,64,128]{3,2,1,0:T(8,128)(2,1)} custom-call(s32[2,4]{1,0:T(2,128)} %offsets.13, bf16[4,3,64,512]{3,2,1,0:T(8,128)(2,1)S(1)} %get-tuple-element.18.kept, bf16[4,3,64,512]{3,2,1,0:T(8,128)(2,1)S(1)} %collective-permute-done.1.received), custom_call_target="tpu_custom_call" | custom-call | flops 1000 | bytes 1000 | tf_op jit(solution)/shard_map/pack_second/pallas_call | solution.py:477
  11.5 6.8 %all-to-all-start = ((bf16[16,3,64,128]{3,2,1,0:T(8,128)(2,1)}), bf16[16,3,64,128]{3,2,1,0:T(8,128)(2,1)S(1)}, u32[]{:S(2)}, u32[]{:S(2)}) async-start(bf16[16,3,64,128]{3,2,1,0:T(8,128)(2,1)} %pack_second.1), calls=%async_computation | async-start | bytes 1572864 | tf_op jit(solution)/shard_map/all_to_all | solution.py:502
  18.3 0.0 collective-permute-done.4.vo_in.vo
  18.3 13.2 %local_kernel.1 = (bf16[256,2176]{1,0:T(8,128)(2,1)S(1)}, bf16[256,2176]{1,0:T(8,128)(2,1)}) custom-call(s32[2,4]{1,0:T(2,128)} %offsets.13, bf16[512,2048]{1,0:T(8,128)(2,1)} %q.3, bf16[512,2048]{1,0:T(8,128)(2,1)} %collective-permute-done.2.qo_in, bf16[512,2048]{1,0:T(8,128)(2,1)} %k.3, bf16[512,2048]{1,0:T(8,128)(2,1)} %collective-permute-done.3.ko_in.ko, ...), custom_call_target="tpu_custom_call" | custom-call | flops 10000000000 | bytes 1000 | tf_op jit(solution)/shard_map/local_kernel/pallas_call | solution.py:477
  31.5 2.2 %collective-permute-start.6 = (bf16[16,3,64,128]{3,2,1,0:T(8,128)(2,1)S(1)}, bf16[16,3,64,128]{3,2,1,0:T(8,128)(2,1)S(1)}, u32[]{:S(2)}, u32[]{:S(2)}) collective-permute-start(bf16[16,3,64,128]{3,2,1,0:T(8,128)(2,1)S(1)} %all-to-all-done.mine), channel_id=1, source_target_pairs={{0,1},{1,0},{2,3},{3,2},{4,5},{5,4},{6,7},{7,6},{8,9},{9,8},{10,11... | collective-permute-start | bytes 2359304 | tf_op jit(solution)/shard_map/ppermute | solution.py:65
  33.8 0.0 collective-permute-start.8
  33.8 0.5 collective-permute-start.5
  34.3 5.1 %near_even.1 = bf16[256,1152]{1,0:T(8,128)(2,1)} custom-call(s32[2,4]{1,0:T(2,128)} %offsets.13, bf16[2,256,1024]{2,1,0:T(8,128)(2,1)S(1)} %collective-permute-done.qr.kv_a, bf16[512,2048]{1,0:T(8,128)(2,1)} %k.3, bf16[512,2048]{1,0:T(8,128)(2,1)} %collective-permute-done.3.ko_in.ko, bf16[512,2048]{1,0:T(8,128)(2,1)} %v.3, ...), custom_call_target="tpu_custom_call" | custom-call | flops 1000 | bytes 1000 | tf_op jit(solution)/shard_map/near_even/pallas_call | solution.py:477
  39.4 2.1 %collective-permute-start.7 = (bf16[256,1152]{1,0:T(8,128)(2,1)}, bf16[256,1152]{1,0:T(8,128)(2,1)}, u32[]{:S(2)}, u32[]{:S(2)}) collective-permute-start(bf16[256,1152]{1,0:T(8,128)(2,1)} %near_even.1), channel_id=1, source_target_pairs={{0,2},{1,3},{4,6},{5,7},{8,10},{9,11},{12,14},{13,15},{16,18},{17,... | collective-permute-start | bytes 1769480 | tf_op jit(solution)/shard_map/ppermute | solution.py:65
  41.5 4.3 %far_kernel.1 = bf16[16,80,128]{2,1,0:T(8,128)(2,1)} custom-call(s32[2,4]{1,0:T(2,128)} %offsets.13, bf16[16,3,64,128]{3,2,1,0:T(8,128)(2,1)S(1)} %all-to-all-done.mine, bf16[16,3,64,128]{3,2,1,0:T(8,128)(2,1)S(1)} %collective-permute-done.6.other), custom_call_target="tpu_custom_call" | custom-call | flops 1000 | bytes 1000 | tf_op jit(solution)/shard_map/far_kernel/pallas_call | solution.py:477
  45.8 6.0 %all-to-all-start.1 = ((bf16[16,80,128]{2,1,0:T(8,128)(2,1)}), bf16[16,80,128]{2,1,0:T(8,128)(2,1)S(1)}, u32[]{:S(2)}, u32[]{:S(2)}) async-start(bf16[16,80,128]{2,1,0:T(8,128)(2,1)} %far_kernel.1), calls=%async_computation.1 | async-start | bytes 655360 | tf_op jit(solution)/shard_map/all_to_all | solution.py:529
  51.8 1.3 %near_odd.1.near_b = bf16[256,1152]{1,0:T(8,128)(2,1)S(1)} custom-call(s32[2,4]{1,0:T(2,128)} %offsets.13, bf16[512,2048]{1,0:T(8,128)(2,1)} %q.3, bf16[2,256,1024]{2,1,0:T(8,128)(2,1)S(1)} %collective-permute-done.qr.kv_a, bf16[2,256,1024]{2,1,0:T(8,128)(2,1)} %collective-permute-done.8.kv_b), custom_call_target="tpu_custom_call" | custom-call | flops 1000 | bytes 1000 | tf_op jit(solution)/shard_map/near_odd/pallas_call | solution.py:477
  53.1 0.8 %collective-permute-done.7.near_a = bf16[256,1152]{1,0:T(8,128)(2,1)} collective-permute-done((bf16[256,1152]{1,0:T(8,128)(2,1)}, bf16[256,1152]{1,0:T(8,128)(2,1)}, u32[]{:S(2)}, u32[]{:S(2)}) %collective-permute-start.7) | collective-permute-done | bytes 589856 | tf_op jit(solution)/shard_map/ppermute | solution.py:65
  53.9 6.1 %all-to-all-done.1.far_own = bf16[16,80,128]{2,1,0:T(8,128)(2,1)S(1)} async-done(((bf16[16,80,128]{2,1,0:T(8,128)(2,1)}), bf16[16,80,128]{2,1,0:T(8,128)(2,1)S(1)}, u32[]{:S(2)}, u32[]{:S(2)}) %all-to-all-start.1) | async-done | bytes 327712 | tf_op jit(solution)/shard_map/all_to_all | solution.py:529
  60.1 1.8 %collective-permute-start.9 = (bf16[16,80,128]{2,1,0:T(8,128)(2,1)S(1)}, bf16[16,80,128]{2,1,0:T(8,128)(2,1)S(1)}, u32[]{:S(2)}, u32[]{:S(2)}) collective-permute-start(bf16[16,80,128]{2,1,0:T(8,128)(2,1)S(1)} %all-to-all-done.1.far_own), channel_id=1, source_target_pairs={{0,1},{1,0},{2,3},{3,2},{4,5},{5,4},{6,7},{7,6},{8,9},{9,8},{10,11... | collective-permute-start | bytes 983048 | tf_op jit(solution)/shard_map/ppermute | solution.py:65
  61.9 1.3 %collective-permute-done.9.far_oth = bf16[16,80,128]{2,1,0:T(8,128)(2,1)S(1)} collective-permute-done((bf16[16,80,128]{2,1,0:T(8,128)(2,1)S(1)}, bf16[16,80,128]{2,1,0:T(8,128)(2,1)S(1)}, u32[]{:S(2)}, u32[]{:S(2)}) %collective-permute-start.9) | collective-permute-done | bytes 327712 | tf_op jit(solution)/shard_map/ppermute | solution.py:65
  63.2 2.9 %merge_kernel.1 = bf16[512,2048]{1,0:T(8,128)(2,1)} custom-call(s32[2,4]{1,0:T(2,128)} %offsets.13, bf16[256,2176]{1,0:T(8,128)(2,1)S(1)} %get-tuple-element.21.mine, bf16[256,2176]{1,0:T(8,128)(2,1)} %collective-permute-done.5.back, bf16[256,1152]{1,0:T(8,128)(2,1)} %collective-permute-done.7.near_a, bf16[256,1152]{1,0:T(8,128)(2,1)S(1)} %near_odd.1.near_b, ...), custom_call_target="tpu_custom_call" | custom-call | flops 1000 | bytes 1000 | tf_op jit(solution)/shard_map/merge_kernel/pallas_call | solution.py:477
  (7 shorter events, 0.0 us)
Async XLA Ops:
  0.0 18.3 %collective-permute-start.2 = (bf16[512,2048]{1,0:T(8,128)(2,1)}, bf16[512,2048]{1,0:T(8,128)(2,1)}, u32[]{:S(2)}, u32[]{:S(2)}) collective-permute-start(bf16[512,2048]{1,0:T(8,128)(2,1)} %q.3), channel_id=1, source_target_pairs={{0,1},{1,0},{2,3},{3,2},{4,5},{5,4},{6,7},{7,6},{8,9},{9,8},{10,11... | collective-permute-start | bytes 6291464 | tf_op jit(solution)/shard_map/ppermute | solution.py:65
  0.7 17.6 %collective-permute-start.3 = (bf16[512,2048]{1,0:T(8,128)(2,1)}, bf16[512,2048]{1,0:T(8,128)(2,1)}, u32[]{:S(2)}, u32[]{:S(2)}) collective-permute-start(bf16[512,2048]{1,0:T(8,128)(2,1)} %k.3), channel_id=1, source_target_pairs={{0,1},{1,0},{2,3},{3,2},{4,5},{5,4},{6,7},{7,6},{8,9},{9,8},{10,11... | collective-permute-start | bytes 6291464 | tf_op jit(solution)/shard_map/ppermute | solution.py:65
  0.7 17.6 %collective-permute-start.4 = (bf16[512,2048]{1,0:T(8,128)(2,1)}, bf16[512,2048]{1,0:T(8,128)(2,1)}, u32[]{:S(2)}, u32[]{:S(2)}) collective-permute-start(bf16[512,2048]{1,0:T(8,128)(2,1)} %v.3), channel_id=1, source_target_pairs={{0,1},{1,0},{2,3},{3,2},{4,5},{5,4},{6,7},{7,6},{8,9},{9,8},{10,11... | collective-permute-start | bytes 6291464 | tf_op jit(solution)/shard_map/ppermute | solution.py:65
  5.0 4.7 %collective-permute-start.1 = (bf16[4,3,64,512]{3,2,1,0:T(8,128)(2,1)S(1)}, bf16[4,3,64,512]{3,2,1,0:T(8,128)(2,1)S(1)}, u32[]{:S(2)}, u32[]{:S(2)}) collective-permute-start(bf16[4,3,64,512]{3,2,1,0:T(8,128)(2,1)S(1)} %get-tuple-element.19), channel_id=1, source_target_pairs={{0,1},{1,0},{2,3},{3,2},{4,5},{5,4},{6,7},{7,6},{8,9},{9,8},{10,11... | collective-permute-start | bytes 2359304 | tf_op jit(solution)/shard_map/ppermute | solution.py:65
  5.1 26.4 %collective-permute-start = (bf16[2,256,1024]{2,1,0:T(8,128)(2,1)}, bf16[2,256,1024]{2,1,0:T(8,128)(2,1)S(1)}, u32[]{:S(2)}, u32[]{:S(2)}) collective-permute-start(bf16[2,256,1024]{2,1,0:T(8,128)(2,1)} %get-tuple-element.17), channel_id=1, source_target_pairs={{0,2},{1,3},{2,0},{3,1},{4,6},{5,7},{6,4},{7,5},{8,10},{9,11},{10,... | collective-permute-start | bytes 3145736 | tf_op jit(solution)/shard_map/ppermute | solution.py:65
  11.5 20.0 %all-to-all-start = ((bf16[16,3,64,128]{3,2,1,0:T(8,128)(2,1)}), bf16[16,3,64,128]{3,2,1,0:T(8,128)(2,1)S(1)}, u32[]{:S(2)}, u32[]{:S(2)}) async-start(bf16[16,3,64,128]{3,2,1,0:T(8,128)(2,1)} %pack_second.1), calls=%async_computation | async-start | bytes 1572864 | tf_op jit(solution)/shard_map/all_to_all | solution.py:502
  31.5 10.0 %collective-permute-start.6 = (bf16[16,3,64,128]{3,2,1,0:T(8,128)(2,1)S(1)}, bf16[16,3,64,128]{3,2,1,0:T(8,128)(2,1)S(1)}, u32[]{:S(2)}, u32[]{:S(2)}) collective-permute-start(bf16[16,3,64,128]{3,2,1,0:T(8,128)(2,1)S(1)} %all-to-all-done.mine), channel_id=1, source_target_pairs={{0,1},{1,0},{2,3},{3,2},{4,5},{5,4},{6,7},{7,6},{8,9},{9,8},{10,11... | collective-permute-start | bytes 2359304 | tf_op jit(solution)/shard_map/ppermute | solution.py:65
  33.8 18.0 %collective-permute-start.8 = (bf16[2,256,1024]{2,1,0:T(8,128)(2,1)S(1)}, bf16[2,256,1024]{2,1,0:T(8,128)(2,1)}, u32[]{:S(2)}, u32[]{:S(2)}) collective-permute-start(bf16[2,256,1024]{2,1,0:T(8,128)(2,1)S(1)} %collective-permute-done.qr.kv_a), channel_id=1, source_target_pairs={{0,1},{1,0},{2,3},{3,2},{4,5},{5,4},{6,7},{7,6},{8,9},{9,8},{10,11... | collective-permute-start | bytes 3145736 | tf_op jit(solution)/shard_map/ppermute | solution.py:65
  33.8 28.1 %collective-permute-start.5 = (bf16[256,2176]{1,0:T(8,128)(2,1)}, bf16[256,2176]{1,0:T(8,128)(2,1)}, u32[]{:S(2)}, u32[]{:S(2)}) collective-permute-start(bf16[256,2176]{1,0:T(8,128)(2,1)} %get-tuple-element.22), channel_id=1, source_target_pairs={{0,1},{1,0},{2,3},{3,2},{4,5},{5,4},{6,7},{7,6},{8,9},{9,8},{10,11... | collective-permute-start | bytes 3342344 | tf_op jit(solution)/shard_map/ppermute | solution.py:65
  39.4 14.6 %collective-permute-start.7 = (bf16[256,1152]{1,0:T(8,128)(2,1)}, bf16[256,1152]{1,0:T(8,128)(2,1)}, u32[]{:S(2)}, u32[]{:S(2)}) collective-permute-start(bf16[256,1152]{1,0:T(8,128)(2,1)} %near_even.1), channel_id=1, source_target_pairs={{0,2},{1,3},{4,6},{5,7},{8,10},{9,11},{12,14},{13,15},{16,18},{17,... | collective-permute-start | bytes 1769480 | tf_op jit(solution)/shard_map/ppermute | solution.py:65
  45.8 14.3 %all-to-all-start.1 = ((bf16[16,80,128]{2,1,0:T(8,128)(2,1)}), bf16[16,80,128]{2,1,0:T(8,128)(2,1)S(1)}, u32[]{:S(2)}, u32[]{:S(2)}) async-start(bf16[16,80,128]{2,1,0:T(8,128)(2,1)} %far_kernel.1), calls=%async_computation.1 | async-start | bytes 655360 | tf_op jit(solution)/shard_map/all_to_all | solution.py:529
  60.1 3.1 %collective-permute-start.9 = (bf16[16,80,128]{2,1,0:T(8,128)(2,1)S(1)}, bf16[16,80,128]{2,1,0:T(8,128)(2,1)S(1)}, u32[]{:S(2)}, u32[]{:S(2)}) collective-permute-start(bf16[16,80,128]{2,1,0:T(8,128)(2,1)S(1)} %all-to-all-done.1.far_own), channel_id=1, source_target_pairs={{0,1},{1,0},{2,3},{3,2},{4,5},{5,4},{6,7},{7,6},{8,9},{9,8},{10,11... | collective-permute-start | bytes 983048 | tf_op jit(solution)/shard_map/ppermute | solution.py:65
